TPU v7x, 512 devices: a whole 4x4x16 slice. The times are simulated.
512 devices in a mesh: cell: 64 (over z, y_hi, core), band: 8 (over x, y_lo).
Axes of the slice: x: 4, y: 4 (y_hi: 2, y_lo: 2; y = y_hi * 2 + y_lo), z: 16, core: 2. Of those that a mesh axis runs over, the one named last changes fastest.
Arguments:
- positions: bfloat16 [128, 3, 96, 192], P('cell', None, 'band'), may hold values from -6 to 6
- densities: bfloat16 [128, 3, 96, 192], P('cell', None, 'band'), may hold values from -6 to 6
- operator: bfloat16 [640, 96, 192], P('cell', 'band'), may hold values from -0.046875 to 0.046875
- target_shift: int32 [128, 16], P('cell'), may hold values from 0 to 191
- weights: float32 [640], replicated, may hold values from 0.02 to 0.2
Outputs:
- velocity: float32 [128, 3, 16], P('cell')
All inputs are finite; a program needn't handle non-finite values.
Results may differ from a plain program's by a relative error of at most 0.0003.
Values may be sent and summed in bfloat16 or wider, within the bound.
No kernel may reach another device: no remote copies, remote signals or barrier semaphores. Data moves between devices by JAX's collectives and lax.ppermute only.
A program may use at most 64 MiB of HBM per device.

v0:
```python
import jax
import jax.numpy as jnp
from jax import lax
from jax.sharding import Mesh
from jax.sharding import PartitionSpec as P

CELL = ("cell_0", "cell_1", "cell_2")


blob_radius = 0.5


def laid_out(parts, dim):
    parts = jnp.moveaxis(parts, 0, dim)
    shape = parts.shape
    return parts.reshape(*shape[:dim], shape[dim] * shape[dim + 1], *shape[dim + 2 :])


def gather_in_order(array, axes, sequence):
    parts = array[None]
    for k in sequence:
        parts = lax.all_gather(parts, axes[k], axis=0, tiled=True)
    block = [lax.axis_size(axes[k]) for k in reversed(sequence)]
    parts = parts.reshape(*block, *array.shape)
    turned = sorted(range(len(sequence)), key=lambda place: sequence[len(sequence) - 1 - place])
    return parts.transpose(*turned, *range(len(sequence), parts.ndim)).reshape(-1, *array.shape)


def gathered_by_axis(array, axes, sequence, dim):
    return laid_out(gather_in_order(array, axes, sequence), dim)


def copy_for_each(array, axis):
    copies = jnp.broadcast_to(array, (lax.axis_size(axis), *array.shape))
    return lax.all_to_all(copies, axis, split_axis=0, concat_axis=0, tiled=True)


def of_everyone(array, axis):
    everything = copy_for_each(array, axis)
    return jnp.sum(everything, axis=0)


def stokes(target, rows, weights):
    spread = target[:, :, :, None] - rows[:, 0:3]
    force = rows[:, 3:6]
    dist_sq = jnp.sum(spread * spread, axis=1)
    along = jnp.sum(spread * force, axis=1)
    blob_sq = blob_radius * blob_radius
    numer = (dist_sq + 2.0 * blob_sq)[:, None] * force + along[:, None] * spread
    kernel = weights / (dist_sq + blob_sq) ** 1.5
    return jnp.sum(numer * kernel[:, None], axis=-1)


def shifted_rows(source, shifts):
    caps_count, comps, lat_count, lon_count = source.shape
    doubled = jnp.concatenate([source, source], axis=3)
    zero = jnp.int32(0)

    def per_capsule(block, capsule_shifts):

        def per_target(offset):
            return lax.dynamic_slice(block, (zero, zero, offset), (comps, lat_count, lon_count))

        return jax.vmap(per_target)(capsule_shifts)

    rolled = jax.vmap(per_capsule)(doubled, shifts)
    rolled = jnp.transpose(rolled, (0, 2, 1, 3, 4))
    return rolled.reshape(caps_count * comps * shifts.shape[1], lat_count * lon_count)


def contract(left, right):
    return lax.dot_general(
        left, right, (((1,), (1,)), ((), ())), preferred_element_type=jnp.float32
    )


def per_device(positions, densities, operator, target_shift, weights):
    source = jnp.concatenate([positions, densities], axis=1)
    caps_here = source.shape[0]
    targets = target_shift.shape[1]
    rows = shifted_rows(source, target_shift)
    piece = gathered_by_axis(operator, CELL, (1, 0, 2), 0)
    rotated = contract(rows, piece.reshape(piece.shape[0], -1))
    partial_value = rotated.reshape(caps_here, 6, targets, -1)
    summed = of_everyone(partial_value, "band")
    velocity = stokes(summed[:, 0:3, :, 0], summed, weights)
    return velocity


def solution(mesh):
    split = Mesh(
        mesh.devices.reshape(16, 2, 2, mesh.shape["band"]), ("cell_0", "cell_1", "cell_2", "band")
    )
    in_specs = (
        P(CELL, None, "band", None),
        P(CELL, None, "band", None),
        P(CELL, "band", None),
        P(CELL, None),
        P(),
    )
    out_specs = P(CELL, None, None)
    return jax.shard_map(
        per_device, mesh=split, in_specs=in_specs, out_specs=out_specs, check_vma=False
    )
```

profile of v0, /device:TPU:32, one launch (start us, length us, event | category | flops | bytes accessed | tf_op | source)
XLA Modules:
  0.0 204.7 jit_solution(14913355248644693017)
XLA Ops:
  6.5 8.1 %all-gather = bf16[20,12,192]{2,1,0:T(8,128)(2,1)} all-gather(bf16[10,12,192]{2,1,0:T(8,128)(2,1)} %param.7), channel_id=2, replica_groups=mesh['cell_0'=16,'cell_1'=2,'cell_2'=2,'band'=8] {'cell_1'}, dimensions={0}, use_global_device_ids=true | all-gather | bytes 138240 | tf_op jit(solution)/shard_map/all_gather | solution.py:22
  14.6 0.0 all-gather.4.cloned.1.call-update
  14.6 0.0 copy-start
  14.7 0.0 all-gather.6.cloned.1.call-start
  14.7 78.0 %all-gather.4.cloned.1.call-done = bf16[32,10,12,192]{3,2,1,0:T(8,128)(2,1)} async-done(((bf16[2,10,12,192]{3,2,1,0:T(8,128)(2,1)}), bf16[32,10,12,192]{3,2,1,0:T(8,128)(2,1)}) %all-gather.4.cloned.1.call-update) | async-done | bytes 1474576 | tf_op jit(solution)/shard_map/all_gather | solution.py:22
  92.7 4.1 %copy.30 = bf16[32,10,12,192]{3,0,2,1:T(8,128)(2,1)} copy(bf16[32,10,12,192]{3,2,1,0:T(8,128)(2,1)} %all-gather.4.cloned.1.call-done) | data formatting | bytes 2949120 | tf_op jit(solution)/shard_map/all_gather | solution.py:22
  96.8 0.0 all-gather.6.cloned.1.call-update
  96.8 0.2 maximum_maximum_fusion
  97.0 2.4 %copy.28 = bf16[2,6,12,384]{2,1,0,3:T(8,128)(2,1)S(1)} copy(bf16[2,6,12,384]{3,0,2,1:T(2,128)(2,1)S(1)} %maximum_maximum_fusion) | data formatting | bytes 221184 | tf_op jit(solution)/shard_map/concatenate | solution.py:56
  99.4 0.1 reshape.18
  99.5 8.4 %gather_fusion = bf16[32,6,12,192]{2,1,3,0:T(8,128)(2,1)} fusion(bf16[2,6,12,384]{2,1,0,3:T(8,128)(2,1)S(1)} %copy.28, s32[32]{0:T(128)S(1)} %reshape.18), kind=kCustom, calls=%fused_computation | custom fusion | bytes 1769984 | tf_op jit(solution)/shard_map/vmap(vmap())/gather | solution.py:62
  107.9 13.8 %copy.29 = bf16[2,16,6,12,192]{4,3,1,2,0:T(8,128)(2,1)S(1)} copy(bf16[2,16,6,12,192]{3,2,4,1,0:T(8,128)(2,1)} %bitcast.19) | data formatting | bytes 1769472 | tf_op jit(solution)/shard_map/vmap(vmap())/gather | solution.py:62
  121.7 2.1 %dot_general.5 = bf16[2,6,16,2304]{3,2,1,0:T(8,128)(2,1)} reshape(bf16[2,6,16,12,192]{4,3,2,1,0:T(8,128)(2,1)S(1)} %bitcast.21) | data formatting | bytes 1769472 | tf_op jit(solution)/shard_map/dot_general | solution.py:72
  123.9 8.8 %reshape.17 = bf16[2,16,2,10,12,192]{5,2,1,0,4,3:T(2,128)(2,1)} reshape(bf16[64,10,12,192]{3,0,2,1:T(8,128)(2,1)} %all-gather.6.cloned.1.call-done) | data formatting | bytes 5898240 | tf_op jit(solution)/shard_map/reshape | solution.py:24
  132.7 6.8 %copy.31 = bf16[16,2,2,10,12,192]{5,4,3,2,1,0:T(8,128)(2,1)} copy(bf16[16,2,2,10,12,192]{5,1,0,2,4,3:T(2,128)(2,1)} %bitcast.20) | data formatting | bytes 5898240 | tf_op jit(solution)/shard_map/transpose | solution.py:26
  139.5 7.1 %reshape.30 = bf16[640,2304,1,1]{1,0,2,3:T(8,128)(2,1)S(1)} reshape(bf16[16,2,2,10,12,192]{5,4,3,2,1,0:T(8,128)(2,1)} %copy.31) | data formatting | bytes 5898240 | tf_op jit(solution)/shard_map/reshape;reshape;reshape | solution.py:83
  146.6 2.3 %fusion = f32[2,6,16,640]{3,2,1,0:T(8,128)S(1)} fusion(bf16[2,6,16,2304]{3,2,1,0:T(8,128)(2,1)} %dot_general.5, bf16[640,2304,1,1]{1,0,2,3:T(8,128)(2,1)S(1)} %reshape.30), kind=kOutput, calls=%fused_computation.1 | convolution fusion | flops 566231040 | bytes 4325376 | tf_op jit(solution)/shard_map/dot_general | solution.py:72
  148.9 0.4 broadcast_in_dim.15
  149.2 45.2 %all_to_all.5 = f32[8,2,6,16,640]{4,3,2,1,0:T(8,128)} all-to-all(f32[8,2,6,16,640]{4,3,2,1,0:T(8,128)S(1)} %broadcast_in_dim.15), channel_id=1, replica_groups=mesh['cell_0'=16,'cell_1'=2,'cell_2'=2,'band'=8] {'band'}, dimensions={0} | all-to-all | bytes 7864320 | tf_op jit(solution)/shard_map/all_to_all | solution.py:35
  194.4 2.4 %reduce_sum.36 = f32[2,6,16,640]{3,2,1,0:T(8,128)S(1)} reduce(f32[8,2,6,16,640]{4,3,2,1,0:T(8,128)} %all_to_all.5, f32[]{:T(128)} %constant.2.clone.1), dimensions={0}, to_apply=%region_0.0 | reduce | flops 860160 | bytes 4423684 | tf_op jit(solution)/shard_map/reduce_sum | solution.py:40
  196.8 0.1 copy.32
  196.9 0.1 multiply_reduce_fusion.1
  197.1 0.2 multiply_reduce_fusion
  197.3 0.6 copy.34
  (13 shorter events, 0.1 us)
Async XLA Ops:
  6.5 86.1 %all-gather.4.cloned.1.call-start = ((), (), s32[]{:S(2)}) async-start(), calls=%async_computation.1 | async-start | bytes 2785280 | tf_op jit(solution)/shard_map/all_gather | solution.py:22
  14.6 82.2 %copy-start = (bf16[2,3,12,192]{3,0,2,1:T(2,128)(2,1)S(1)}, bf16[2,3,12,192]{3,0,2,1:T(2,128)(2,1)}, u32[]{:S(2)}) copy-start(bf16[2,3,12,192]{3,0,2,1:T(2,128)(2,1)} %param.6) | copy-start | bytes 82948
  14.6 82.2 %copy-start.1 = (bf16[2,3,12,192]{3,0,2,1:T(2,128)(2,1)S(1)}, bf16[2,3,12,192]{3,0,2,1:T(2,128)(2,1)}, u32[]{:S(2)}) copy-start(bf16[2,3,12,192]{3,0,2,1:T(2,128)(2,1)} %param.5) | copy-start | bytes 82948
  14.7 109.2 %all-gather.6.cloned.1.call-start = ((), (), s32[]{:S(2)}) async-start(), calls=%async_computation.2 | async-start | bytes 5898240 | tf_op jit(solution)/shard_map/all_gather | solution.py:22
  96.8 2.6 %copy-start.3 = (s32[2,16]{1,0:T(2,128)S(1)}, s32[2,16]{1,0:T(2,128)}, u32[]{:S(2)}) copy-start(s32[2,16]{1,0:T(2,128)} %param.8) | copy-start | bytes 388
  194.4 2.6 %copy-start.2 = (f32[640]{0:T(1024)S(1)}, f32[640]{0:T(1024)}, u32[]{:S(2)}) copy-start(f32[640]{0:T(1024)} %param.9) | copy-start | bytes 7684
Sparse Core Ops, SparseCore 0:
  14.7 77.8 all-gather.3
  96.9 20.2 all-gather.5
where the time goes:
time: 206 us; the launch traced here: 205 us
  waiting for transfers between devices  78 us (38%)
  local copies, waits for them, and re-layouts  54.7 us (27%)
  blocking collectives  53.2 us (26%)
  between operations  13.5 us (7%)
  other arithmetic  2.92 us (1%)
  matrix products  2.27 us (1%)
    all_gather x2, waiting for transfers between devices, gather_in_order(): parts = lax.all_gather(parts, axes[k], axis=0, tiled=True)  78 us
    all_to_all x1, blocking collectives, copy_for_each(): return lax.all_to_all(copies, axis, split_axis=0, concat_axis=0, tiled=True)  45.2 us
    gather x3, local copies, waits for them, and re-layouts, per_target(): lax.dynamic_slice(block, (zero, zero, offset), (comps, lat_count, lon_cou...  22.3 us
    reshape x1, local copies, waits for them, and re-layouts, gather_in_order(): parts = parts.reshape(*block, *array.shape)  8.8 us
    all_gather x1, blocking collectives, gather_in_order(): parts = lax.all_gather(parts, axes[k], axis=0, tiled=True)  8.07 us
    another operation x1, local copies, waits for them, and re-layouts, per_device(): rotated = contract(rows, piece.reshape(piece.shape[0], -1))  7.07 us
    transpose x1, local copies, waits for them, and re-layouts, gather_in_order(): parts.transpose(*turned, *range(len(sequence), parts.ndim))  6.83 us
    all_gather x1, local copies, waits for them, and re-layouts, gather_in_order(): parts = lax.all_gather(parts, axes[k], axis=0, tiled=True)  4.12 us
  transfers between devices with their start and end apart: 2, of which 1 were waited for; matrix products, arithmetic and copies ran while one was open for 13% of the time, Pallas kernels for 0%

commit v1 on v0

v1 whole, which is shorter than its diff:
```python
import jax
import jax.numpy as jnp
from jax import lax
from jax.experimental import pallas as pl
from jax.experimental.pallas import tpu as pltpu
from jax.sharding import Mesh
from jax.sharding import PartitionSpec as P

F32 = jnp.float32
BF16 = jnp.bfloat16

LAT_HERE = 12
LON = 192
COLS = LAT_HERE * LON
TGT = 16
ROWS_HERE = 10
SLOT = 16
Z = 16
QUAD = 4
BAND = 8
CAPS = 2 * QUAD
NODES = Z * ROWS_HERE

CELL = ("z", "y_hi", "core")
GROUP = ("y_hi", "core")
STRIP = ("x", "y_lo")

blob_radius = 0.5


def rotate_kernel(src_ref, shift_ref, op_ref, out_ref, tiles, rolled, acc):
    for p in range(QUAD):
        block = src_ref[p].astype(F32)
        here = pl.ds(p * 144, 144)
        tiles[0, here, :] = block[:, 0:128]
        tiles[1, here, :] = jnp.concatenate([block[:, 128:192], block[:, 0:64]], axis=1)
        tiles[2, here, :] = block[:, 64:192]

    lane = lax.broadcasted_iota(jnp.int32, (TGT, 128), 1)
    low_half = lane < 64

    def per_capsule(c, carry):
        shift = jnp.broadcast_to(shift_ref[pl.ds(pl.multiple_of(c * TGT, TGT), TGT), :], (TGT, 128))
        place = lane + shift
        even = jnp.bitwise_and(place, 127)
        odd = jnp.bitwise_and(place + 64, 127)
        e0, e1, e2 = place < 128, place < 256, place + 128 < 256
        h0, h1 = place - 64 < 128, place + 64 < 256
        h2 = place + 64 < 128

        def per_component(k, carry):
            base = c * 72 + k * LAT_HERE
            to = pl.ds(pl.multiple_of((c * 6 + k) * TGT, TGT), TGT)
            for m in range(LAT_HERE // 2):

                def picked(a, where):
                    return [
                        jnp.take_along_axis(
                            jnp.broadcast_to(tiles[q, pl.ds(base + a, 1), :], (TGT, 128)),
                            where,
                            axis=1,
                            mode="promise_in_bounds",
                        )
                        for q in range(3)
                    ]

                g = picked(2 * m, even)
                h = picked(2 * m + 1, odd)
                first = jnp.where(e0, g[0], jnp.where(e1, g[1], g[2]))
                middle = jnp.where(low_half, jnp.where(e2, g[1], g[2]), jnp.where(h0, h[0], h[1]))
                last = jnp.where(h2, h[0], jnp.where(h1, h[1], h[2]))
                for n, value in enumerate((first, middle, last)):
                    rolled[to, pl.ds((3 * m + n) * 128, 128)] = value.astype(BF16)
            return carry

        return lax.fori_loop(0, 6, per_component, carry)

    lax.fori_loop(0, CAPS, per_capsule, 0)

    slot = lax.broadcasted_iota(jnp.int32, (NODES, Z * SLOT), 1)
    node = lax.broadcasted_iota(jnp.int32, (NODES, Z * SLOT), 0)
    within = jnp.bitwise_and(slot, SLOT - 1)
    kept = jnp.right_shift(slot, 4) * ROWS_HERE + within
    chosen = jnp.where((kept == node) & (within < ROWS_HERE), 1.0, 0.0).astype(BF16)
    held = jnp.dot(chosen, op_ref[...], preferred_element_type=F32).astype(BF16)
    acc[...] = lax.dot_general(
        rolled[...], held, (((1,), (1,)), ((), ())), preferred_element_type=F32
    )

    upper = lax.broadcasted_iota(jnp.int32, (8, NODES), 0) < 4
    for c in range(CAPS):
        for half in range(2):
            tails = [[], []]
            for pair in range(3):
                at = c * 96 + pair * 32 + half * 8
                one = acc[at : at + 8, :]
                two = acc[at + 16 : at + 24, :]
                lo = jnp.where(upper, one, pltpu.roll(two, 4, 0))
                hi = jnp.where(upper, pltpu.roll(one, 4, 0), two)
                for j, tile in enumerate((lo, hi)):
                    dest = (c // 2) * BAND + (c % 2) * 4 + half * 2 + j
                    out_ref[dest, pair * 8 : pair * 8 + 8, :] = tile[:, 0:128]
                    tails[j].append(tile[:, 128:NODES])
            for j in range(2):
                dest = (c // 2) * BAND + (c % 2) * 4 + half * 2 + j
                blank = jnp.zeros((8, 32), F32)
                out_ref[dest, 24:32, :] = jnp.concatenate([*tails[j], blank], axis=1)


def stokes_kernel(parts_ref, weight_ref, out_ref):
    blob_sq = blob_radius * blob_radius
    total = jnp.zeros((3, 4, 1), F32)
    pole = None
    sums = [jnp.zeros((4, 1), F32) for _ in range(3)]
    for g in range(QUAD):
        whole = parts_ref[g, 0]
        for b in range(1, BAND):
            whole = whole + parts_ref[g, b]
        main = [whole[4 * k : 4 * k + 4, :] for k in range(6)]
        tail = whole[24:32, :]
        rest = [
            tail[4 * (k % 2) : 4 * (k % 2) + 4, 32 * (k // 2) : 32 * (k // 2) + 32] for k in range(6)
        ]
        if g == 0:
            pole = [main[k][:, 0:1] for k in range(3)]
        for rows, weights in (
            (main, weight_ref[g : g + 1, 0:128]),
            (rest, weight_ref[g : g + 1, 128:NODES]),
        ):
            d = [pole[k] - rows[k] for k in range(3)]
            f = rows[3:6]
            q = d[0] * d[0] + d[1] * d[1] + d[2] * d[2]
            along = d[0] * f[0] + d[1] * f[1] + d[2] * f[2]
            s = q + blob_sq
            r = lax.rsqrt(s)
            kernel = weights * (r * r * r)
            near = (q + 2.0 * blob_sq) * kernel
            along = along * kernel
            for k in range(3):
                sums[k] = sums[k] + jnp.sum(near * f[k] + along * d[k], axis=1, keepdims=True)
    lane = lax.broadcasted_iota(jnp.int32, (4, 128), 1)
    packed = jnp.where(lane == 0, sums[0], jnp.where(lane == 1, sums[1], sums[2]))
    packed = jnp.concatenate([packed, jnp.zeros((4, 128), F32)], axis=0)
    for b in range(BAND):
        out_ref[b] = packed


def per_device(positions, densities, operator, target_shift, weights):
    vmem = pl.BlockSpec(memory_space=pltpu.VMEM)
    source = jnp.concatenate([positions, densities], axis=1).reshape(144, LON)
    source = lax.all_to_all(
        jnp.broadcast_to(source[None], (QUAD, 144, LON)), GROUP, 0, 0, tiled=True
    )
    shifts = lax.all_to_all(
        jnp.broadcast_to(target_shift[None], (QUAD, 2, TGT)), GROUP, 0, 0, tiled=True
    )
    rows = jnp.pad(operator.reshape(ROWS_HERE, COLS), ((0, SLOT - ROWS_HERE), (0, 0)))
    rows = lax.all_gather(rows, "z", axis=0, tiled=True)
    parts = pl.pallas_call(
        rotate_kernel,
        out_shape=jax.ShapeDtypeStruct((QUAD * BAND, 32, 128), F32),
        in_specs=[vmem] * 3,
        out_specs=vmem,
        scratch_shapes=[
            pltpu.VMEM((3, QUAD * 144, 128), F32),
            pltpu.VMEM((CAPS * 6 * TGT, COLS), BF16),
            pltpu.VMEM((CAPS * 6 * TGT, NODES), F32),
        ],
        compiler_params=pltpu.CompilerParams(vmem_limit_bytes=48 * 2**20),
        name="rotate",
    )(source, shifts.reshape(CAPS * TGT, 1), rows)
    parts = lax.all_to_all(parts, GROUP + STRIP, 0, 0, tiled=True)
    weights = weights.reshape(Z, QUAD, ROWS_HERE).transpose(1, 0, 2).reshape(QUAD, NODES)
    found = pl.pallas_call(
        stokes_kernel,
        out_shape=jax.ShapeDtypeStruct((BAND, 8, 128), F32),
        in_specs=[vmem] * 2,
        out_specs=vmem,
        compiler_params=pltpu.CompilerParams(vmem_limit_bytes=32 * 2**20),
        name="stokes",
    )(parts.reshape(QUAD, BAND, 32, 128), weights)
    found = lax.all_to_all(found, STRIP, 0, 0, tiled=True)
    return found[:, 0:4, 0:3].reshape(2, TGT, 3).transpose(0, 2, 1)


def solution(mesh):
    split = Mesh(mesh.devices.reshape(16, 2, 2, 4, 2), CELL + STRIP)
    in_specs = (
        P(CELL, None, STRIP, None),
        P(CELL, None, STRIP, None),
        P(CELL, STRIP, None),
        P(CELL, None),
        P(),
    )
    return jax.shard_map(
        per_device, mesh=split, in_specs=in_specs, out_specs=P(CELL, None, None), check_vma=False
    )
```

time: 206 us -> 133 us (0.65)
  the two profiles are of different devices: /device:TPU:32 before, /device:TPU:1 now
where the time goes in v1:
time: 133 us; the launch traced here: 132 us
  waiting for transfers between devices  61.4 us (46%)
  starting transfers between devices  31.6 us (24%)
  between operations  13.5 us (10%)
  Pallas kernels  10.8 us (8%)
  blocking collectives  7.91 us (6%)
  local copies, waits for them, and re-layouts  6 us (5%)
    all_gather x1, waiting for transfers between devices, per_device(): rows = lax.all_gather(rows, 'z', axis=0, tiled=True)  40.5 us
    all_to_all x1, starting transfers between devices, per_device(): parts = lax.all_to_all(parts, GROUP + STRIP, 0, 0, tiled=True)  17.2 us
    pallas_call x1, Pallas kernels, per_device(): pl.pallas_call(rotate_kernel, out_shape=jax.ShapeDtypeStruct((QUAD * BAND...  10.5 us
    all_to_all x1, waiting for transfers between devices, per_device(): parts = lax.all_to_all(parts, GROUP + STRIP, 0, 0, tiled=True)  10.5 us
    all_to_all x1, starting transfers between devices, per_device(): lax.all_to_all(jnp.broadcast_to(target_shift[None], (QUAD, 2, TGT)), GROU...  10.1 us
    all_to_all x1, blocking collectives, per_device(): found = lax.all_to_all(found, STRIP, 0, 0, tiled=True)  7.91 us
    all_to_all x1, waiting for transfers between devices, per_device(): lax.all_to_all(jnp.broadcast_to(source[None], (QUAD, 144, LON)), GROUP, 0...  6.93 us
    all_to_all x1, starting transfers between devices, per_device(): lax.all_to_all(jnp.broadcast_to(source[None], (QUAD, 144, LON)), GROUP, 0...  4.26 us
  transfers between devices with their start and end apart: 4, of which 4 were waited for; matrix products, arithmetic and copies ran while one was open for 3% of the time, Pallas kernels for 0%

profile of v1, /device:TPU:1, one launch (start us, length us, event | category | flops | bytes accessed | tf_op | source)
XLA Modules:
  0.0 132.1 jit_solution(8209308765087756821)
XLA Ops:
  6.5 0.0 all-gather.2.cloned.1.call-start
  6.5 1.0 reshape.21
  7.6 0.6 pad.4
  8.2 0.0 all-gather.2.cloned.1.call-update
  8.2 1.3 broadcast_in_dim.15
  9.5 10.1 %all-to-all-start.1 = ((s32[4,2,16]{2,1,0:T(2,128)}), s32[4,2,16]{2,1,0:T(2,128)S(1)}, u32[]{:S(2)}, u32[]{:S(2)}) async-start(s32[4,2,16]{2,1,0:T(2,128)} %broadcast_in_dim.15), calls=%async_computation.1 | async-start | bytes 8192 | tf_op jit(solution)/shard_map/all_to_all | solution.py:154
  19.6 0.9 pad_maximum_fusion
  20.5 3.5 %all-to-all-done.1 = s32[4,2,16]{2,1,0:T(2,128)S(1)} async-done(((s32[4,2,16]{2,1,0:T(2,128)}), s32[4,2,16]{2,1,0:T(2,128)S(1)}, u32[]{:S(2)}, u32[]{:S(2)}) %all-to-all-start.1) | async-done | bytes 544 | tf_op jit(solution)/shard_map/all_to_all | solution.py:154
  24.0 0.7 broadcast_in_dim.14
  24.8 4.3 %all-to-all-start = ((bf16[4,144,192]{2,1,0:T(8,128)(2,1)}), bf16[4,144,192]{2,1,0:T(8,128)(2,1)S(1)}, u32[]{:S(2)}, u32[]{:S(2)}) async-start(bf16[4,144,192]{2,1,0:T(8,128)(2,1)} %broadcast_in_dim.14), calls=%async_computation | async-start | bytes 589824 | tf_op jit(solution)/shard_map/all_to_all | solution.py:151
  29.0 0.0 copy-start.1
  29.0 0.1 reshape.26.shift_ref
  29.1 6.9 %all-to-all-done.src_ref = bf16[4,144,192]{2,1,0:T(8,128)(2,1)S(1)} async-done(((bf16[4,144,192]{2,1,0:T(8,128)(2,1)}), bf16[4,144,192]{2,1,0:T(8,128)(2,1)S(1)}, u32[]{:S(2)}, u32[]{:S(2)}) %all-to-all-start) | async-done | bytes 221216 | tf_op jit(solution)/shard_map/all_to_all | solution.py:151
  36.0 40.5 %all-gather.2.cloned.1.call-done.op_ref = bf16[256,2304]{1,0:T(8,128)(2,1)} async-done(((bf16[16,2304]{1,0:T(8,128)(2,1)}), bf16[256,2304]{1,0:T(8,128)(2,1)}) %all-gather.2.cloned.1.call-update) | async-done | bytes 1179664 | tf_op jit(solution)/shard_map/all_gather | solution.py:158
  76.5 1.3 copy-done
  77.8 10.5 %rotate.1 = f32[32,32,128]{2,1,0:T(8,128)} custom-call(bf16[4,144,192]{2,1,0:T(8,128)(2,1)S(1)} %all-to-all-done.src_ref, s32[128,1]{1,0:T(8,128)S(1)} %reshape.26.shift_ref, bf16[256,2304]{1,0:T(8,128)(2,1)S(1)} %copy-done), custom_call_target="tpu_custom_call" | custom-call | tf_op jit(solution)/shard_map/rotate/pallas_call | solution.py:159
  88.3 17.2 %all-to-all-start.2 = ((f32[32,32,128]{2,1,0:T(8,128)}), f32[32,32,128]{2,1,0:T(8,128)S(1)}, u32[]{:S(2)}, u32[]{:S(2)}) async-start(f32[32,32,128]{2,1,0:T(8,128)} %rotate.1), calls=%async_computation.2 | async-start | bytes 1048576 | tf_op jit(solution)/shard_map/all_to_all | solution.py:172
  105.6 0.0 copy-done.1
  105.6 0.1 reshape.23
  105.8 0.1 reshape.24.weight_ref
  105.9 10.5 %all-to-all-done.2 = f32[32,32,128]{2,1,0:T(8,128)S(1)} async-done(((f32[32,32,128]{2,1,0:T(8,128)}), f32[32,32,128]{2,1,0:T(8,128)S(1)}, u32[]{:S(2)}, u32[]{:S(2)}) %all-to-all-start.2) | async-done | bytes 524320 | tf_op jit(solution)/shard_map/all_to_all | solution.py:172
  116.4 0.3 stokes.1
  116.6 7.9 %all_to_all.20 = f32[8,8,128]{2,1,0:T(8,128)S(1)} all-to-all(f32[8,8,128]{2,1,0:T(8,128)S(1)} %stokes.1), channel_id=1, replica_groups=mesh['z'=16,'y_hi'=2,'core'=2,'x'=4,'y_lo'=2] {'x','y_lo'}, dimensions={0} | all-to-all | bytes 65536 | tf_op jit(solution)/shard_map/all_to_all | solution.py:182
  124.5 0.7 copy.12
  (5 shorter events, 0.1 us)
Async XLA Ops:
  6.5 70.0 %all-gather.2.cloned.1.call-start = ((), (), s32[]{:S(2)}) async-start(), calls=%async_computation.4 | async-start | bytes 1253376 | tf_op jit(solution)/shard_map/all_gather | solution.py:158
  9.5 14.5 %all-to-all-start.1 = ((s32[4,2,16]{2,1,0:T(2,128)}), s32[4,2,16]{2,1,0:T(2,128)S(1)}, u32[]{:S(2)}, u32[]{:S(2)}) async-start(s32[4,2,16]{2,1,0:T(2,128)} %broadcast_in_dim.15), calls=%async_computation.1 | async-start | bytes 8192 | tf_op jit(solution)/shard_map/all_to_all | solution.py:154
  24.8 11.3 %all-to-all-start = ((bf16[4,144,192]{2,1,0:T(8,128)(2,1)}), bf16[4,144,192]{2,1,0:T(8,128)(2,1)S(1)}, u32[]{:S(2)}, u32[]{:S(2)}) async-start(bf16[4,144,192]{2,1,0:T(8,128)(2,1)} %broadcast_in_dim.14), calls=%async_computation | async-start | bytes 589824 | tf_op jit(solution)/shard_map/all_to_all | solution.py:151
  29.0 76.6 %copy-start.1 = (f32[640]{0:T(1024)S(1)}, f32[640]{0:T(1024)}, u32[]{:S(2)}) copy-start(f32[640]{0:T(1024)} %param.9) | copy-start | bytes 7684
  76.5 1.3 copy-start
  88.3 28.0 %all-to-all-start.2 = ((f32[32,32,128]{2,1,0:T(8,128)}), f32[32,32,128]{2,1,0:T(8,128)S(1)}, u32[]{:S(2)}, u32[]{:S(2)}) async-start(f32[32,32,128]{2,1,0:T(8,128)} %rotate.1), calls=%async_computation.2 | async-start | bytes 1048576 | tf_op jit(solution)/shard_map/all_to_all | solution.py:172
Sparse Core Ops, SparseCore 0:
  9.4 67.0 all-gather.1

commit v2 on v1

--- a/solution.py
+++ b/solution.py
@@ -14,12 +14,12 @@
 COLS = LAT_HERE * LON
 TGT = 16
 ROWS_HERE = 10
-SLOT = 16
 Z = 16
 QUAD = 4
 BAND = 8
 CAPS = 2 * QUAD
 NODES = Z * ROWS_HERE
+LINES = ROWS_HERE * COLS // 128
 
 CELL = ("z", "y_hi", "core")
 GROUP = ("y_hi", "core")
@@ -28,9 +28,9 @@
 blob_radius = 0.5
 
 
-def rotate_kernel(src_ref, shift_ref, op_ref, out_ref, tiles, rolled, acc):
+def roll_kernel(src_ref, rolled_ref, tiles):
     for p in range(QUAD):
-        block = src_ref[p].astype(F32)
+        block = src_ref[p, 0:144, :].astype(F32)
         here = pl.ds(p * 144, 144)
         tiles[0, here, :] = block[:, 0:128]
         tiles[1, here, :] = jnp.concatenate([block[:, 128:192], block[:, 0:64]], axis=1)
@@ -39,9 +39,10 @@
     lane = lax.broadcasted_iota(jnp.int32, (TGT, 128), 1)
     low_half = lane < 64
 
-    def per_capsule(c, carry):
-        shift = jnp.broadcast_to(shift_ref[pl.ds(pl.multiple_of(c * TGT, TGT), TGT), :], (TGT, 128))
-        place = lane + shift
+    for c in range(CAPS):
+        at = (c % 2) * 96
+        shift = src_ref[c // 2, 144:160, at : at + 1].astype(F32).astype(jnp.int32)
+        place = lane + jnp.broadcast_to(shift, (TGT, 128))
         even = jnp.bitwise_and(place, 127)
         odd = jnp.bitwise_and(place + 64, 127)
         e0, e1, e2 = place < 128, place < 256, place + 128 < 256
@@ -70,21 +71,20 @@
                 middle = jnp.where(low_half, jnp.where(e2, g[1], g[2]), jnp.where(h0, h[0], h[1]))
                 last = jnp.where(h2, h[0], jnp.where(h1, h[1], h[2]))
                 for n, value in enumerate((first, middle, last)):
-                    rolled[to, pl.ds((3 * m + n) * 128, 128)] = value.astype(BF16)
+                    rolled_ref[to, pl.ds((3 * m + n) * 128, 128)] = value.astype(BF16)
             return carry
 
-        return lax.fori_loop(0, 6, per_component, carry)
-
-    lax.fori_loop(0, CAPS, per_capsule, 0)
-
-    slot = lax.broadcasted_iota(jnp.int32, (NODES, Z * SLOT), 1)
-    node = lax.broadcasted_iota(jnp.int32, (NODES, Z * SLOT), 0)
-    within = jnp.bitwise_and(slot, SLOT - 1)
-    kept = jnp.right_shift(slot, 4) * ROWS_HERE + within
-    chosen = jnp.where((kept == node) & (within < ROWS_HERE), 1.0, 0.0).astype(BF16)
-    held = jnp.dot(chosen, op_ref[...], preferred_element_type=F32).astype(BF16)
+        lax.fori_loop(0, 6, per_component, 0)
+
+
+def rotate_kernel(rolled_ref, op_ref, out_ref, lines, held, acc):
+    for z in range(Z):
+        lines[z * LINES : (z + 1) * LINES, :] = op_ref[z].astype(F32)
+    for n in range(COLS // 128):
+        rows = lines[pl.ds(n, NODES, stride=COLS // 128), :]
+        held[:, n * 128 : (n + 1) * 128] = rows.astype(BF16)
     acc[...] = lax.dot_general(
-        rolled[...], held, (((1,), (1,)), ((), ())), preferred_element_type=F32
+        rolled_ref[...], held[...], (((1,), (1,)), ((), ())), preferred_element_type=F32
     )
 
     upper = lax.broadcasted_iota(jnp.int32, (8, NODES), 0) < 4
@@ -147,28 +147,37 @@
 
 def per_device(positions, densities, operator, target_shift, weights):
     vmem = pl.BlockSpec(memory_space=pltpu.VMEM)
+    lines = operator.reshape(LINES, 128)
+    lines = lax.all_gather(lines[None], "z", axis=0, tiled=True)
     source = jnp.concatenate([positions, densities], axis=1).reshape(144, LON)
+    shifts = jnp.broadcast_to(target_shift.T[:, :, None], (TGT, 2, LON // 2)).reshape(TGT, LON)
+    source = jnp.concatenate([source, shifts.astype(BF16)], axis=0)
     source = lax.all_to_all(
-        jnp.broadcast_to(source[None], (QUAD, 144, LON)), GROUP, 0, 0, tiled=True
-    )
-    shifts = lax.all_to_all(
-        jnp.broadcast_to(target_shift[None], (QUAD, 2, TGT)), GROUP, 0, 0, tiled=True
-    )
-    rows = jnp.pad(operator.reshape(ROWS_HERE, COLS), ((0, SLOT - ROWS_HERE), (0, 0)))
-    rows = lax.all_gather(rows, "z", axis=0, tiled=True)
+        jnp.broadcast_to(source[None], (QUAD, *source.shape)), GROUP, 0, 0, tiled=True
+    )
+    rolled = pl.pallas_call(
+        roll_kernel,
+        out_shape=jax.ShapeDtypeStruct((CAPS * 6 * TGT, COLS), BF16),
+        in_specs=[vmem],
+        out_specs=vmem,
+        scratch_shapes=[pltpu.VMEM((3, QUAD * 144, 128), F32)],
+        compiler_params=pltpu.CompilerParams(vmem_limit_bytes=32 * 2**20),
+        cost_estimate=pl.CostEstimate(flops=10**9, bytes_accessed=2**23, transcendentals=0),
+        name="roll",
+    )(source)
     parts = pl.pallas_call(
         rotate_kernel,
         out_shape=jax.ShapeDtypeStruct((QUAD * BAND, 32, 128), F32),
-        in_specs=[vmem] * 3,
+        in_specs=[vmem] * 2,
         out_specs=vmem,
         scratch_shapes=[
-            pltpu.VMEM((3, QUAD * 144, 128), F32),
-            pltpu.VMEM((CAPS * 6 * TGT, COLS), BF16),
+            pltpu.VMEM((Z * LINES, 128), F32),
+            pltpu.VMEM((NODES, COLS), BF16),
             pltpu.VMEM((CAPS * 6 * TGT, NODES), F32),
         ],
-        compiler_params=pltpu.CompilerParams(vmem_limit_bytes=48 * 2**20),
+        compiler_params=pltpu.CompilerParams(vmem_limit_bytes=32 * 2**20),
         name="rotate",
-    )(source, shifts.reshape(CAPS * TGT, 1), rows)
+    )(rolled, lines)
     parts = lax.all_to_all(parts, GROUP + STRIP, 0, 0, tiled=True)
     weights = weights.reshape(Z, QUAD, ROWS_HERE).transpose(1, 0, 2).reshape(QUAD, NODES)
     found = pl.pallas_call(

time: 133 us -> 87.1 us (0.65)
  waiting for transfers between devices: 61.4 us -> 10.5 us
  blocking collectives: 7.91 us -> 36.8 us
  between operations: 13.5 us -> 0.09 us
  starting transfers between devices: 31.6 us -> 24.1 us
  local copies, waits for them, and re-layouts: 6 us -> 2.98 us
    all_gather x1 -> x0, waiting for transfers between devices: 40.5 us -> none  [per_device(): rows = lax.all_gather(rows, 'z', axis=0, tiled=True)]
    all_gather x0 -> x1, blocking collectives: none -> 28.9 us  [per_device(): lines = lax.all_gather(lines[None], 'z', axis=0, tiled=True)]
    all_to_all x2 -> x1, waiting for transfers between devices: 10.4 us -> 0.01 us  [per_device(): lax.all_to_all(jnp.broadcast_to(source[None], (QUAD, *source.shape)), GRO...]
    pallas_call x1, Pallas kernels: 10.5 us -> 2.18 us  [per_device(): pl.pallas_call(rotate_kernel, out_shape=jax.ShapeDtypeStruct((QUAD * BAND...]
    pallas_call x0 -> x1, Pallas kernels: none -> 8.18 us  [per_device(): pl.pallas_call(roll_kernel, out_shape=jax.ShapeDtypeStruct((CAPS * 6 * TG...]
    all_to_all x2 -> x1, starting transfers between devices: 14.3 us -> 10.3 us  [per_device(): lax.all_to_all(jnp.broadcast_to(source[None], (QUAD, *source.shape)), GRO...]
    all_to_all x1, starting transfers between devices: 17.2 us -> 13.8 us  [per_device(): parts = lax.all_to_all(parts, GROUP + STRIP, 0, 0, tiled=True)]
  transfers between devices with their start and end apart: 4 -> 2, of which waited for: 4 -> 1; matrix products, arithmetic and copies ran while one was open for 3% -> 1% of each run, Pallas kernels for 0% -> 0%
where the time goes in v2:
time: 87.1 us; the launch traced here: 86.7 us
  blocking collectives  36.8 us (42%)
  starting transfers between devices  24.1 us (28%)
  Pallas kernels  10.6 us (12%)
  waiting for transfers between devices  10.5 us (12%)
  local copies, waits for them, and re-layouts  2.98 us (3%)
  other arithmetic  1.6 us (2%)
    all_gather x1, blocking collectives, per_device(): lines = lax.all_gather(lines[None], 'z', axis=0, tiled=True)  28.9 us
    all_to_all x1, starting transfers between devices, per_device(): parts = lax.all_to_all(parts, GROUP + STRIP, 0, 0, tiled=True)  13.8 us
    all_to_all x1, waiting for transfers between devices, per_device(): parts = lax.all_to_all(parts, GROUP + STRIP, 0, 0, tiled=True)  10.5 us
    all_to_all x1, starting transfers between devices, per_device(): lax.all_to_all(jnp.broadcast_to(source[None], (QUAD, *source.shape)), GRO...  10.3 us
    pallas_call x1, Pallas kernels, per_device(): pl.pallas_call(roll_kernel, out_shape=jax.ShapeDtypeStruct((CAPS * 6 * TG...  8.18 us
    all_to_all x1, blocking collectives, per_device(): found = lax.all_to_all(found, STRIP, 0, 0, tiled=True)  7.91 us
    pallas_call x1, Pallas kernels, per_device(): pl.pallas_call(rotate_kernel, out_shape=jax.ShapeDtypeStruct((QUAD * BAND...  2.18 us
  transfers between devices with their start and end apart: 2, of which 1 were waited for; matrix products, arithmetic and copies ran while one was open for 1% of the time, Pallas kernels for 0%

profile of v2, /device:TPU:1, one launch (start us, length us, event | category | flops | bytes accessed | tf_op | source)
XLA Modules:
  0.0 86.7 jit_solution(17772691469871146470)
XLA Ops:
  0.0 0.9 %pad_maximum_fusion.1 = bf16[2,6,12,192]{3,0,2,1:T(2,128)(2,1)S(1)} fusion(bf16[2,3,12,192]{3,0,2,1:T(2,128)(2,1)} %param.6, bf16[2,3,12,192]{3,0,2,1:T(2,128)(2,1)} %param.5), kind=kLoop, calls=%fused_computation.1 | loop fusion | flops 27648 | bytes 110592 | tf_op jit(solution)/shard_map/concatenate | solution.py:152
  1.0 0.7 convert_bitcast_fusion
  1.6 0.1 copy.13
  1.7 0.1 broadcast_in_dim.4
  1.8 0.1 convert_element_type.12
  1.9 0.7 broadcast_in_dim.5
  2.7 10.3 %all-to-all-start = ((bf16[4,160,192]{2,1,0:T(8,128)(2,1)}), bf16[4,160,192]{2,1,0:T(8,128)(2,1)S(1)}, u32[]{:S(2)}, u32[]{:S(2)}) async-start(bf16[4,160,192]{2,1,0:T(8,128)(2,1)} %broadcast_in_dim.5), calls=%async_computation | async-start | bytes 655360 | tf_op jit(solution)/shard_map/all_to_all | solution.py:155
  13.0 1.0 %broadcast_in_dim_reshape.3 = bf16[1,180,128]{2,1,0:T(8,128)(2,1)S(1)} reshape(bf16[10,12,192]{2,1,0:T(8,128)(2,1)} %param.7) | data formatting | bytes 92160 | tf_op jit(solution)/shard_map/broadcast_in_dim;reshape | solution.py:151
  14.0 28.9 %all_gather.3.op_ref = bf16[16,180,128]{2,1,0:T(8,128)(2,1)S(1)} all-gather(bf16[1,180,128]{2,1,0:T(8,128)(2,1)S(1)} %broadcast_in_dim_reshape.3), channel_id=1, replica_groups=mesh['z'=16,'y_hi'=2,'core'=2,'x'=4,'y_lo'=2] {'z'}, dimensions={0}, use_global_device_ids=true | all-gather | bytes 783360 | tf_op jit(solution)/shard_map/all_gather | solution.py:151
  42.9 0.0 all-to-all-done.src_ref
  42.9 8.2 %roll.1.rolled_ref = bf16[768,2304]{1,0:T(8,128)(2,1)S(1)} custom-call(bf16[4,160,192]{2,1,0:T(8,128)(2,1)S(1)} %all-to-all-done.src_ref), custom_call_target="tpu_custom_call" | custom-call | flops 1000000000 | bytes 8388608 | tf_op jit(solution)/shard_map/roll/pallas_call | solution.py:158
  51.1 0.0 copy-start
  51.1 2.2 %rotate.1 = f32[32,32,128]{2,1,0:T(8,128)} custom-call(bf16[768,2304]{1,0:T(8,128)(2,1)S(1)} %roll.1.rolled_ref, bf16[16,180,128]{2,1,0:T(8,128)(2,1)S(1)} %all_gather.3.op_ref), custom_call_target="tpu_custom_call" | custom-call | tf_op jit(solution)/shard_map/rotate/pallas_call | solution.py:168
  53.3 13.8 %all-to-all-start.1 = ((f32[32,32,128]{2,1,0:T(8,128)}), f32[32,32,128]{2,1,0:T(8,128)S(1)}, u32[]{:S(2)}, u32[]{:S(2)}) async-start(f32[32,32,128]{2,1,0:T(8,128)} %rotate.1), calls=%async_computation.1 | async-start | bytes 1048576 | tf_op jit(solution)/shard_map/all_to_all | solution.py:181
  67.0 0.0 copy-done
  67.1 0.1 reshape.21
  67.2 0.1 reshape.22.weight_ref
  67.3 10.5 %all-to-all-done.1 = f32[32,32,128]{2,1,0:T(8,128)S(1)} async-done(((f32[32,32,128]{2,1,0:T(8,128)}), f32[32,32,128]{2,1,0:T(8,128)S(1)}, u32[]{:S(2)}, u32[]{:S(2)}) %all-to-all-start.1) | async-done | bytes 524320 | tf_op jit(solution)/shard_map/all_to_all | solution.py:181
  77.8 0.3 stokes.1
  78.1 7.9 %all_to_all.15 = f32[8,8,128]{2,1,0:T(8,128)S(1)} all-to-all(f32[8,8,128]{2,1,0:T(8,128)S(1)} %stokes.1), channel_id=1, replica_groups=mesh['z'=16,'y_hi'=2,'core'=2,'x'=4,'y_lo'=2] {'x','y_lo'}, dimensions={0} | all-to-all | bytes 65536 | tf_op jit(solution)/shard_map/all_to_all | solution.py:191
  86.0 0.7 copy.16
  (5 shorter events, 0.1 us)
Async XLA Ops:
  2.7 40.2 %all-to-all-start = ((bf16[4,160,192]{2,1,0:T(8,128)(2,1)}), bf16[4,160,192]{2,1,0:T(8,128)(2,1)S(1)}, u32[]{:S(2)}, u32[]{:S(2)}) async-start(bf16[4,160,192]{2,1,0:T(8,128)(2,1)} %broadcast_in_dim.5), calls=%async_computation | async-start | bytes 655360 | tf_op jit(solution)/shard_map/all_to_all | solution.py:155
  51.1 16.0 %copy-start = (f32[640]{0:T(1024)S(1)}, f32[640]{0:T(1024)}, u32[]{:S(2)}) copy-start(f32[640]{0:T(1024)} %param.9) | copy-start | bytes 7684
  53.3 24.6 %all-to-all-start.1 = ((f32[32,32,128]{2,1,0:T(8,128)}), f32[32,32,128]{2,1,0:T(8,128)S(1)}, u32[]{:S(2)}, u32[]{:S(2)}) async-start(f32[32,32,128]{2,1,0:T(8,128)} %rotate.1), calls=%async_computation.1 | async-start | bytes 1048576 | tf_op jit(solution)/shard_map/all_to_all | solution.py:181

commit v3 on v2

--- a/solution.py
+++ b/solution.py
@@ -77,7 +77,8 @@
         lax.fori_loop(0, 6, per_component, 0)
 
 
-def rotate_kernel(rolled_ref, op_ref, out_ref, lines, held, acc):
+def rotate_kernel(rolled_ref, op_ref, weight_ref, out_ref, weight_out_ref, lines, held, acc):
+    weight_out_ref[...] = weight_ref[...]
     for z in range(Z):
         lines[z * LINES : (z + 1) * LINES, :] = op_ref[z].astype(F32)
     for n in range(COLS // 128):
@@ -147,14 +148,16 @@
 
 def per_device(positions, densities, operator, target_shift, weights):
     vmem = pl.BlockSpec(memory_space=pltpu.VMEM)
-    lines = operator.reshape(LINES, 128)
-    lines = lax.all_gather(lines[None], "z", axis=0, tiled=True)
+    lines = jnp.broadcast_to(operator.reshape(LINES, 128)[None], (Z, LINES, 128))
+    lines, positions, densities, target_shift, weights = lax.optimization_barrier(
+        (lines, positions, densities, target_shift, weights)
+    )
+    lines = lax.all_to_all(lines, "z", 0, 0, tiled=True)
+    weights = weights.reshape(Z, QUAD, ROWS_HERE).transpose(1, 0, 2).reshape(QUAD, NODES)
     source = jnp.concatenate([positions, densities], axis=1).reshape(144, LON)
     shifts = jnp.broadcast_to(target_shift.T[:, :, None], (TGT, 2, LON // 2)).reshape(TGT, LON)
     source = jnp.concatenate([source, shifts.astype(BF16)], axis=0)
-    source = lax.all_to_all(
-        jnp.broadcast_to(source[None], (QUAD, *source.shape)), GROUP, 0, 0, tiled=True
-    )
+    source = lax.all_gather(source[None], GROUP, axis=0, tiled=True)
     rolled = pl.pallas_call(
         roll_kernel,
         out_shape=jax.ShapeDtypeStruct((CAPS * 6 * TGT, COLS), BF16),
@@ -165,11 +168,14 @@
         cost_estimate=pl.CostEstimate(flops=10**9, bytes_accessed=2**23, transcendentals=0),
         name="roll",
     )(source)
-    parts = pl.pallas_call(
+    parts, weights = pl.pallas_call(
         rotate_kernel,
-        out_shape=jax.ShapeDtypeStruct((QUAD * BAND, 32, 128), F32),
-        in_specs=[vmem] * 2,
-        out_specs=vmem,
+        out_shape=(
+            jax.ShapeDtypeStruct((QUAD * BAND, 32, 128), F32),
+            jax.ShapeDtypeStruct((QUAD, NODES), F32),
+        ),
+        in_specs=[vmem] * 3,
+        out_specs=(vmem, vmem),
         scratch_shapes=[
             pltpu.VMEM((Z * LINES, 128), F32),
             pltpu.VMEM((NODES, COLS), BF16),
@@ -177,9 +183,8 @@
         ],
         compiler_params=pltpu.CompilerParams(vmem_limit_bytes=32 * 2**20),
         name="rotate",
-    )(rolled, lines)
+    )(rolled, lines, weights)
     parts = lax.all_to_all(parts, GROUP + STRIP, 0, 0, tiled=True)
-    weights = weights.reshape(Z, QUAD, ROWS_HERE).transpose(1, 0, 2).reshape(QUAD, NODES)
     found = pl.pallas_call(
         stokes_kernel,
         out_shape=jax.ShapeDtypeStruct((BAND, 8, 128), F32),

time: 87.1 us -> 86.5 us (level)
  starting transfers between devices: 24.1 us -> 15.8 us
  waiting for transfers between devices: 10.5 us -> 13.8 us
  blocking collectives: 36.8 us -> 39.7 us
  local copies, waits for them, and re-layouts: 2.98 us -> 3.91 us
    all_to_all x0 -> x1, blocking collectives: none -> 23.2 us  [per_device(): parts = lax.all_to_all(parts, GROUP + STRIP, 0, 0, tiled=True)]
    all_gather x1, blocking collectives: 28.9 us -> 8.6 us  [per_device(): source = lax.all_gather(source[None], GROUP, axis=0, tiled=True)]
    all_to_all x2 -> x1, starting transfers between devices: 24.1 us -> 15.8 us  [per_device(): lines = lax.all_to_all(lines, 'z', 0, 0, tiled=True)]
    all_to_all x2 -> x1, waiting for transfers between devices: 10.5 us -> 13.8 us  [per_device(): lines = lax.all_to_all(lines, 'z', 0, 0, tiled=True)]
    broadcast_in_dim x1 -> x2, local copies, waits for them, and re-layouts: 0.74 us -> 1.99 us  [per_device(): jnp.broadcast_to(operator.reshape(LINES, 128)[None], (Z, LINES, 128))]
    another operation x1 -> x0, local copies, waits for them, and re-layouts: 1.01 us -> none  [per_device(): lines = lax.all_gather(lines[None], 'z', axis=0, tiled=True)]
  transfers between devices with their start and end apart: 2 -> 1, of which waited for: 1 -> 1; matrix products, arithmetic and copies ran while one was open for 1% -> 3% of each run, Pallas kernels for 0% -> 10%
where the time goes in v3:
time: 86.5 us; the launch traced here: 85.8 us
  blocking collectives  39.7 us (46%)
  starting transfers between devices  15.8 us (18%)
  waiting for transfers between devices  13.8 us (16%)
  Pallas kernels  11 us (13%)
  local copies, waits for them, and re-layouts  3.91 us (5%)
  other arithmetic  1.6 us (2%)
    all_to_all x1, blocking collectives, per_device(): parts = lax.all_to_all(parts, GROUP + STRIP, 0, 0, tiled=True)  23.2 us
    all_to_all x1, starting transfers between devices, per_device(): lines = lax.all_to_all(lines, 'z', 0, 0, tiled=True)  15.8 us
    all_to_all x1, waiting for transfers between devices, per_device(): lines = lax.all_to_all(lines, 'z', 0, 0, tiled=True)  13.8 us
    all_gather x1, blocking collectives, per_device(): source = lax.all_gather(source[None], GROUP, axis=0, tiled=True)  8.6 us
    pallas_call x1, Pallas kernels, per_device(): pl.pallas_call(roll_kernel, out_shape=jax.ShapeDtypeStruct((CAPS * 6 * TG...  8.18 us
    all_to_all x1, blocking collectives, per_device(): found = lax.all_to_all(found, STRIP, 0, 0, tiled=True)  7.91 us
    pallas_call x1, Pallas kernels, per_device(): pl.pallas_call(rotate_kernel, out_shape=(jax.ShapeDtypeStruct((QUAD * BAN...  2.52 us
    broadcast_in_dim x2, local copies, waits for them, and re-layouts, per_device(): jnp.broadcast_to(operator.reshape(LINES, 128)[None], (Z, LINES, 128))  1.99 us
  transfers between devices with their start and end apart: 1, of which 1 were waited for; matrix products, arithmetic and copies ran while one was open for 3% of the time, Pallas kernels for 10%

profile of v3, /device:TPU:1, one launch (start us, length us, event | category | flops | bytes accessed | tf_op | source)
XLA Modules:
  0.0 85.8 jit_solution(17438363846516117972)
XLA Ops:
  0.0 1.0 %broadcast_in_dim.16 = bf16[180,128]{1,0:T(8,128)(2,1)S(1)} reshape(bf16[10,12,192]{2,1,0:T(8,128)(2,1)} %param.7) | data formatting | bytes 92160 | tf_op jit(solution)/shard_map/broadcast_in_dim | solution.py:151
  1.0 1.0 %broadcast_in_dim.17 = bf16[16,180,128]{2,1,0:T(8,128)(2,1)} broadcast(bf16[180,128]{1,0:T(8,128)(2,1)S(1)} %broadcast_in_dim.16), dimensions={1,2} | broadcast | bytes 783360 | tf_op jit(solution)/shard_map/broadcast_in_dim | solution.py:151
  2.0 15.8 %all-to-all-start = ((bf16[16,180,128]{2,1,0:T(8,128)(2,1)}), bf16[16,180,128]{2,1,0:T(8,128)(2,1)}, u32[]{:S(2)}, u32[]{:S(2)}) async-start(bf16[16,180,128]{2,1,0:T(8,128)(2,1)} %broadcast_in_dim.17), calls=%async_computation | async-start | bytes 1507328 | tf_op jit(solution)/shard_map/all_to_all | solution.py:155
  17.8 0.7 convert_bitcast_fusion
  18.5 0.1 copy.9
  18.6 0.1 broadcast_in_dim.18
  18.7 0.1 convert_element_type.12
  18.8 0.8 reshape.20
  19.6 0.1 reshape.21.weight_ref
  19.7 0.9 %pad_maximum_fusion.1 = bf16[2,6,12,192]{3,0,2,1:T(2,128)(2,1)S(1)} fusion(bf16[2,3,12,192]{3,0,2,1:T(2,128)(2,1)} %param.6, bf16[2,3,12,192]{3,0,2,1:T(2,128)(2,1)} %param.5), kind=kLoop, calls=%fused_computation.1 | loop fusion | flops 27648 | bytes 110592 | tf_op jit(solution)/shard_map/concatenate | solution.py:157
  20.7 8.6 %all-gather = bf16[640,192]{1,0:T(8,128)(2,1)S(1)} all-gather(bf16[160,192]{1,0:T(8,128)(2,1)S(1)} %pad_maximum_fusion), channel_id=2, replica_groups=mesh['z'=16,'y_hi'=2,'core'=2,'x'=4,'y_lo'=2] {'y_hi','core'}, dimensions={0}, use_global_device_ids=true | all-gather | bytes 307200 | tf_op jit(solution)/shard_map/all_gather | solution.py:160
  29.3 8.2 %roll.1.rolled_ref = bf16[768,2304]{1,0:T(8,128)(2,1)S(1)} custom-call(bf16[4,160,192]{2,1,0:T(8,128)(2,1)S(1)} %bitcast.8), custom_call_target="tpu_custom_call" | custom-call | flops 1000000000 | bytes 8388608 | tf_op jit(solution)/shard_map/roll/pallas_call | solution.py:161
  37.5 13.8 %all-to-all-done.op_ref = bf16[16,180,128]{2,1,0:T(8,128)(2,1)} async-done(((bf16[16,180,128]{2,1,0:T(8,128)(2,1)}), bf16[16,180,128]{2,1,0:T(8,128)(2,1)}, u32[]{:S(2)}, u32[]{:S(2)}) %all-to-all-start) | async-done | bytes 737312 | tf_op jit(solution)/shard_map/all_to_all | solution.py:155
  51.2 2.5 %rotate.1 = (f32[32,32,128]{2,1,0:T(8,128)S(1)}, f32[4,160]{1,0:T(4,128)S(1)}) custom-call(bf16[768,2304]{1,0:T(8,128)(2,1)S(1)} %roll.1.rolled_ref, bf16[16,180,128]{2,1,0:T(8,128)(2,1)} %all-to-all-done.op_ref, f32[4,160]{1,0:T(4,128)S(1)} %reshape.21.weight_ref), custom_call_target="tpu_custom_call" | custom-call | tf_op jit(solution)/shard_map/rotate/pallas_call | solution.py:171
  53.8 23.2 %all_to_all.15 = f32[32,32,128]{2,1,0:T(8,128)S(1)} all-to-all(f32[32,32,128]{2,1,0:T(8,128)S(1)} %get-tuple-element.17), channel_id=1, replica_groups=mesh['z'=16,'y_hi'=2,'core'=2,'x'=4,'y_lo'=2] {'y_hi','core','x','y_lo'}, dimensions={0} | all-to-all | bytes 1048576 | tf_op jit(solution)/shard_map/all_to_all | solution.py:187
  77.0 0.3 stokes.1
  77.2 7.9 %all_to_all.16 = f32[8,8,128]{2,1,0:T(8,128)S(1)} all-to-all(f32[8,8,128]{2,1,0:T(8,128)S(1)} %stokes.1), channel_id=1, replica_groups=mesh['z'=16,'y_hi'=2,'core'=2,'x'=4,'y_lo'=2] {'x','y_lo'}, dimensions={0} | all-to-all | bytes 65536 | tf_op jit(solution)/shard_map/all_to_all | solution.py:196
  85.1 0.7 copy.12
  (5 shorter events, 0.1 us)
Async XLA Ops:
  2.0 49.2 %all-to-all-start = ((bf16[16,180,128]{2,1,0:T(8,128)(2,1)}), bf16[16,180,128]{2,1,0:T(8,128)(2,1)}, u32[]{:S(2)}, u32[]{:S(2)}) async-start(bf16[16,180,128]{2,1,0:T(8,128)(2,1)} %broadcast_in_dim.17), calls=%async_computation | async-start | bytes 1507328 | tf_op jit(solution)/shard_map/all_to_all | solution.py:155

commit v4 on v3

v4 whole, which is shorter than its diff:
```python
import jax
import jax.numpy as jnp
from jax import lax
from jax.experimental import pallas as pl
from jax.experimental.pallas import tpu as pltpu
from jax.sharding import Mesh
from jax.sharding import PartitionSpec as P

F32 = jnp.float32
BF16 = jnp.bfloat16

LAT_HERE = 12
LON = 192
COLS = LAT_HERE * LON
TGT = 16
ROWS_HERE = 10
Z = 8
QUAD = 4
PARITY = 2
GROUPS = PARITY * QUAD
BAND = 8
HALF_CAPS = 2 * QUAD
NODES = Z * ROWS_HERE
TILES = COLS // 128
LINES = ROWS_HERE * TILES
LEFT = 128 - NODES

CELL = ("z_half", "z_low", "y_hi", "core")
GROUP = ("y_hi", "core")
STRIP = ("x", "y_lo")

blob_radius = 0.5


def pack_kernel(op_ref, out_ref, lines):
    for r in range(ROWS_HERE):
        row = op_ref[r].astype(F32)
        high = row[:, 128:LON]
        at = r * TILES
        lines[at : at + LAT_HERE, :] = row[:, 0:128]
        lines[at + LAT_HERE : at + TILES, :] = jnp.concatenate([high[0:6], high[6:12]], axis=1)
    packed = lines[...].astype(BF16)
    for z in range(Z):
        out_ref[z] = packed


def roll_kernel(src_ref, rolled_ref, tiles):
    for p in range(QUAD):
        block = src_ref[p, 0:144, :].astype(F32)
        here = pl.ds(p * 144, 144)
        tiles[0, here, :] = block[:, 0:128]
        tiles[1, here, :] = jnp.concatenate([block[:, 128:192], block[:, 0:64]], axis=1)
        tiles[2, here, :] = block[:, 64:192]

    lane = lax.broadcasted_iota(jnp.int32, (TGT, 128), 1)

    for c in range(HALF_CAPS):
        column = (c % 2) * 96
        shift = src_ref[c // 2, 144:160, column : column + 1].astype(F32).astype(jnp.int32)
        shift = jnp.broadcast_to(shift, (TGT, 128))
        take = jnp.bitwise_and(lane + shift, 127)
        goal = jnp.bitwise_and(lane - shift, 127)
        place = goal + shift
        early, late, low = place < 128, place < 256, goal < 64

        def rolled(value):
            return jnp.take_along_axis(value, take, axis=1, mode="promise_in_bounds").astype(BF16)

        def per_component(k, carry):
            base = c * 72 + k * LAT_HERE
            to = pl.ds(pl.multiple_of((c * 6 + k) * TGT, TGT), TGT)

            def row(q, a):
                return jnp.broadcast_to(tiles[q, pl.ds(base + a, 1), :], (TGT, 128))

            for m in range(6):
                t = [row(q, m) for q in range(3)]
                u = [row(q, m + 6) for q in range(3)]
                first = jnp.where(early, t[0], jnp.where(late, t[1], t[2]))
                second = jnp.where(early, u[0], jnp.where(late, u[1], u[2]))
                high = jnp.where(
                    low,
                    jnp.where(early, t[1], t[2]),
                    jnp.where(early, u[2], jnp.where(late, u[0], u[1])),
                )
                rolled_ref[to, m * 128 : m * 128 + 128] = rolled(first)
                rolled_ref[to, (m + 6) * 128 : (m + 6) * 128 + 128] = rolled(second)
                rolled_ref[to, (m + 12) * 128 : (m + 12) * 128 + 128] = rolled(high)
            return carry

        lax.fori_loop(0, 6, per_component, 0)


def rotate_kernel(
    mine_ref, next_ref, op_ref, weight_ref, side_ref, out_ref, weight_out_ref, lines, held, acc
):
    weight_out_ref[...] = weight_ref[...]
    for z in range(Z):
        lines[z * LINES : (z + 1) * LINES, :] = op_ref[z].astype(F32)
    for n in range(TILES):
        held[:, n * 128 : (n + 1) * 128] = lines[pl.ds(n, NODES, stride=TILES), :].astype(BF16)
    side = side_ref[0]
    upper = lax.broadcasted_iota(jnp.int32, (8, NODES), 0) < 4
    blank = jnp.zeros((8, 2 * 128 - 3 * NODES), F32)
    for o, rolled_ref in enumerate((mine_ref, next_ref)):
        acc[o] = lax.dot_general(
            rolled_ref[...], held[...], (((1,), (1,)), ((), ())), preferred_element_type=F32
        )
        first = jnp.bitwise_xor(side, o) * (QUAD * BAND)
        for c in range(HALF_CAPS):
            for half in range(2):
                found = [[], []]
                for pair in range(3):
                    at = c * 96 + pair * 32 + half * 8
                    one = acc[o, at : at + 8, :]
                    two = acc[o, at + 16 : at + 24, :]
                    found[0].append(jnp.where(upper, one, pltpu.roll(two, 4, 0)))
                    found[1].append(jnp.where(upper, pltpu.roll(one, 4, 0), two))
                for j in range(2):
                    dest = first + ((c // 2) * BAND + (c % 2) * 4 + half * 2 + j)
                    a, b, d = found[j]
                    out_ref[dest, 0:8, :] = jnp.concatenate([a, b[:, 0:LEFT]], axis=1)
                    out_ref[dest, 8:16, :] = jnp.concatenate([b[:, LEFT:NODES], d, blank], axis=1)


def stokes_kernel(parts_ref, weight_ref, out_ref):
    blob_sq = blob_radius * blob_radius
    pole = None
    sums = [jnp.zeros((4, 1), F32) for _ in range(3)]
    for g in range(GROUPS):
        whole = parts_ref[g, 0]
        for b in range(1, BAND):
            whole = whole + parts_ref[g, b]
        one, two = whole[0:8, :], whole[8:16, :]
        rest = NODES - LEFT
        pairs = (
            one[:, 0:NODES],
            jnp.concatenate([one[:, NODES:128], two[:, 0:rest]], axis=1),
            two[:, rest : rest + NODES],
        )
        rows = [pairs[k // 2][4 * (k % 2) : 4 * (k % 2) + 4, :] for k in range(6)]
        if g == 0:
            pole = [rows[k][:, 0:1] for k in range(3)]
        weights = weight_ref[g : g + 1, :]
        d = [pole[k] - rows[k] for k in range(3)]
        f = rows[3:6]
        q = d[0] * d[0] + d[1] * d[1] + d[2] * d[2]
        along = d[0] * f[0] + d[1] * f[1] + d[2] * f[2]
        r = lax.rsqrt(q + blob_sq)
        kernel = weights * (r * r * r)
        near = (q + 2.0 * blob_sq) * kernel
        along = along * kernel
        for k in range(3):
            sums[k] = sums[k] + jnp.sum(near * f[k] + along * d[k], axis=1, keepdims=True)
    lane = lax.broadcasted_iota(jnp.int32, (4, 128), 1)
    packed = jnp.where(lane == 0, sums[0], jnp.where(lane == 1, sums[1], sums[2]))
    packed = jnp.concatenate([packed, jnp.zeros((4, 128), F32)], axis=0)
    for b in range(BAND):
        out_ref[b] = packed


def roll_sources(source):
    vmem = pl.BlockSpec(memory_space=pltpu.VMEM)
    return pl.pallas_call(
        roll_kernel,
        out_shape=jax.ShapeDtypeStruct((HALF_CAPS * 6 * TGT, COLS), BF16),
        in_specs=[vmem],
        out_specs=vmem,
        scratch_shapes=[pltpu.VMEM((3, QUAD * 144, 128), F32)],
        compiler_params=pltpu.CompilerParams(vmem_limit_bytes=24 * 2**20),
        cost_estimate=pl.CostEstimate(flops=10**9, bytes_accessed=2**22, transcendentals=0),
        name="roll",
    )(source)


def per_device(positions, densities, operator, target_shift, weights):
    vmem = pl.BlockSpec(memory_space=pltpu.VMEM)
    smem = pl.BlockSpec(memory_space=pltpu.SMEM)
    lines = pl.pallas_call(
        pack_kernel,
        out_shape=jax.ShapeDtypeStruct((Z, LINES, 128), BF16),
        in_specs=[vmem],
        out_specs=vmem,
        scratch_shapes=[pltpu.VMEM((LINES, 128), F32)],
        compiler_params=pltpu.CompilerParams(vmem_limit_bytes=16 * 2**20),
        name="pack",
    )(operator)
    lines, positions, densities, target_shift, weights = lax.optimization_barrier(
        (lines, positions, densities, target_shift, weights)
    )
    lines = lax.all_to_all(lines, "z_half", 0, 0, tiled=True)
    weights = weights.reshape(Z, GROUPS, ROWS_HERE).transpose(1, 0, 2).reshape(GROUPS, NODES)
    source = jnp.concatenate([positions, densities], axis=1).reshape(144, LON)
    shifts = jnp.broadcast_to(target_shift.T[:, :, None], (TGT, 2, LON // 2)).reshape(TGT, LON)
    source = jnp.concatenate([source, shifts.astype(BF16)], axis=0)
    source = lax.all_gather(source[None], GROUP, axis=0, tiled=True)
    other = lax.ppermute(source, "z_low", [(0, 1), (1, 0)])
    mine = roll_sources(source)
    other = roll_sources(other)
    side = lax.axis_index("z_low").astype(jnp.int32)[None]
    parts, weights = pl.pallas_call(
        rotate_kernel,
        out_shape=(
            jax.ShapeDtypeStruct((GROUPS * BAND, 16, 128), F32),
            jax.ShapeDtypeStruct((GROUPS, NODES), F32),
        ),
        in_specs=[vmem] * 4 + [smem],
        out_specs=(vmem, vmem),
        scratch_shapes=[
            pltpu.VMEM((Z * LINES, 128), F32),
            pltpu.VMEM((NODES, COLS), BF16),
            pltpu.VMEM((PARITY, HALF_CAPS * 6 * TGT, NODES), F32),
        ],
        compiler_params=pltpu.CompilerParams(vmem_limit_bytes=32 * 2**20),
        name="rotate",
    )(mine, other, lines, weights, side)
    parts = lax.all_to_all(parts, ("z_low",) + GROUP + STRIP, 0, 0, tiled=True)
    found = pl.pallas_call(
        stokes_kernel,
        out_shape=jax.ShapeDtypeStruct((BAND, 8, 128), F32),
        in_specs=[vmem] * 2,
        out_specs=vmem,
        compiler_params=pltpu.CompilerParams(vmem_limit_bytes=32 * 2**20),
        name="stokes",
    )(parts.reshape(GROUPS, BAND, 16, 128), weights)
    found = lax.all_to_all(found, STRIP, 0, 0, tiled=True)
    return found[:, 0:4, 0:3].reshape(2, TGT, 3).transpose(0, 2, 1)


def solution(mesh):
    split = Mesh(mesh.devices.reshape(8, 2, 2, 2, 4, 2), CELL + STRIP)
    in_specs = (
        P(CELL, None, STRIP, None),
        P(CELL, None, STRIP, None),
        P(CELL, STRIP, None),
        P(CELL, None),
        P(),
    )
    return jax.shard_map(
        per_device, mesh=split, in_specs=in_specs, out_specs=P(CELL, None, None), check_vma=False
    )
```

time: 86.5 us -> 87.5 us (1.012)
  waiting for transfers between devices: 13.8 us -> 5.2 us
  Pallas kernels: 11 us -> 16.9 us
  local copies, waits for them, and re-layouts: 3.91 us -> 6.51 us
  starting transfers between devices: 15.8 us -> 18.3 us
  blocking collectives: 39.7 us -> 38.3 us
    all_to_all x1, waiting for transfers between devices: 13.8 us -> 0.01 us  [per_device(): lines = lax.all_to_all(lines, 'z_half', 0, 0, tiled=True)]
    pallas_call x2 -> x4, Pallas kernels: 10.7 us -> 16.5 us  [the longest x2 12.5 us: roll_sources(): pl.pallas_call(roll_kernel, out_shape=jax.ShapeDtypeStruct((HALF_CAPS * 6...]
    ppermute x0 -> x1, waiting for transfers between devices: none -> 5.2 us  [per_device(): other = lax.ppermute(source, 'z_low', [(0, 1), (1, 0)])]
    unnamed x0 -> x6, local copies, waits for them, and re-layouts: none -> 4.62 us
    ppermute x0 -> x1, starting transfers between devices: none -> 2.64 us  [per_device(): other = lax.ppermute(source, 'z_low', [(0, 1), (1, 0)])]
    broadcast_in_dim x2 -> x0, local copies, waits for them, and re-layouts: 1.99 us -> none  [per_device(): jnp.broadcast_to(operator.reshape(LINES, 128)[None], (Z, LINES, 128))]
    all_to_all x1, blocking collectives: 23.2 us -> 21.8 us  [per_device(): parts = lax.all_to_all(parts, ('z_low',) + GROUP + STRIP, 0, 0, tiled=True)]
  transfers between devices with their start and end apart: 1 -> 2, of which waited for: 1 -> 1; matrix products, arithmetic and copies ran while one was open for 3% -> 3% of each run, Pallas kernels for 10% -> 14%
where the time goes in v4:
time: 87.5 us; the launch traced here: 86.9 us
  blocking collectives  38.3 us (44%)
  starting transfers between devices  18.3 us (21%)
  Pallas kernels  16.9 us (19%)
  local copies, waits for them, and re-layouts  6.51 us (7%)
  waiting for transfers between devices  5.2 us (6%)
  other arithmetic  1.6 us (2%)
    all_to_all x1, blocking collectives, per_device(): parts = lax.all_to_all(parts, ('z_low',) + GROUP + STRIP, 0, 0, tiled=True)  21.8 us
    all_to_all x1, starting transfers between devices, per_device(): lines = lax.all_to_all(lines, 'z_half', 0, 0, tiled=True)  15.6 us
    pallas_call x2, Pallas kernels, roll_sources(): pl.pallas_call(roll_kernel, out_shape=jax.ShapeDtypeStruct((HALF_CAPS * 6...  12.5 us
    all_gather x1, blocking collectives, per_device(): source = lax.all_gather(source[None], GROUP, axis=0, tiled=True)  9.05 us
    all_to_all x1, blocking collectives, per_device(): found = lax.all_to_all(found, STRIP, 0, 0, tiled=True)  7.44 us
    ppermute x1, waiting for transfers between devices, per_device(): other = lax.ppermute(source, 'z_low', [(0, 1), (1, 0)])  5.2 us
    unnamed x6, local copies, waits for them, and re-layouts  4.62 us
    pallas_call x1, Pallas kernels, per_device(): pl.pallas_call(rotate_kernel, out_shape=(jax.ShapeDtypeStruct((GROUPS * B...  3.2 us
  transfers between devices with their start and end apart: 2, of which 1 were waited for; matrix products, arithmetic and copies ran while one was open for 3% of the time, Pallas kernels for 14%

profile of v4, /device:TPU:1, one launch (start us, length us, event | category | flops | bytes accessed | tf_op | source)
XLA Modules:
  0.0 86.9 jit_solution(2929646582116483631)
XLA Ops:
  0.0 0.9 %copy-done.2 = bf16[10,12,192]{2,1,0:T(8,128)(2,1)S(1)} copy-done((bf16[10,12,192]{2,1,0:T(8,128)(2,1)S(1)}, bf16[10,12,192]{2,1,0:T(8,128)(2,1)}, u32[]{:S(2)}) %copy-start.2) | copy-done | bytes 46104
  0.9 0.9 pack.1
  1.7 15.6 %all-to-all-start = ((bf16[8,180,128]{2,1,0:T(8,128)(2,1)}), bf16[8,180,128]{2,1,0:T(8,128)(2,1)}, u32[]{:S(2)}, u32[]{:S(2)}) async-start(bf16[8,180,128]{2,1,0:T(8,128)(2,1)} %pack.1), calls=%async_computation | async-start | bytes 753664 | tf_op jit(solution)/shard_map/all_to_all | solution.py:191
  17.4 0.7 convert_bitcast_fusion
  18.1 0.1 copy.9
  18.2 0.1 broadcast_in_dim.12
  18.3 0.1 convert_element_type.12
  18.3 0.9 %pad_maximum_fusion.1 = bf16[2,6,12,192]{3,0,2,1:T(2,128)(2,1)S(1)} fusion(bf16[2,3,12,192]{3,0,2,1:T(2,128)(2,1)} %param.6, bf16[2,3,12,192]{3,0,2,1:T(2,128)(2,1)} %param.5), kind=kLoop, calls=%fused_computation.1 | loop fusion | flops 27648 | bytes 110592 | tf_op jit(solution)/shard_map/concatenate | solution.py:193
  19.3 9.0 %all-gather = bf16[640,192]{1,0:T(8,128)(2,1)} all-gather(bf16[160,192]{1,0:T(8,128)(2,1)S(1)} %pad_maximum_fusion), channel_id=2, replica_groups=mesh['z_half'=8,'z_low'=2,'y_hi'=2,'core'=2,'x'=4,'y_lo'=2] {'y_hi','core'}, dimensions={0}, use_global_device_ids=true | all-gather | bytes 307200 | tf_op jit(solution)/shard_map/all_gather | solution.py:196
  28.4 2.6 %collective-permute-start = (bf16[4,160,192]{2,1,0:T(8,128)(2,1)}, bf16[4,160,192]{2,1,0:T(8,128)(2,1)}, u32[]{:S(2)}, u32[]{:S(2)}) collective-permute-start(bf16[4,160,192]{2,1,0:T(8,128)(2,1)} %bitcast.1.src_ref), channel_id=1, source_target_pairs={{0,32},{32,0},{1,33},{33,1},{2,34},{34,2},{3,35},{35,3},{4,36},{36... | collective-permute-start | bytes 737288 | tf_op jit(solution)/shard_map/ppermute | solution.py:197
  31.0 0.8 reshape.19
  31.9 0.1 reshape.20.weight_ref
  31.9 6.2 %roll.2.mine_ref = bf16[768,2304]{1,0:T(8,128)(2,1)S(1)} custom-call(bf16[4,160,192]{2,1,0:T(8,128)(2,1)} %bitcast.1.src_ref), custom_call_target="tpu_custom_call" | custom-call | flops 1000000000 | bytes 4194304 | tf_op jit(solution)/shard_map/roll/pallas_call | solution.py:164
  38.2 5.2 %collective-permute-done.src_ref = bf16[4,160,192]{2,1,0:T(8,128)(2,1)} collective-permute-done((bf16[4,160,192]{2,1,0:T(8,128)(2,1)}, bf16[4,160,192]{2,1,0:T(8,128)(2,1)}, u32[]{:S(2)}, u32[]{:S(2)}) %collective-permute-start) | collective-permute-done | bytes 245792 | tf_op jit(solution)/shard_map/ppermute | solution.py:197
  43.4 6.2 %roll.3.next_ref = bf16[768,2304]{1,0:T(8,128)(2,1)S(1)} custom-call(bf16[4,160,192]{2,1,0:T(8,128)(2,1)} %collective-permute-done.src_ref), custom_call_target="tpu_custom_call" | custom-call | flops 1000000000 | bytes 4194304 | tf_op jit(solution)/shard_map/roll/pallas_call | solution.py:164
  49.6 0.0 copy-start
  49.6 1.7 %copy-done = bf16[768,2304]{1,0:T(8,128)(2,1)} copy-done((bf16[768,2304]{1,0:T(8,128)(2,1)}, bf16[768,2304]{1,0:T(8,128)(2,1)S(1)}, u32[]{:S(2)}) %copy-start) | copy-done | bytes 3538968
  51.4 0.0 all-to-all-done.op_ref
  51.4 2.0 %copy-done.1 = bf16[768,2304]{1,0:T(8,128)(2,1)S(1)} copy-done((bf16[768,2304]{1,0:T(8,128)(2,1)S(1)}, bf16[768,2304]{1,0:T(8,128)(2,1)}, u32[]{:S(2)}) %copy-start.1) | copy-done | bytes 3538968
  53.4 3.2 %rotate.1 = (f32[64,16,128]{2,1,0:T(8,128)S(1)}, f32[8,80]{1,0:T(8,128)S(1)}) custom-call(bf16[768,2304]{1,0:T(8,128)(2,1)S(1)} %roll.2.mine_ref, bf16[768,2304]{1,0:T(8,128)(2,1)S(1)} %copy-done.1, bf16[8,180,128]{2,1,0:T(8,128)(2,1)} %all-to-all-done.op_ref, f32[8,80]{1,0:T(8,128)S(1)} %reshape.20.weight_ref, s32[1]{0:T(128)} %bitcast.3.side_ref), custom_call_target="tpu_custom_call" | custom-call | tf_op jit(solution)/shard_map/rotate/pallas_call | solution.py:201
  56.6 21.8 %all_to_all.15 = f32[64,16,128]{2,1,0:T(8,128)S(1)} all-to-all(f32[64,16,128]{2,1,0:T(8,128)S(1)} %get-tuple-element.17), channel_id=1, replica_groups=mesh['z_half'=8,'z_low'=2,'y_hi'=2,'core'=2,'x'=4,'y_lo'=2] {'z_low','y_..., dimensions={0} | all-to-all | bytes 1048576 | tf_op jit(solution)/shard_map/all_to_all | solution.py:217
  78.4 0.3 stokes.1
  78.8 7.4 %all_to_all.16 = f32[8,8,128]{2,1,0:T(8,128)S(1)} all-to-all(f32[8,8,128]{2,1,0:T(8,128)S(1)} %stokes.1), channel_id=1, replica_groups=mesh['z_half'=8,'z_low'=2,'y_hi'=2,'core'=2,'x'=4,'y_lo'=2] {'x','y_lo'}, dimensions={0} | all-to-all | bytes 65536 | tf_op jit(solution)/shard_map/all_to_all | solution.py:226
  86.2 0.7 copy.12
  (7 shorter events, 0.1 us)
Async XLA Ops:
  0.0 0.9 %copy-start.2 = (bf16[10,12,192]{2,1,0:T(8,128)(2,1)S(1)}, bf16[10,12,192]{2,1,0:T(8,128)(2,1)}, u32[]{:S(2)}) copy-start(bf16[10,12,192]{2,1,0:T(8,128)(2,1)} %op_ref.1) | copy-start | bytes 138244
  1.7 49.6 %all-to-all-start = ((bf16[8,180,128]{2,1,0:T(8,128)(2,1)}), bf16[8,180,128]{2,1,0:T(8,128)(2,1)}, u32[]{:S(2)}, u32[]{:S(2)}) async-start(bf16[8,180,128]{2,1,0:T(8,128)(2,1)} %pack.1), calls=%async_computation | async-start | bytes 753664 | tf_op jit(solution)/shard_map/all_to_all | solution.py:191
  28.4 15.0 %collective-permute-start = (bf16[4,160,192]{2,1,0:T(8,128)(2,1)}, bf16[4,160,192]{2,1,0:T(8,128)(2,1)}, u32[]{:S(2)}, u32[]{:S(2)}) collective-permute-start(bf16[4,160,192]{2,1,0:T(8,128)(2,1)} %bitcast.1.src_ref), channel_id=1, source_target_pairs={{0,32},{32,0},{1,33},{33,1},{2,34},{34,2},{3,35},{35,3},{4,36},{36... | collective-permute-start | bytes 737288 | tf_op jit(solution)/shard_map/ppermute | solution.py:197
  49.6 1.7 %copy-start = (bf16[768,2304]{1,0:T(8,128)(2,1)}, bf16[768,2304]{1,0:T(8,128)(2,1)S(1)}, u32[]{:S(2)}) copy-start(bf16[768,2304]{1,0:T(8,128)(2,1)S(1)} %roll.3.next_ref) | copy-start | bytes 10616836
  51.4 2.0 %copy-start.1 = (bf16[768,2304]{1,0:T(8,128)(2,1)S(1)}, bf16[768,2304]{1,0:T(8,128)(2,1)}, u32[]{:S(2)}) copy-start(bf16[768,2304]{1,0:T(8,128)(2,1)} %copy-done) | copy-start | bytes 10616836

commit v5 on v4

v5 whole, which is shorter than its diff:
```python
import jax
import jax.numpy as jnp
from jax import lax
from jax.experimental import pallas as pl
from jax.experimental.pallas import tpu as pltpu
from jax.sharding import Mesh
from jax.sharding import PartitionSpec as P

F32 = jnp.float32
BF16 = jnp.bfloat16

LAT_HERE = 12
LON = 192
COLS = LAT_HERE * LON
TGT = 16
ROWS_HERE = 10
Z = 8
QUAD = 4
PARITY = 2
BAND = 8
CAPS = 2 * QUAD
NODES = Z * ROWS_HERE
TILES = COLS // 128
LINES = ROWS_HERE * TILES
LEFT = 128 - NODES

CELL = ("z_half", "z_low", "y_hi", "core")
GROUP = ("y_hi", "core")
STRIP = ("x", "y_lo")

blob_radius = 0.5


def pack_kernel(op_ref, out_ref, lines):
    for r in range(ROWS_HERE):
        row = op_ref[r].astype(F32)
        high = row[:, 128:LON]
        at = r * TILES
        lines[at : at + LAT_HERE, :] = row[:, 0:128]
        lines[at + LAT_HERE : at + TILES, :] = jnp.concatenate([high[0:6], high[6:12]], axis=1)
    packed = lines[...].astype(BF16)
    for z in range(Z):
        out_ref[z] = packed


def roll_kernel(src_ref, rolled_ref, tiles):
    for p in range(QUAD):
        block = src_ref[p, 0:144, :].astype(F32)
        here = pl.ds(p * 144, 144)
        tiles[0, here, :] = block[:, 0:128]
        tiles[1, here, :] = jnp.concatenate([block[:, 128:192], block[:, 0:64]], axis=1)
        tiles[2, here, :] = block[:, 64:192]

    lane = lax.broadcasted_iota(jnp.int32, (TGT, 128), 1)

    def per_capsule(c, carry):
        column = src_ref[c // 2, 144:160, :].astype(F32)
        column = jnp.where(c % 2 == 0, column[:, 0:1], column[:, 96:97])
        shift = jnp.broadcast_to(column.astype(jnp.int32), (TGT, 128))
        take = jnp.bitwise_and(lane + shift, 127)
        goal = jnp.bitwise_and(lane - shift, 127)
        place = goal + shift
        early, late, low = place < 128, place < 256, goal < 64

        def rolled(value):
            return jnp.take_along_axis(value, take, axis=1, mode="promise_in_bounds").astype(BF16)

        for k in range(6):
            base = c * 72 + k * LAT_HERE
            to = pl.ds(pl.multiple_of((c * 6 + k) * TGT, TGT), TGT)

            def row(q, a):
                return jnp.broadcast_to(tiles[q, pl.ds(base + a, 1), :], (TGT, 128))

            for m in range(6):
                t = [row(q, m) for q in range(3)]
                u = [row(q, m + 6) for q in range(3)]
                first = jnp.where(early, t[0], jnp.where(late, t[1], t[2]))
                second = jnp.where(early, u[0], jnp.where(late, u[1], u[2]))
                high = jnp.where(
                    low,
                    jnp.where(early, t[1], t[2]),
                    jnp.where(early, u[2], jnp.where(late, u[0], u[1])),
                )
                rolled_ref[to, m * 128 : m * 128 + 128] = rolled(first)
                rolled_ref[to, (m + 6) * 128 : (m + 6) * 128 + 128] = rolled(second)
                rolled_ref[to, (m + 12) * 128 : (m + 12) * 128 + 128] = rolled(high)
        return carry

    lax.fori_loop(0, CAPS, per_capsule, 0)


def contract(rolled_ref, op_ref, lines, held, acc):
    for z in range(Z):
        lines[z * LINES : (z + 1) * LINES, :] = op_ref[z].astype(F32)
    for n in range(TILES):
        held[:, n * 128 : (n + 1) * 128] = lines[pl.ds(n, NODES, stride=TILES), :].astype(BF16)
    acc[...] = lax.dot_general(
        rolled_ref[...], held[...], (((1,), (1,)), ((), ())), preferred_element_type=F32
    )


def by_target(acc, store):
    upper = lax.broadcasted_iota(jnp.int32, (8, NODES), 0) < 4
    blank = jnp.zeros((8, 2 * 128 - 3 * NODES), F32)
    for c in range(CAPS):
        for half in range(2):
            found = [[], []]
            for pair in range(3):
                at = c * 96 + pair * 32 + half * 8
                one = acc[at : at + 8, :]
                two = acc[at + 16 : at + 24, :]
                found[0].append(jnp.where(upper, one, pltpu.roll(two, 4, 0)))
                found[1].append(jnp.where(upper, pltpu.roll(one, 4, 0), two))
            for j in range(2):
                a, b, d = found[j]
                store(
                    (c // 2) * BAND + (c % 2) * 4 + half * 2 + j,
                    jnp.concatenate([a, b[:, 0:LEFT]], axis=1),
                    jnp.concatenate([b[:, LEFT:NODES], d, blank], axis=1),
                )


def rotate_mine_kernel(rolled_ref, op_ref, out_ref, lines, held, acc):
    contract(rolled_ref, op_ref, lines, held, acc)

    def store(dest, one, two):
        out_ref[dest, 0:8, :] = one
        out_ref[dest, 8:16, :] = two

    by_target(acc, store)


def rotate_next_kernel(rolled_ref, op_ref, mine_ref, side_ref, out_ref, lines, held, acc):
    side = side_ref[0]
    out_ref[:, pl.ds(pl.multiple_of(side * 16, 16), 16), :] = mine_ref[...]
    contract(rolled_ref, op_ref, lines, held, acc)
    at = pl.multiple_of((1 - side) * 16, 16)

    def store(dest, one, two):
        out_ref[dest, pl.ds(at, 8), :] = one
        out_ref[dest, pl.ds(at + 8, 8), :] = two

    by_target(acc, store)


def stokes_kernel(parts_ref, weight_ref, out_ref):
    blob_sq = blob_radius * blob_radius
    pole = None
    sums = [jnp.zeros((4, 1), F32) for _ in range(3)]
    for n in range(QUAD * PARITY):
        g, rows_at = n // PARITY, (n % PARITY) * 16
        one = parts_ref[g, 0, rows_at : rows_at + 8, :]
        two = parts_ref[g, 0, rows_at + 8 : rows_at + 16, :]
        for b in range(1, BAND):
            one = one + parts_ref[g, b, rows_at : rows_at + 8, :]
            two = two + parts_ref[g, b, rows_at + 8 : rows_at + 16, :]
        rest = NODES - LEFT
        pairs = (
            one[:, 0:NODES],
            jnp.concatenate([one[:, NODES:128], two[:, 0:rest]], axis=1),
            two[:, rest : rest + NODES],
        )
        rows = [pairs[k // 2][4 * (k % 2) : 4 * (k % 2) + 4, :] for k in range(6)]
        if n == 0:
            pole = [rows[k][:, 0:1] for k in range(3)]
        weights = weight_ref[n : n + 1, :]
        d = [pole[k] - rows[k] for k in range(3)]
        f = rows[3:6]
        q = d[0] * d[0] + d[1] * d[1] + d[2] * d[2]
        along = d[0] * f[0] + d[1] * f[1] + d[2] * f[2]
        r = lax.rsqrt(q + blob_sq)
        kernel = weights * (r * r * r)
        near = (q + 2.0 * blob_sq) * kernel
        along = along * kernel
        for k in range(3):
            sums[k] = sums[k] + jnp.sum(near * f[k] + along * d[k], axis=1, keepdims=True)
    lane = lax.broadcasted_iota(jnp.int32, (4, 128), 1)
    packed = jnp.where(lane == 0, sums[0], jnp.where(lane == 1, sums[1], sums[2]))
    packed = jnp.concatenate([packed, jnp.zeros((4, 128), F32)], axis=0)
    for b in range(BAND):
        out_ref[b] = packed


def per_device(positions, densities, operator, target_shift, weights):
    vmem = pl.BlockSpec(memory_space=pltpu.VMEM)
    smem = pl.BlockSpec(memory_space=pltpu.SMEM)
    lines = pl.pallas_call(
        pack_kernel,
        out_shape=jax.ShapeDtypeStruct((Z, LINES, 128), BF16),
        in_specs=[vmem],
        out_specs=vmem,
        scratch_shapes=[pltpu.VMEM((LINES, 128), F32)],
        compiler_params=pltpu.CompilerParams(vmem_limit_bytes=16 * 2**20),
        name="pack",
    )(operator)
    lines, positions, densities, target_shift = lax.optimization_barrier(
        (lines, positions, densities, target_shift)
    )
    mine = lax.all_to_all(lines, "z_half", 0, 0, tiled=True)
    source = jnp.concatenate([positions, densities], axis=1).reshape(144, LON)
    shifts = jnp.broadcast_to(target_shift.T[:, :, None], (TGT, 2, LON // 2)).reshape(TGT, LON)
    source = jnp.concatenate([source, shifts.astype(BF16)], axis=0)
    source = lax.all_gather(source[None], GROUP, axis=0, tiled=True)
    mine, source = lax.optimization_barrier((mine, source))
    other = lax.ppermute(mine, "z_low", [(0, 1), (1, 0)])
    rolled = pl.pallas_call(
        roll_kernel,
        out_shape=jax.ShapeDtypeStruct((CAPS * 6 * TGT, COLS), BF16),
        in_specs=[vmem],
        out_specs=vmem,
        scratch_shapes=[pltpu.VMEM((3, QUAD * 144, 128), F32)],
        compiler_params=pltpu.CompilerParams(vmem_limit_bytes=24 * 2**20),
        cost_estimate=pl.CostEstimate(flops=10**9, bytes_accessed=2**22, transcendentals=0),
        name="roll",
    )(source)
    scratch = [
        pltpu.VMEM((Z * LINES, 128), F32),
        pltpu.VMEM((NODES, COLS), BF16),
        pltpu.VMEM((CAPS * 6 * TGT, NODES), F32),
    ]
    parts = pl.pallas_call(
        rotate_mine_kernel,
        out_shape=jax.ShapeDtypeStruct((QUAD * BAND, 16, 128), F32),
        in_specs=[vmem] * 2,
        out_specs=vmem,
        scratch_shapes=scratch,
        compiler_params=pltpu.CompilerParams(vmem_limit_bytes=24 * 2**20),
        cost_estimate=pl.CostEstimate(flops=10**9, bytes_accessed=2**22, transcendentals=0),
        name="rotate_mine",
    )(rolled, mine)
    side = lax.axis_index("z_low").astype(jnp.int32)[None]
    parts = pl.pallas_call(
        rotate_next_kernel,
        out_shape=jax.ShapeDtypeStruct((QUAD * BAND, 32, 128), F32),
        in_specs=[vmem] * 3 + [smem],
        out_specs=vmem,
        scratch_shapes=scratch,
        compiler_params=pltpu.CompilerParams(vmem_limit_bytes=24 * 2**20),
        name="rotate_next",
    )(rolled, other, parts, side)
    parts = lax.all_to_all(parts, GROUP + STRIP, 0, 0, tiled=True)
    weights = weights.reshape(Z, PARITY, QUAD, ROWS_HERE).transpose(2, 1, 0, 3)
    weights = weights.reshape(QUAD * PARITY, NODES)
    found = pl.pallas_call(
        stokes_kernel,
        out_shape=jax.ShapeDtypeStruct((BAND, 8, 128), F32),
        in_specs=[vmem] * 2,
        out_specs=vmem,
        compiler_params=pltpu.CompilerParams(vmem_limit_bytes=32 * 2**20),
        name="stokes",
    )(parts.reshape(QUAD, BAND, 32, 128), weights)
    found = lax.all_to_all(found, STRIP, 0, 0, tiled=True)
    return found[:, 0:4, 0:3].reshape(2, TGT, 3).transpose(0, 2, 1)


def solution(mesh):
    split = Mesh(mesh.devices.reshape(8, 2, 2, 2, 4, 2), CELL + STRIP)
    in_specs = (
        P(CELL, None, STRIP, None),
        P(CELL, None, STRIP, None),
        P(CELL, STRIP, None),
        P(CELL, None),
        P(),
    )
    return jax.shard_map(
        per_device, mesh=split, in_specs=in_specs, out_specs=P(CELL, None, None), check_vma=False
    )
```

time: 87.5 us -> 83.8 us (0.958)
  the two profiles are of different devices: /device:TPU:1 before, /device:TPU:64 now
where the time goes in v5:
time: 83.8 us; the launch traced here: 83.4 us
  waiting for transfers between devices  30.7 us (37%)
  starting transfers between devices  24 us (29%)
  blocking collectives  16.5 us (20%)
  Pallas kernels  8.36 us (10%)
  local copies, waits for them, and re-layouts  2.11 us (3%)
  other arithmetic  1.6 us (2%)
    all_to_all x1, starting transfers between devices, per_device(): mine = lax.all_to_all(lines, 'z_half', 0, 0, tiled=True)  14.7 us
    all_to_all x1, waiting for transfers between devices, per_device(): mine = lax.all_to_all(lines, 'z_half', 0, 0, tiled=True)  14.6 us
    all_to_all x1, waiting for transfers between devices, per_device(): parts = lax.all_to_all(parts, GROUP + STRIP, 0, 0, tiled=True)  11.5 us
    all_to_all x1, blocking collectives, per_device(): found = lax.all_to_all(found, STRIP, 0, 0, tiled=True)  8.71 us
    all_gather x1, blocking collectives, per_device(): source = lax.all_gather(source[None], GROUP, axis=0, tiled=True)  7.81 us
    all_to_all x1, starting transfers between devices, per_device(): parts = lax.all_to_all(parts, GROUP + STRIP, 0, 0, tiled=True)  7.32 us
    ppermute x1, waiting for transfers between devices, per_device(): other = lax.ppermute(mine, 'z_low', [(0, 1), (1, 0)])  4.71 us
    pallas_call x1, Pallas kernels, per_device(): pl.pallas_call(roll_kernel, out_shape=jax.ShapeDtypeStruct((CAPS * 6 * TG...  3.77 us
  transfers between devices with their start and end apart: 3, of which 3 were waited for; matrix products, arithmetic and copies ran while one was open for 3% of the time, Pallas kernels for 6%

profile of v5, /device:TPU:64, one launch (start us, length us, event | category | flops | bytes accessed | tf_op | source)
XLA Modules:
  0.0 83.4 jit_solution(15905062579885796526)
XLA Ops:
  0.0 0.9 %copy-done = bf16[10,12,192]{2,1,0:T(8,128)(2,1)S(1)} copy-done((bf16[10,12,192]{2,1,0:T(8,128)(2,1)S(1)}, bf16[10,12,192]{2,1,0:T(8,128)(2,1)}, u32[]{:S(2)}) %copy-start) | copy-done | bytes 46104
  0.9 0.9 %pack.1 = bf16[8,180,128]{2,1,0:T(8,128)(2,1)} custom-call(bf16[10,12,192]{2,1,0:T(8,128)(2,1)S(1)} %copy-done), custom_call_target="tpu_custom_call" | custom-call | tf_op jit(solution)/shard_map/pack/pallas_call | solution.py:188
  1.7 14.7 %all-to-all-start = ((bf16[8,180,128]{2,1,0:T(8,128)(2,1)}), bf16[8,180,128]{2,1,0:T(8,128)(2,1)S(1)}, u32[]{:S(2)}, u32[]{:S(2)}) async-start(bf16[8,180,128]{2,1,0:T(8,128)(2,1)} %pack.1), calls=%async_computation | async-start | bytes 753664 | tf_op jit(solution)/shard_map/all_to_all | solution.py:200
  16.5 0.9 %pad_maximum_fusion.1 = bf16[2,6,12,192]{3,0,2,1:T(2,128)(2,1)S(1)} fusion(bf16[2,3,12,192]{3,0,2,1:T(2,128)(2,1)} %param.6, bf16[2,3,12,192]{3,0,2,1:T(2,128)(2,1)} %param.5), kind=kLoop, calls=%fused_computation.1 | loop fusion | flops 27648 | bytes 110592 | tf_op jit(solution)/shard_map/concatenate | solution.py:201
  17.4 0.7 convert_bitcast_fusion
  18.1 0.1 copy.9
  18.2 0.1 broadcast_in_dim.12
  18.3 0.1 convert_element_type.12
  18.4 7.8 %all-gather = bf16[640,192]{1,0:T(8,128)(2,1)S(1)} all-gather(bf16[160,192]{1,0:T(8,128)(2,1)S(1)} %pad_maximum_fusion), channel_id=2, replica_groups=mesh['z_half'=8,'z_low'=2,'y_hi'=2,'core'=2,'x'=4,'y_lo'=2] {'y_hi','core'}, dimensions={0}, use_global_device_ids=true | all-gather | bytes 307200 | tf_op jit(solution)/shard_map/all_gather | solution.py:204
  26.2 14.6 %all-to-all-done.op_ref = bf16[8,180,128]{2,1,0:T(8,128)(2,1)S(1)} async-done(((bf16[8,180,128]{2,1,0:T(8,128)(2,1)}), bf16[8,180,128]{2,1,0:T(8,128)(2,1)S(1)}, u32[]{:S(2)}, u32[]{:S(2)}) %all-to-all-start) | async-done | bytes 368672 | tf_op jit(solution)/shard_map/all_to_all | solution.py:200
  40.8 1.9 %collective-permute-start = (bf16[8,180,128]{2,1,0:T(8,128)(2,1)S(1)}, bf16[8,180,128]{2,1,0:T(8,128)(2,1)S(1)}, u32[]{:S(2)}, u32[]{:S(2)}) collective-permute-start(bf16[8,180,128]{2,1,0:T(8,128)(2,1)S(1)} %all-to-all-done.op_ref), channel_id=1, source_target_pairs={{0,32},{32,0},{1,33},{33,1},{2,34},{34,2},{3,35},{35,3},{4,36},{36... | collective-permute-start | bytes 1105928 | tf_op jit(solution)/shard_map/ppermute | solution.py:206
  42.7 3.8 %roll.1.rolled_ref = bf16[768,2304]{1,0:T(8,128)(2,1)S(1)} custom-call(bf16[4,160,192]{2,1,0:T(8,128)(2,1)S(1)} %bitcast.11), custom_call_target="tpu_custom_call" | custom-call | flops 1000000000 | bytes 4194304 | tf_op jit(solution)/shard_map/roll/pallas_call | solution.py:207
  46.5 1.3 %rotate_mine.1.mine_ref = f32[32,16,128]{2,1,0:T(8,128)S(1)} custom-call(bf16[768,2304]{1,0:T(8,128)(2,1)S(1)} %roll.1.rolled_ref, bf16[8,180,128]{2,1,0:T(8,128)(2,1)S(1)} %all-to-all-done.op_ref), custom_call_target="tpu_custom_call" | custom-call | flops 1000000000 | bytes 4194304 | tf_op jit(solution)/shard_map/rotate_mine/pallas_call | solution.py:222
  47.8 0.0 copy-start.1
  47.8 4.7 %collective-permute-done.op_ref = bf16[8,180,128]{2,1,0:T(8,128)(2,1)S(1)} collective-permute-done((bf16[8,180,128]{2,1,0:T(8,128)(2,1)S(1)}, bf16[8,180,128]{2,1,0:T(8,128)(2,1)S(1)}, u32[]{:S(2)}, u32[]{:S(2)}) %collective-permute-start) | collective-permute-done | bytes 368672 | tf_op jit(solution)/shard_map/ppermute | solution.py:206
  52.5 2.1 %rotate_next.1 = f32[32,32,128]{2,1,0:T(8,128)} custom-call(bf16[768,2304]{1,0:T(8,128)(2,1)S(1)} %roll.1.rolled_ref, bf16[8,180,128]{2,1,0:T(8,128)(2,1)S(1)} %collective-permute-done.op_ref, f32[32,16,128]{2,1,0:T(8,128)S(1)} %rotate_mine.1.mine_ref, s32[1]{0:T(128)} %bitcast.2.side_ref), custom_call_target="tpu_custom_call" | custom-call | tf_op jit(solution)/shard_map/rotate_next/pallas_call | solution.py:233
  54.6 7.3 %all-to-all-start.1 = ((f32[32,32,128]{2,1,0:T(8,128)}), f32[32,32,128]{2,1,0:T(8,128)S(1)}, u32[]{:S(2)}, u32[]{:S(2)}) async-start(f32[32,32,128]{2,1,0:T(8,128)} %rotate_next.1), calls=%async_computation.1 | async-start | bytes 1048576 | tf_op jit(solution)/shard_map/all_to_all | solution.py:242
  61.9 0.0 copy-done.1
  61.9 0.1 reshape.20
  62.1 0.1 reshape.21.weight_ref
  62.2 11.5 %all-to-all-done.1 = f32[32,32,128]{2,1,0:T(8,128)S(1)} async-done(((f32[32,32,128]{2,1,0:T(8,128)}), f32[32,32,128]{2,1,0:T(8,128)S(1)}, u32[]{:S(2)}, u32[]{:S(2)}) %all-to-all-start.1) | async-done | bytes 524320 | tf_op jit(solution)/shard_map/all_to_all | solution.py:242
  73.6 0.3 stokes.1
  74.0 8.7 %all_to_all.15 = f32[8,8,128]{2,1,0:T(8,128)S(1)} all-to-all(f32[8,8,128]{2,1,0:T(8,128)S(1)} %stokes.1), channel_id=1, replica_groups=mesh['z_half'=8,'z_low'=2,'y_hi'=2,'core'=2,'x'=4,'y_lo'=2] {'x','y_lo'}, dimensions={0} | all-to-all | bytes 65536 | tf_op jit(solution)/shard_map/all_to_all | solution.py:253
  82.7 0.7 copy.12
  (6 shorter events, 0.1 us)
Async XLA Ops:
  0.0 0.9 %copy-start = (bf16[10,12,192]{2,1,0:T(8,128)(2,1)S(1)}, bf16[10,12,192]{2,1,0:T(8,128)(2,1)}, u32[]{:S(2)}) copy-start(bf16[10,12,192]{2,1,0:T(8,128)(2,1)} %op_ref.1) | copy-start | bytes 138244
  1.7 39.1 %all-to-all-start = ((bf16[8,180,128]{2,1,0:T(8,128)(2,1)}), bf16[8,180,128]{2,1,0:T(8,128)(2,1)S(1)}, u32[]{:S(2)}, u32[]{:S(2)}) async-start(bf16[8,180,128]{2,1,0:T(8,128)(2,1)} %pack.1), calls=%async_computation | async-start | bytes 753664 | tf_op jit(solution)/shard_map/all_to_all | solution.py:200
  40.8 11.7 %collective-permute-start = (bf16[8,180,128]{2,1,0:T(8,128)(2,1)S(1)}, bf16[8,180,128]{2,1,0:T(8,128)(2,1)S(1)}, u32[]{:S(2)}, u32[]{:S(2)}) collective-permute-start(bf16[8,180,128]{2,1,0:T(8,128)(2,1)S(1)} %all-to-all-done.op_ref), channel_id=1, source_target_pairs={{0,32},{32,0},{1,33},{33,1},{2,34},{34,2},{3,35},{35,3},{4,36},{36... | collective-permute-start | bytes 1105928 | tf_op jit(solution)/shard_map/ppermute | solution.py:206
  47.8 14.1 %copy-start.1 = (f32[640]{0:T(1024)S(1)}, f32[640]{0:T(1024)}, u32[]{:S(2)}) copy-start(f32[640]{0:T(1024)} %param.9) | copy-start | bytes 7684
  54.6 19.0 %all-to-all-start.1 = ((f32[32,32,128]{2,1,0:T(8,128)}), f32[32,32,128]{2,1,0:T(8,128)S(1)}, u32[]{:S(2)}, u32[]{:S(2)}) async-start(f32[32,32,128]{2,1,0:T(8,128)} %rotate_next.1), calls=%async_computation.1 | async-start | bytes 1048576 | tf_op jit(solution)/shard_map/all_to_all | solution.py:242

commit v6 on v5

v6 whole, which is shorter than its diff:
```python
import jax
import jax.numpy as jnp
from jax import lax
from jax.experimental import pallas as pl
from jax.experimental.pallas import tpu as pltpu
from jax.sharding import Mesh
from jax.sharding import PartitionSpec as P

F32 = jnp.float32
BF16 = jnp.bfloat16

LAT_HERE = 12
LON = 192
COLS = LAT_HERE * LON
TGT = 16
ROWS_HERE = 10
Z = 8
GROUPS = 8
BAND = 8
CAPS = 2 * GROUPS
NODES = Z * ROWS_HERE
TILES = COLS // 128
LINES = ROWS_HERE * TILES
LEFT = 128 - NODES
HIGH_AT = 160
SOURCE_LINES = 240
HALF_ROWS = CAPS // 2 * 6 * TGT

CELL = ("z_half", "z_low", "y_hi", "core")
GROUP = ("z_low", "y_hi", "core")
STRIP = ("x", "y_lo")

blob_radius = 0.5


def pack_kernel(op_ref, out_ref, lines):
    for r in range(ROWS_HERE):
        row = op_ref[r].astype(F32)
        high = row[:, 128:LON]
        at = r * TILES
        lines[at : at + LAT_HERE, :] = row[:, 0:128]
        lines[at + LAT_HERE : at + TILES, :] = jnp.concatenate([high[0:6], high[6:12]], axis=1)
    packed = lines[...].astype(BF16)
    for z in range(Z):
        out_ref[z] = packed


def pack_source_kernel(source_ref, shift_ref, out_ref):
    rows = source_ref[...].astype(F32)
    out_ref[0:144, :] = rows[:, 0:128].astype(BF16)
    high = jnp.concatenate([rows[0:72, 128:LON], rows[72:144, 128:LON]], axis=1)
    high = jnp.concatenate([high, jnp.zeros((8, 128), F32)], axis=0)
    out_ref[HIGH_AT:SOURCE_LINES, :] = high.astype(BF16)
    same = lax.broadcasted_iota(jnp.int32, (TGT, TGT), 0) == lax.broadcasted_iota(
        jnp.int32, (TGT, TGT), 1
    )
    columns = []
    for i in range(2):
        shift = jnp.broadcast_to(shift_ref[i : i + 1, :].astype(F32), (TGT, TGT))
        column = jnp.sum(jnp.where(same, shift, 0.0), axis=1, keepdims=True)
        columns.append(jnp.broadcast_to(column, (TGT, 64)))
    out_ref[144:HIGH_AT, :] = jnp.concatenate(columns, axis=1).astype(BF16)


def roll_half(src_ref, half, rolled_ref, tiles):
    base_p = half * (GROUPS // 2)
    for p in range(GROUPS // 2):
        high = src_ref[base_p + p, HIGH_AT:SOURCE_LINES, :].astype(F32)[0:72, :]
        for i in range(2):
            here = pl.ds(p * 144 + i * 72, 72)
            low = src_ref[base_p + p, 0:144, :].astype(F32)[72 * i : 72 * i + 72, :]
            rest = high[:, 64 * i : 64 * i + 64]
            tiles[0, here, :] = low
            tiles[1, here, :] = jnp.concatenate([rest, low[:, 0:64]], axis=1)
            tiles[2, here, :] = jnp.concatenate([low[:, 64:128], rest], axis=1)

    lane = lax.broadcasted_iota(jnp.int32, (TGT, 128), 1)

    def per_capsule(c, carry):
        column = src_ref[base_p + c // 2, 144:HIGH_AT, :].astype(F32)
        column = jnp.where(c % 2 == 0, column[:, 0:1], column[:, 64:65])
        shift = jnp.broadcast_to(column.astype(jnp.int32), (TGT, 128))
        take = jnp.bitwise_and(lane + shift, 127)
        goal = jnp.bitwise_and(lane - shift, 127)
        place = goal + shift
        early, late, low = place < 128, place < 256, goal < 64

        def rolled(value):
            return jnp.take_along_axis(value, take, axis=1, mode="promise_in_bounds").astype(BF16)

        for k in range(6):
            base = c * 72 + k * LAT_HERE
            to = pl.ds(pl.multiple_of((c * 6 + k) * TGT, TGT), TGT)

            def row(q, a):
                return jnp.broadcast_to(tiles[q, pl.ds(base + a, 1), :], (TGT, 128))

            for m in range(6):
                t = [row(q, m) for q in range(3)]
                u = [row(q, m + 6) for q in range(3)]
                first = jnp.where(early, t[0], jnp.where(late, t[1], t[2]))
                second = jnp.where(early, u[0], jnp.where(late, u[1], u[2]))
                high = jnp.where(
                    low,
                    jnp.where(early, t[1], t[2]),
                    jnp.where(early, u[2], jnp.where(late, u[0], u[1])),
                )
                rolled_ref[to, m * 128 : m * 128 + 128] = rolled(first)
                rolled_ref[to, (m + 6) * 128 : (m + 6) * 128 + 128] = rolled(second)
                rolled_ref[to, (m + 12) * 128 : (m + 12) * 128 + 128] = rolled(high)
        return carry

    lax.fori_loop(0, CAPS // 2, per_capsule, 0)


def roll_kernel(src_ref, rolled_ref, tiles):
    roll_half(src_ref, 0, rolled_ref, tiles)


def rotate_kernel(src_ref, rolled_ref, op_ref, out_ref, tiles, rolled, lines, held, acc):
    roll_half(src_ref, 1, rolled, tiles)
    for z in range(Z):
        lines[z * LINES : (z + 1) * LINES, :] = op_ref[z].astype(F32)
    for n in range(TILES):
        held[:, n * 128 : (n + 1) * 128] = lines[pl.ds(n, NODES, stride=TILES), :].astype(BF16)
    for i, half_ref in enumerate((rolled_ref, rolled)):
        acc[i * HALF_ROWS : (i + 1) * HALF_ROWS, :] = lax.dot_general(
            half_ref[...], held[...], (((1,), (1,)), ((), ())), preferred_element_type=F32
        )
    upper = lax.broadcasted_iota(jnp.int32, (8, NODES), 0) < 4
    blank = jnp.zeros((8, 2 * 128 - 3 * NODES), F32)
    for c in range(CAPS):
        for half in range(2):
            found = [[], []]
            for pair in range(3):
                at = c * 96 + pair * 32 + half * 8
                one = acc[at : at + 8, :]
                two = acc[at + 16 : at + 24, :]
                found[0].append(jnp.where(upper, one, pltpu.roll(two, 4, 0)))
                found[1].append(jnp.where(upper, pltpu.roll(one, 4, 0), two))
            for j in range(2):
                dest = (c // 2) * BAND + (c % 2) * 4 + half * 2 + j
                a, b, d = found[j]
                out_ref[dest, 0:8, :] = jnp.concatenate([a, b[:, 0:LEFT]], axis=1)
                out_ref[dest, 8:16, :] = jnp.concatenate([b[:, LEFT:NODES], d, blank], axis=1)


def stokes_kernel(parts_ref, weight_ref, out_ref):
    blob_sq = blob_radius * blob_radius
    pole = None
    sums = [jnp.zeros((4, 1), F32) for _ in range(3)]
    for g in range(GROUPS):
        whole = parts_ref[g, 0]
        for b in range(1, BAND):
            whole = whole + parts_ref[g, b]
        one, two = whole[0:8, :], whole[8:16, :]
        rest = NODES - LEFT
        pairs = (
            one[:, 0:NODES],
            jnp.concatenate([one[:, NODES:128], two[:, 0:rest]], axis=1),
            two[:, rest : rest + NODES],
        )
        rows = [pairs[k // 2][4 * (k % 2) : 4 * (k % 2) + 4, :] for k in range(6)]
        if g == 0:
            pole = [rows[k][:, 0:1] for k in range(3)]
        weights = weight_ref[g : g + 1, :]
        d = [pole[k] - rows[k] for k in range(3)]
        f = rows[3:6]
        q = d[0] * d[0] + d[1] * d[1] + d[2] * d[2]
        along = d[0] * f[0] + d[1] * f[1] + d[2] * f[2]
        r = lax.rsqrt(q + blob_sq)
        kernel = weights * (r * r * r)
        near = (q + 2.0 * blob_sq) * kernel
        along = along * kernel
        for k in range(3):
            sums[k] = sums[k] + jnp.sum(near * f[k] + along * d[k], axis=1, keepdims=True)
    lane = lax.broadcasted_iota(jnp.int32, (4, 128), 1)
    packed = jnp.where(lane == 0, sums[0], jnp.where(lane == 1, sums[1], sums[2]))
    packed = jnp.concatenate([packed, jnp.zeros((4, 128), F32)], axis=0)
    for b in range(BAND):
        out_ref[b] = packed


def per_device(positions, densities, operator, target_shift, weights):
    vmem = pl.BlockSpec(memory_space=pltpu.VMEM)
    lines = pl.pallas_call(
        pack_kernel,
        out_shape=jax.ShapeDtypeStruct((Z, LINES, 128), BF16),
        in_specs=[vmem],
        out_specs=vmem,
        scratch_shapes=[pltpu.VMEM((LINES, 128), F32)],
        compiler_params=pltpu.CompilerParams(vmem_limit_bytes=16 * 2**20),
        name="pack",
    )(operator)
    lines, positions, densities, target_shift = lax.optimization_barrier(
        (lines, positions, densities, target_shift)
    )
    lines = lax.all_to_all(lines, "z_half", 0, 0, tiled=True)
    source = jnp.concatenate([positions, densities], axis=1).reshape(144, LON)
    source = pl.pallas_call(
        pack_source_kernel,
        out_shape=jax.ShapeDtypeStruct((SOURCE_LINES, 128), BF16),
        in_specs=[vmem] * 2,
        out_specs=vmem,
        compiler_params=pltpu.CompilerParams(vmem_limit_bytes=16 * 2**20),
        name="pack_source",
    )(source, target_shift)
    source = lax.all_gather(source[None], GROUP, axis=0, tiled=True)
    rolled = pl.pallas_call(
        roll_kernel,
        out_shape=jax.ShapeDtypeStruct((HALF_ROWS, COLS), BF16),
        in_specs=[vmem],
        out_specs=vmem,
        scratch_shapes=[pltpu.VMEM((3, GROUPS * 72, 128), F32)],
        compiler_params=pltpu.CompilerParams(vmem_limit_bytes=16 * 2**20),
        cost_estimate=pl.CostEstimate(flops=10**9, bytes_accessed=2**22, transcendentals=0),
        name="roll",
    )(source)
    parts = pl.pallas_call(
        rotate_kernel,
        out_shape=jax.ShapeDtypeStruct((GROUPS * BAND, 16, 128), F32),
        in_specs=[vmem] * 3,
        out_specs=vmem,
        scratch_shapes=[
            pltpu.VMEM((3, GROUPS * 72, 128), F32),
            pltpu.VMEM((HALF_ROWS, COLS), BF16),
            pltpu.VMEM((Z * LINES, 128), F32),
            pltpu.VMEM((NODES, COLS), BF16),
            pltpu.VMEM((CAPS * 6 * TGT, NODES), F32),
        ],
        compiler_params=pltpu.CompilerParams(vmem_limit_bytes=16 * 2**20),
        name="rotate",
    )(source, rolled, lines)
    parts = lax.all_to_all(parts, GROUP + STRIP, 0, 0, tiled=True)
    weights = weights.reshape(Z, GROUPS, ROWS_HERE).transpose(1, 0, 2).reshape(GROUPS, NODES)
    found = pl.pallas_call(
        stokes_kernel,
        out_shape=jax.ShapeDtypeStruct((BAND, 8, 128), F32),
        in_specs=[vmem] * 2,
        out_specs=vmem,
        compiler_params=pltpu.CompilerParams(vmem_limit_bytes=32 * 2**20),
        name="stokes",
    )(parts.reshape(GROUPS, BAND, 16, 128), weights)
    found = lax.all_to_all(found, STRIP, 0, 0, tiled=True)
    return found[:, 0:4, 0:3].reshape(2, TGT, 3).transpose(0, 2, 1)


def solution(mesh):
    split = Mesh(mesh.devices.reshape(8, 2, 2, 2, 4, 2), CELL + STRIP)
    in_specs = (
        P(CELL, None, STRIP, None),
        P(CELL, None, STRIP, None),
        P(CELL, STRIP, None),
        P(CELL, None),
        P(),
    )
    return jax.shard_map(
        per_device, mesh=split, in_specs=in_specs, out_specs=P(CELL, None, None), check_vma=False
    )
```

time: 83.8 us -> 87.7 us (1.047)
  the two profiles are of different devices: /device:TPU:64 before, /device:TPU:1 now
where the time goes in v6:
time: 87.7 us; the launch traced here: 86.2 us
  blocking collectives  34.4 us (39%)
  starting transfers between devices  21.5 us (25%)
  waiting for transfers between devices  12.3 us (14%)
  Pallas kernels  12 us (14%)
  local copies, waits for them, and re-layouts  5.09 us (6%)
  other arithmetic  0.9 us (1%)
    all_gather x1, blocking collectives, per_device(): source = lax.all_gather(source[None], GROUP, axis=0, tiled=True)  26.9 us
    all_to_all x1, starting transfers between devices, per_device(): lines = lax.all_to_all(lines, 'z_half', 0, 0, tiled=True)  15.6 us
    all_to_all x1, waiting for transfers between devices, per_device(): parts = lax.all_to_all(parts, GROUP + STRIP, 0, 0, tiled=True)  12.2 us
    all_to_all x1, blocking collectives, per_device(): found = lax.all_to_all(found, STRIP, 0, 0, tiled=True)  7.44 us
    pallas_call x1, Pallas kernels, per_device(): pl.pallas_call(rotate_kernel, out_shape=jax.ShapeDtypeStruct((GROUPS * BA...  6.94 us
    all_to_all x1, starting transfers between devices, per_device(): parts = lax.all_to_all(parts, GROUP + STRIP, 0, 0, tiled=True)  5.9 us
    unnamed x12, local copies, waits for them, and re-layouts  4.16 us
    pallas_call x1, Pallas kernels, per_device(): pl.pallas_call(roll_kernel, out_shape=jax.ShapeDtypeStruct((HALF_ROWS, CO...  3.74 us
  transfers between devices with their start and end apart: 2, of which 1 were waited for; matrix products, arithmetic and copies ran while one was open for 1% of the time, Pallas kernels for 4%

profile of v6, /device:TPU:1, one launch (start us, length us, event | category | flops | bytes accessed | tf_op | source)
XLA Modules:
  0.0 86.2 jit_solution(3965079301164090938)
XLA Ops:
  0.0 0.9 %copy-done.3 = bf16[10,12,192]{2,1,0:T(8,128)(2,1)S(1)} copy-done((bf16[10,12,192]{2,1,0:T(8,128)(2,1)S(1)}, bf16[10,12,192]{2,1,0:T(8,128)(2,1)}, u32[]{:S(2)}) %copy-start.3) | copy-done | bytes 46104
  0.9 0.9 pack.1
  1.7 15.6 %all-to-all-start = ((bf16[8,180,128]{2,1,0:T(8,128)(2,1)}), bf16[8,180,128]{2,1,0:T(8,128)(2,1)}, u32[]{:S(2)}, u32[]{:S(2)}) async-start(bf16[8,180,128]{2,1,0:T(8,128)(2,1)} %pack.1), calls=%async_computation | async-start | bytes 753664 | tf_op jit(solution)/shard_map/all_to_all | solution.py:198
  17.4 0.9 %pad_maximum_fusion = bf16[2,6,12,192]{3,0,2,1:T(2,128)(2,1)S(1)} fusion(bf16[2,3,12,192]{3,0,2,1:T(2,128)(2,1)} %param.6, bf16[2,3,12,192]{3,0,2,1:T(2,128)(2,1)} %param.5), kind=kLoop, calls=%fused_computation | loop fusion | flops 27648 | bytes 110592 | tf_op jit(solution)/shard_map/concatenate | solution.py:199
  18.3 0.0 copy-start.4
  18.4 0.7 copy-done.4
  19.0 0.1 pack_source.1
  19.1 26.9 %all-gather = bf16[1920,128]{1,0:T(8,128)(2,1)S(1)} all-gather(bf16[240,128]{1,0:T(8,128)(2,1)S(1)} %pack_source.1), channel_id=2, replica_groups=mesh['z_half'=8,'z_low'=2,'y_hi'=2,'core'=2,'x'=4,'y_lo'=2] {'z_low','y_..., dimensions={0}, use_global_device_ids=true | all-gather | bytes 552960 | tf_op jit(solution)/shard_map/all_gather | solution.py:208
  46.0 3.7 %roll.1.rolled_ref = bf16[768,2304]{1,0:T(8,128)(2,1)S(1)} custom-call(bf16[8,240,128]{2,1,0:T(8,128)(2,1)S(1)} %bitcast.5), custom_call_target="tpu_custom_call" | custom-call | flops 1000000000 | bytes 4194304 | tf_op jit(solution)/shard_map/roll/pallas_call | solution.py:209
  49.8 0.0 copy-start
  49.8 0.8 copy-done
  50.5 0.0 all-to-all-done.op_ref
  50.6 1.0 %copy-done.1 = bf16[1920,128]{1,0:T(8,128)(2,1)S(1)} copy-done((bf16[1920,128]{1,0:T(8,128)(2,1)S(1)}, bf16[1920,128]{1,0:T(8,128)(2,1)}, u32[]{:S(2)}) %copy-start.1) | copy-done | bytes 491544
  51.6 6.9 %rotate.1 = f32[64,16,128]{2,1,0:T(8,128)S(1)} custom-call(bf16[8,240,128]{2,1,0:T(8,128)(2,1)S(1)} %bitcast.6, bf16[768,2304]{1,0:T(8,128)(2,1)S(1)} %roll.1.rolled_ref, bf16[8,180,128]{2,1,0:T(8,128)(2,1)} %all-to-all-done.op_ref), custom_call_target="tpu_custom_call" | custom-call | tf_op jit(solution)/shard_map/rotate/pallas_call | solution.py:219
  58.5 0.0 copy-start.2
  58.5 0.8 copy-done.2
  59.3 5.9 %all-to-all-start.1 = ((f32[64,16,128]{2,1,0:T(8,128)}), f32[64,16,128]{2,1,0:T(8,128)S(1)}, u32[]{:S(2)}, u32[]{:S(2)}) async-start(f32[64,16,128]{2,1,0:T(8,128)} %copy-done.2), calls=%async_computation.1 | async-start | bytes 1048576 | tf_op jit(solution)/shard_map/all_to_all | solution.py:234
  65.2 0.0 copy-done.5
  65.3 0.1 reshape.17
  65.4 0.1 reshape.18.weight_ref
  65.5 12.2 %all-to-all-done.1 = f32[64,16,128]{2,1,0:T(8,128)S(1)} async-done(((f32[64,16,128]{2,1,0:T(8,128)}), f32[64,16,128]{2,1,0:T(8,128)S(1)}, u32[]{:S(2)}, u32[]{:S(2)}) %all-to-all-start.1) | async-done | bytes 524320 | tf_op jit(solution)/shard_map/all_to_all | solution.py:234
  77.7 0.3 stokes.1
  78.1 7.4 %all_to_all.15 = f32[8,8,128]{2,1,0:T(8,128)S(1)} all-to-all(f32[8,8,128]{2,1,0:T(8,128)S(1)} %stokes.1), channel_id=1, replica_groups=mesh['z_half'=8,'z_low'=2,'y_hi'=2,'core'=2,'x'=4,'y_lo'=2] {'x','y_lo'}, dimensions={0} | all-to-all | bytes 65536 | tf_op jit(solution)/shard_map/all_to_all | solution.py:244
  85.5 0.7 copy.11
  (7 shorter events, 0.1 us)
Async XLA Ops:
  0.0 0.9 %copy-start.3 = (bf16[10,12,192]{2,1,0:T(8,128)(2,1)S(1)}, bf16[10,12,192]{2,1,0:T(8,128)(2,1)}, u32[]{:S(2)}) copy-start(bf16[10,12,192]{2,1,0:T(8,128)(2,1)} %op_ref.1) | copy-start | bytes 138244
  1.7 48.8 %all-to-all-start = ((bf16[8,180,128]{2,1,0:T(8,128)(2,1)}), bf16[8,180,128]{2,1,0:T(8,128)(2,1)}, u32[]{:S(2)}, u32[]{:S(2)}) async-start(bf16[8,180,128]{2,1,0:T(8,128)(2,1)} %pack.1), calls=%async_computation | async-start | bytes 753664 | tf_op jit(solution)/shard_map/all_to_all | solution.py:198
  18.3 0.7 copy-start.4
  49.8 0.8 copy-start
  50.6 1.0 %copy-start.1 = (bf16[1920,128]{1,0:T(8,128)(2,1)S(1)}, bf16[1920,128]{1,0:T(8,128)(2,1)}, u32[]{:S(2)}) copy-start(bf16[1920,128]{1,0:T(8,128)(2,1)} %copy-done) | copy-start | bytes 1474564
  51.6 13.7 %copy-start.5 = (f32[640]{0:T(1024)S(1)}, f32[640]{0:T(1024)}, u32[]{:S(2)}) copy-start(f32[640]{0:T(1024)} %param.9) | copy-start | bytes 7684
  58.5 0.8 copy-start.2
  59.3 18.4 %all-to-all-start.1 = ((f32[64,16,128]{2,1,0:T(8,128)}), f32[64,16,128]{2,1,0:T(8,128)S(1)}, u32[]{:S(2)}, u32[]{:S(2)}) async-start(f32[64,16,128]{2,1,0:T(8,128)} %copy-done.2), calls=%async_computation.1 | async-start | bytes 1048576 | tf_op jit(solution)/shard_map/all_to_all | solution.py:234

commit v7 on v5

--- a/solution.py
+++ b/solution.py
@@ -131,7 +131,10 @@
     by_target(acc, store)
 
 
-def rotate_next_kernel(rolled_ref, op_ref, mine_ref, side_ref, out_ref, lines, held, acc):
+def rotate_next_kernel(
+    rolled_ref, op_ref, mine_ref, weight_ref, side_ref, out_ref, weight_out_ref, lines, held, acc
+):
+    weight_out_ref[...] = weight_ref[...]
     side = side_ref[0]
     out_ref[:, pl.ds(pl.multiple_of(side * 16, 16), 16), :] = mine_ref[...]
     contract(rolled_ref, op_ref, lines, held, acc)
@@ -182,6 +185,16 @@
         out_ref[b] = packed
 
 
+def swap_pairs():
+    length = Z * PARITY
+    pairs = []
+    for z in range(length):
+        for core in range(2):
+            other = (z + 1 if (z + core) % 2 == 0 else z - 1) % length
+            pairs.append((z * 2 + core, other * 2 + core))
+    return pairs
+
+
 def per_device(positions, densities, operator, target_shift, weights):
     vmem = pl.BlockSpec(memory_space=pltpu.VMEM)
     smem = pl.BlockSpec(memory_space=pltpu.SMEM)
@@ -194,16 +207,14 @@
         compiler_params=pltpu.CompilerParams(vmem_limit_bytes=16 * 2**20),
         name="pack",
     )(operator)
-    lines, positions, densities, target_shift = lax.optimization_barrier(
-        (lines, positions, densities, target_shift)
+    lines, positions, densities, target_shift, weights = lax.optimization_barrier(
+        (lines, positions, densities, target_shift, weights)
     )
     mine = lax.all_to_all(lines, "z_half", 0, 0, tiled=True)
     source = jnp.concatenate([positions, densities], axis=1).reshape(144, LON)
     shifts = jnp.broadcast_to(target_shift.T[:, :, None], (TGT, 2, LON // 2)).reshape(TGT, LON)
     source = jnp.concatenate([source, shifts.astype(BF16)], axis=0)
     source = lax.all_gather(source[None], GROUP, axis=0, tiled=True)
-    mine, source = lax.optimization_barrier((mine, source))
-    other = lax.ppermute(mine, "z_low", [(0, 1), (1, 0)])
     rolled = pl.pallas_call(
         roll_kernel,
         out_shape=jax.ShapeDtypeStruct((CAPS * 6 * TGT, COLS), BF16),
@@ -214,6 +225,10 @@
         cost_estimate=pl.CostEstimate(flops=10**9, bytes_accessed=2**22, transcendentals=0),
         name="roll",
     )(source)
+    weights = weights.reshape(Z, PARITY, QUAD, ROWS_HERE).transpose(2, 1, 0, 3)
+    weights = weights.reshape(QUAD * PARITY, NODES)
+    mine, rolled, weights = lax.optimization_barrier((mine, rolled, weights))
+    other = lax.ppermute(mine, ("z_half", "z_low", "core"), swap_pairs())
     scratch = [
         pltpu.VMEM((Z * LINES, 128), F32),
         pltpu.VMEM((NODES, COLS), BF16),
@@ -230,18 +245,19 @@
         name="rotate_mine",
     )(rolled, mine)
     side = lax.axis_index("z_low").astype(jnp.int32)[None]
-    parts = pl.pallas_call(
+    parts, weights = pl.pallas_call(
         rotate_next_kernel,
-        out_shape=jax.ShapeDtypeStruct((QUAD * BAND, 32, 128), F32),
-        in_specs=[vmem] * 3 + [smem],
-        out_specs=vmem,
+        out_shape=(
+            jax.ShapeDtypeStruct((QUAD * BAND, 32, 128), F32),
+            jax.ShapeDtypeStruct((QUAD * PARITY, NODES), F32),
+        ),
+        in_specs=[vmem] * 4 + [smem],
+        out_specs=(vmem, vmem),
         scratch_shapes=scratch,
         compiler_params=pltpu.CompilerParams(vmem_limit_bytes=24 * 2**20),
         name="rotate_next",
-    )(rolled, other, parts, side)
+    )(rolled, other, parts, weights, side)
     parts = lax.all_to_all(parts, GROUP + STRIP, 0, 0, tiled=True)
-    weights = weights.reshape(Z, PARITY, QUAD, ROWS_HERE).transpose(2, 1, 0, 3)
-    weights = weights.reshape(QUAD * PARITY, NODES)
     found = pl.pallas_call(
         stokes_kernel,
         out_shape=jax.ShapeDtypeStruct((BAND, 8, 128), F32),

time: 83.8 us -> 82.1 us (0.980)
  the two profiles are of different devices: /device:TPU:64 before, /device:TPU:1 now
where the time goes in v7:
time: 82.1 us; the launch traced here: 80.5 us
  blocking collectives  36.6 us (45%)
  starting transfers between devices  17.6 us (21%)
  waiting for transfers between devices  12.3 us (15%)
  Pallas kernels  9.57 us (12%)
  local copies, waits for them, and re-layouts  2.79 us (3%)
  other arithmetic  1.6 us (2%)
    all_to_all x1, blocking collectives, per_device(): parts = lax.all_to_all(parts, GROUP + STRIP, 0, 0, tiled=True)  20.1 us
    all_to_all x1, starting transfers between devices, per_device(): mine = lax.all_to_all(lines, 'z_half', 0, 0, tiled=True)  15.6 us
    all_gather x1, blocking collectives, per_device(): source = lax.all_gather(source[None], GROUP, axis=0, tiled=True)  8.6 us
    all_to_all x1, blocking collectives, per_device(): found = lax.all_to_all(found, STRIP, 0, 0, tiled=True)  7.91 us
    all_to_all x1, waiting for transfers between devices, per_device(): mine = lax.all_to_all(lines, 'z_half', 0, 0, tiled=True)  6.66 us
    ppermute x1, waiting for transfers between devices, per_device(): other = lax.ppermute(mine, ('z_half', 'z_low', 'core'), swap_pairs())  5.64 us
    pallas_call x1, Pallas kernels, per_device(): pl.pallas_call(roll_kernel, out_shape=jax.ShapeDtypeStruct((CAPS * 6 * TG...  3.77 us
    pallas_call x1, Pallas kernels, per_device(): pl.pallas_call(rotate_next_kernel, out_shape=(jax.ShapeDtypeStruct((QUAD...  2.31 us
  transfers between devices with their start and end apart: 2, of which 2 were waited for; matrix products, arithmetic and copies ran while one was open for 4% of the time, Pallas kernels for 8%

profile of v7, /device:TPU:1, one launch (start us, length us, event | category | flops | bytes accessed | tf_op | source)
XLA Modules:
  0.0 80.5 jit_solution(16650249515054577585)
XLA Ops:
  0.0 0.0 copy-start
  0.0 0.9 %copy-done = bf16[10,12,192]{2,1,0:T(8,128)(2,1)S(1)} copy-done((bf16[10,12,192]{2,1,0:T(8,128)(2,1)S(1)}, bf16[10,12,192]{2,1,0:T(8,128)(2,1)}, u32[]{:S(2)}) %copy-start) | copy-done | bytes 46104
  0.9 0.9 %pack.1 = bf16[8,180,128]{2,1,0:T(8,128)(2,1)} custom-call(bf16[10,12,192]{2,1,0:T(8,128)(2,1)S(1)} %copy-done), custom_call_target="tpu_custom_call" | custom-call | tf_op jit(solution)/shard_map/pack/pallas_call | solution.py:201
  1.7 15.6 %all-to-all-start = ((bf16[8,180,128]{2,1,0:T(8,128)(2,1)}), bf16[8,180,128]{2,1,0:T(8,128)(2,1)}, u32[]{:S(2)}, u32[]{:S(2)}) async-start(bf16[8,180,128]{2,1,0:T(8,128)(2,1)} %pack.1), calls=%async_computation | async-start | bytes 753664 | tf_op jit(solution)/shard_map/all_to_all | solution.py:213
  17.4 0.7 convert_bitcast_fusion
  18.1 0.1 copy.9
  18.2 0.1 broadcast_in_dim.12
  18.3 0.1 convert_element_type.12
  18.3 0.8 %reshape.19 = f32[8,2,4,10]{3,2,1,0:T(4,128)S(1)} reshape(f32[640]{0:T(1024)} %param.9) | data formatting | bytes 5120 | tf_op jit(solution)/shard_map/reshape | solution.py:228
  19.2 0.1 reshape.20.weight_ref
  19.3 0.9 %pad_maximum_fusion.1 = bf16[2,6,12,192]{3,0,2,1:T(2,128)(2,1)S(1)} fusion(bf16[2,3,12,192]{3,0,2,1:T(2,128)(2,1)} %param.6, bf16[2,3,12,192]{3,0,2,1:T(2,128)(2,1)} %param.5), kind=kLoop, calls=%fused_computation.1 | loop fusion | flops 27648 | bytes 110592 | tf_op jit(solution)/shard_map/concatenate | solution.py:214
  20.3 8.6 %all-gather = bf16[640,192]{1,0:T(8,128)(2,1)S(1)} all-gather(bf16[160,192]{1,0:T(8,128)(2,1)S(1)} %pad_maximum_fusion), channel_id=2, replica_groups=mesh['z_half'=8,'z_low'=2,'y_hi'=2,'core'=2,'x'=4,'y_lo'=2] {'y_hi','core'}, dimensions={0}, use_global_device_ids=true | all-gather | bytes 307200 | tf_op jit(solution)/shard_map/all_gather | solution.py:217
  28.9 3.8 %roll.1.rolled_ref = bf16[768,2304]{1,0:T(8,128)(2,1)S(1)} custom-call(bf16[4,160,192]{2,1,0:T(8,128)(2,1)S(1)} %bitcast.11), custom_call_target="tpu_custom_call" | custom-call | flops 1000000000 | bytes 4194304 | tf_op jit(solution)/shard_map/roll/pallas_call | solution.py:218
  32.6 6.7 %all-to-all-done.op_ref = bf16[8,180,128]{2,1,0:T(8,128)(2,1)} async-done(((bf16[8,180,128]{2,1,0:T(8,128)(2,1)}), bf16[8,180,128]{2,1,0:T(8,128)(2,1)}, u32[]{:S(2)}, u32[]{:S(2)}) %all-to-all-start) | async-done | bytes 368672 | tf_op jit(solution)/shard_map/all_to_all | solution.py:213
  39.3 1.9 %collective-permute-start = (bf16[8,180,128]{2,1,0:T(8,128)(2,1)}, bf16[8,180,128]{2,1,0:T(8,128)(2,1)}, u32[]{:S(2)}, u32[]{:S(2)}) collective-permute-start(bf16[8,180,128]{2,1,0:T(8,128)(2,1)} %all-to-all-done.op_ref), channel_id=1, source_target_pairs={{0,32},{8,488},{32,0},{40,72},{64,96},{72,40},{96,64},{104,136},{1... | collective-permute-start | bytes 1105928 | tf_op jit(solution)/shard_map/ppermute | solution.py:231
  41.2 2.3 %rotate_mine.1.mine_ref = f32[32,16,128]{2,1,0:T(8,128)S(1)} custom-call(bf16[768,2304]{1,0:T(8,128)(2,1)S(1)} %roll.1.rolled_ref, bf16[8,180,128]{2,1,0:T(8,128)(2,1)} %all-to-all-done.op_ref), custom_call_target="tpu_custom_call" | custom-call | flops 1000000000 | bytes 4194304 | tf_op jit(solution)/shard_map/rotate_mine/pallas_call | solution.py:237
  43.5 5.6 %collective-permute-done.op_ref = bf16[8,180,128]{2,1,0:T(8,128)(2,1)} collective-permute-done((bf16[8,180,128]{2,1,0:T(8,128)(2,1)}, bf16[8,180,128]{2,1,0:T(8,128)(2,1)}, u32[]{:S(2)}, u32[]{:S(2)}) %collective-permute-start) | collective-permute-done | bytes 368672 | tf_op jit(solution)/shard_map/ppermute | solution.py:231
  49.1 2.3 %rotate_next.1 = (f32[32,32,128]{2,1,0:T(8,128)S(1)}, f32[8,80]{1,0:T(8,128)S(1)}) custom-call(bf16[768,2304]{1,0:T(8,128)(2,1)S(1)} %roll.1.rolled_ref, bf16[8,180,128]{2,1,0:T(8,128)(2,1)} %collective-permute-done.op_ref, f32[32,16,128]{2,1,0:T(8,128)S(1)} %rotate_mine.1.mine_ref, f32[8,80]{1,0:T(8,128)S(1)} %reshape.20.weight_ref, s32[1]{0:T(128)} %bitcast.3.side_ref), custom_call_target="tpu_custom_call" | custom-call | tf_op jit(solution)/shard_map/rotate_next/pallas_call | solution.py:248
  51.5 20.1 %all_to_all.15 = f32[32,32,128]{2,1,0:T(8,128)S(1)} all-to-all(f32[32,32,128]{2,1,0:T(8,128)S(1)} %get-tuple-element.23), channel_id=1, replica_groups=mesh['z_half'=8,'z_low'=2,'y_hi'=2,'core'=2,'x'=4,'y_lo'=2] {'y_hi','cor..., dimensions={0} | all-to-all | bytes 1048576 | tf_op jit(solution)/shard_map/all_to_all | solution.py:260
  71.6 0.3 stokes.1
  72.0 7.9 %all_to_all.16 = f32[8,8,128]{2,1,0:T(8,128)S(1)} all-to-all(f32[8,8,128]{2,1,0:T(8,128)S(1)} %stokes.1), channel_id=1, replica_groups=mesh['z_half'=8,'z_low'=2,'y_hi'=2,'core'=2,'x'=4,'y_lo'=2] {'x','y_lo'}, dimensions={0} | all-to-all | bytes 65536 | tf_op jit(solution)/shard_map/all_to_all | solution.py:269
  79.9 0.7 copy.12
  (5 shorter events, 0.1 us)
Async XLA Ops:
  0.0 0.9 %copy-start = (bf16[10,12,192]{2,1,0:T(8,128)(2,1)S(1)}, bf16[10,12,192]{2,1,0:T(8,128)(2,1)}, u32[]{:S(2)}) copy-start(bf16[10,12,192]{2,1,0:T(8,128)(2,1)} %op_ref.1) | copy-start | bytes 138244
  1.7 37.5 %all-to-all-start = ((bf16[8,180,128]{2,1,0:T(8,128)(2,1)}), bf16[8,180,128]{2,1,0:T(8,128)(2,1)}, u32[]{:S(2)}, u32[]{:S(2)}) async-start(bf16[8,180,128]{2,1,0:T(8,128)(2,1)} %pack.1), calls=%async_computation | async-start | bytes 753664 | tf_op jit(solution)/shard_map/all_to_all | solution.py:213
  39.3 9.9 %collective-permute-start = (bf16[8,180,128]{2,1,0:T(8,128)(2,1)}, bf16[8,180,128]{2,1,0:T(8,128)(2,1)}, u32[]{:S(2)}, u32[]{:S(2)}) collective-permute-start(bf16[8,180,128]{2,1,0:T(8,128)(2,1)} %all-to-all-done.op_ref), channel_id=1, source_target_pairs={{0,32},{8,488},{32,0},{40,72},{64,96},{72,40},{96,64},{104,136},{1... | collective-permute-start | bytes 1105928 | tf_op jit(solution)/shard_map/ppermute | solution.py:231

commit v8 on v2

--- a/solution.py
+++ b/solution.py
@@ -19,7 +19,10 @@
 BAND = 8
 CAPS = 2 * QUAD
 NODES = Z * ROWS_HERE
-LINES = ROWS_HERE * COLS // 128
+TILES = COLS // 128
+LINES = ROWS_HERE * TILES
+HIGH_AT = 160
+SOURCE_LINES = 240
 
 CELL = ("z", "y_hi", "core")
 GROUP = ("y_hi", "core")
@@ -28,60 +31,88 @@
 blob_radius = 0.5
 
 
+def pack_kernel(op_ref, source_ref, shift_ref, op_out_ref, source_out_ref, lines):
+    for r in range(ROWS_HERE):
+        row = op_ref[r].astype(F32)
+        high = row[:, 128:LON]
+        at = r * TILES
+        lines[at : at + LAT_HERE, :] = row[:, 0:128]
+        lines[at + LAT_HERE : at + TILES, :] = jnp.concatenate([high[0:6], high[6:12]], axis=1)
+    op_out_ref[0] = lines[...].astype(BF16)
+    rows = source_ref[...].astype(F32)
+    low = rows[:, 0:128].astype(BF16)
+    high = jnp.concatenate([rows[0:72, 128:LON], rows[72:144, 128:LON]], axis=1)
+    high = jnp.concatenate([high, jnp.zeros((8, 128), F32)], axis=0).astype(BF16)
+    same = lax.broadcasted_iota(jnp.int32, (TGT, TGT), 0) == lax.broadcasted_iota(
+        jnp.int32, (TGT, TGT), 1
+    )
+    columns = []
+    for i in range(2):
+        shift = jnp.broadcast_to(shift_ref[i : i + 1, :].astype(F32), (TGT, TGT))
+        column = jnp.sum(jnp.where(same, shift, 0.0), axis=1, keepdims=True)
+        columns.append(jnp.broadcast_to(column, (TGT, 64)))
+    columns = jnp.concatenate(columns, axis=1).astype(BF16)
+    for p in range(QUAD):
+        source_out_ref[p, 0:144, :] = low
+        source_out_ref[p, 144:HIGH_AT, :] = columns
+        source_out_ref[p, HIGH_AT:SOURCE_LINES, :] = high
+
+
 def roll_kernel(src_ref, rolled_ref, tiles):
     for p in range(QUAD):
-        block = src_ref[p, 0:144, :].astype(F32)
-        here = pl.ds(p * 144, 144)
-        tiles[0, here, :] = block[:, 0:128]
-        tiles[1, here, :] = jnp.concatenate([block[:, 128:192], block[:, 0:64]], axis=1)
-        tiles[2, here, :] = block[:, 64:192]
+        high = src_ref[p, HIGH_AT:SOURCE_LINES, :].astype(F32)[0:72, :]
+        for i in range(2):
+            here = pl.ds(p * 144 + i * 72, 72)
+            low = src_ref[p, 0:144, :].astype(F32)[72 * i : 72 * i + 72, :]
+            rest = high[:, 64 * i : 64 * i + 64]
+            tiles[0, here, :] = low
+            tiles[1, here, :] = jnp.concatenate([rest, low[:, 0:64]], axis=1)
+            tiles[2, here, :] = jnp.concatenate([low[:, 64:128], rest], axis=1)
 
     lane = lax.broadcasted_iota(jnp.int32, (TGT, 128), 1)
-    low_half = lane < 64
-
-    for c in range(CAPS):
-        at = (c % 2) * 96
-        shift = src_ref[c // 2, 144:160, at : at + 1].astype(F32).astype(jnp.int32)
-        place = lane + jnp.broadcast_to(shift, (TGT, 128))
-        even = jnp.bitwise_and(place, 127)
-        odd = jnp.bitwise_and(place + 64, 127)
-        e0, e1, e2 = place < 128, place < 256, place + 128 < 256
-        h0, h1 = place - 64 < 128, place + 64 < 256
-        h2 = place + 64 < 128
-
-        def per_component(k, carry):
+
+    def per_capsule(c, carry):
+        column = src_ref[c // 2, 144:HIGH_AT, :].astype(F32)
+        column = jnp.where(c % 2 == 0, column[:, 0:1], column[:, 64:65])
+        shift = jnp.broadcast_to(column.astype(jnp.int32), (TGT, 128))
+        take = jnp.bitwise_and(lane + shift, 127)
+        goal = jnp.bitwise_and(lane - shift, 127)
+        place = goal + shift
+        early, late, low = place < 128, place < 256, goal < 64
+
+        def rolled(value):
+            return jnp.take_along_axis(value, take, axis=1, mode="promise_in_bounds").astype(BF16)
+
+        for k in range(6):
             base = c * 72 + k * LAT_HERE
             to = pl.ds(pl.multiple_of((c * 6 + k) * TGT, TGT), TGT)
-            for m in range(LAT_HERE // 2):
-
-                def picked(a, where):
-                    return [
-                        jnp.take_along_axis(
-                            jnp.broadcast_to(tiles[q, pl.ds(base + a, 1), :], (TGT, 128)),
-                            where,
-                            axis=1,
-                            mode="promise_in_bounds",
-                        )
-                        for q in range(3)
-                    ]
-
-                g = picked(2 * m, even)
-                h = picked(2 * m + 1, odd)
-                first = jnp.where(e0, g[0], jnp.where(e1, g[1], g[2]))
-                middle = jnp.where(low_half, jnp.where(e2, g[1], g[2]), jnp.where(h0, h[0], h[1]))
-                last = jnp.where(h2, h[0], jnp.where(h1, h[1], h[2]))
-                for n, value in enumerate((first, middle, last)):
-                    rolled_ref[to, pl.ds((3 * m + n) * 128, 128)] = value.astype(BF16)
-            return carry
-
-        lax.fori_loop(0, 6, per_component, 0)
+
+            def row(q, a):
+                return jnp.broadcast_to(tiles[q, pl.ds(base + a, 1), :], (TGT, 128))
+
+            for m in range(6):
+                t = [row(q, m) for q in range(3)]
+                u = [row(q, m + 6) for q in range(3)]
+                first = jnp.where(early, t[0], jnp.where(late, t[1], t[2]))
+                second = jnp.where(early, u[0], jnp.where(late, u[1], u[2]))
+                high = jnp.where(
+                    low,
+                    jnp.where(early, t[1], t[2]),
+                    jnp.where(early, u[2], jnp.where(late, u[0], u[1])),
+                )
+                rolled_ref[to, m * 128 : m * 128 + 128] = rolled(first)
+                rolled_ref[to, (m + 6) * 128 : (m + 6) * 128 + 128] = rolled(second)
+                rolled_ref[to, (m + 12) * 128 : (m + 12) * 128 + 128] = rolled(high)
+        return carry
+
+    lax.fori_loop(0, CAPS, per_capsule, 0)
 
 
 def rotate_kernel(rolled_ref, op_ref, out_ref, lines, held, acc):
     for z in range(Z):
         lines[z * LINES : (z + 1) * LINES, :] = op_ref[z].astype(F32)
-    for n in range(COLS // 128):
-        rows = lines[pl.ds(n, NODES, stride=COLS // 128), :]
+    for n in range(TILES):
+        rows = lines[pl.ds(n, NODES, stride=TILES), :]
         held[:, n * 128 : (n + 1) * 128] = rows.astype(BF16)
     acc[...] = lax.dot_general(
         rolled_ref[...], held[...], (((1,), (1,)), ((), ())), preferred_element_type=F32
@@ -147,22 +178,28 @@
 
 def per_device(positions, densities, operator, target_shift, weights):
     vmem = pl.BlockSpec(memory_space=pltpu.VMEM)
-    lines = operator.reshape(LINES, 128)
-    lines = lax.all_gather(lines[None], "z", axis=0, tiled=True)
     source = jnp.concatenate([positions, densities], axis=1).reshape(144, LON)
-    shifts = jnp.broadcast_to(target_shift.T[:, :, None], (TGT, 2, LON // 2)).reshape(TGT, LON)
-    source = jnp.concatenate([source, shifts.astype(BF16)], axis=0)
-    source = lax.all_to_all(
-        jnp.broadcast_to(source[None], (QUAD, *source.shape)), GROUP, 0, 0, tiled=True
-    )
+    lines, source = pl.pallas_call(
+        pack_kernel,
+        out_shape=(
+            jax.ShapeDtypeStruct((1, LINES, 128), BF16),
+            jax.ShapeDtypeStruct((QUAD, SOURCE_LINES, 128), BF16),
+        ),
+        in_specs=[vmem] * 3,
+        out_specs=(vmem, vmem),
+        scratch_shapes=[pltpu.VMEM((LINES, 128), F32)],
+        compiler_params=pltpu.CompilerParams(vmem_limit_bytes=16 * 2**20),
+        name="pack",
+    )(operator, source, target_shift)
+    source = lax.all_to_all(source, GROUP, 0, 0, tiled=True)
+    lines = lax.all_gather(lines, "z", axis=0, tiled=True)
     rolled = pl.pallas_call(
         roll_kernel,
         out_shape=jax.ShapeDtypeStruct((CAPS * 6 * TGT, COLS), BF16),
         in_specs=[vmem],
         out_specs=vmem,
         scratch_shapes=[pltpu.VMEM((3, QUAD * 144, 128), F32)],
-        compiler_params=pltpu.CompilerParams(vmem_limit_bytes=32 * 2**20),
-        cost_estimate=pl.CostEstimate(flops=10**9, bytes_accessed=2**23, transcendentals=0),
+        compiler_params=pltpu.CompilerParams(vmem_limit_bytes=24 * 2**20),
         name="roll",
     )(source)
     parts = pl.pallas_call(
@@ -175,7 +212,7 @@
             pltpu.VMEM((NODES, COLS), BF16),
             pltpu.VMEM((CAPS * 6 * TGT, NODES), F32),
         ],
-        compiler_params=pltpu.CompilerParams(vmem_limit_bytes=32 * 2**20),
+        compiler_params=pltpu.CompilerParams(vmem_limit_bytes=24 * 2**20),
         name="rotate",
     )(rolled, lines)
     parts = lax.all_to_all(parts, GROUP + STRIP, 0, 0, tiled=True)

time: 87.1 us -> 82.3 us (0.945)
  Pallas kernels: 10.6 us -> 6.98 us
    pallas_call x1, Pallas kernels: 8.18 us -> 3.74 us  [per_device(): pl.pallas_call(roll_kernel, out_shape=jax.ShapeDtypeStruct((CAPS * 6 * TG...]
    unnamed x2 -> x6, local copies, waits for them, and re-layouts: 0.01 us -> 1.57 us
    another operation x1 -> x0, local copies, waits for them, and re-layouts: 1.01 us -> none  [per_device(): lines = lax.all_gather(lines[None], 'z', axis=0, tiled=True)]
  transfers between devices with their start and end apart: 2 -> 2, of which waited for: 1 -> 1; matrix products, arithmetic and copies ran while one was open for 1% -> 0% of each run, Pallas kernels for 0% -> 0%
where the time goes in v8:
time: 82.3 us; the launch traced here: 81.8 us
  blocking collectives  36.8 us (45%)
  starting transfers between devices  24 us (29%)
  waiting for transfers between devices  10.5 us (13%)
  Pallas kernels  6.98 us (8%)
  local copies, waits for them, and re-layouts  2.53 us (3%)
  other arithmetic  0.9 us (1%)
    all_gather x1, blocking collectives, per_device(): lines = lax.all_gather(lines, 'z', axis=0, tiled=True)  28.9 us
    all_to_all x1, starting transfers between devices, per_device(): parts = lax.all_to_all(parts, GROUP + STRIP, 0, 0, tiled=True)  13.8 us
    all_to_all x1, waiting for transfers between devices, per_device(): parts = lax.all_to_all(parts, GROUP + STRIP, 0, 0, tiled=True)  10.5 us
    all_to_all x1, starting transfers between devices, per_device(): source = lax.all_to_all(source, GROUP, 0, 0, tiled=True)  10.2 us
    all_to_all x1, blocking collectives, per_device(): found = lax.all_to_all(found, STRIP, 0, 0, tiled=True)  7.91 us
    pallas_call x1, Pallas kernels, per_device(): pl.pallas_call(roll_kernel, out_shape=jax.ShapeDtypeStruct((CAPS * 6 * TG...  3.74 us
    pallas_call x1, Pallas kernels, per_device(): pl.pallas_call(rotate_kernel, out_shape=jax.ShapeDtypeStruct((QUAD * BAND...  2.18 us
  transfers between devices with their start and end apart: 2, of which 1 were waited for; matrix products, arithmetic and copies ran while one was open for 0% of the time, Pallas kernels for 0%

profile of v8, /device:TPU:1, one launch (start us, length us, event | category | flops | bytes accessed | tf_op | source)
XLA Modules:
  0.0 81.8 jit_solution(209874167586924001)
XLA Ops:
  0.0 0.9 %pad_maximum_fusion = bf16[2,6,12,192]{3,0,2,1:T(2,128)(2,1)S(1)} fusion(bf16[2,3,12,192]{3,0,2,1:T(2,128)(2,1)} %param.6, bf16[2,3,12,192]{3,0,2,1:T(2,128)(2,1)} %param.5), kind=kLoop, calls=%fused_computation | loop fusion | flops 27648 | bytes 110592 | tf_op jit(solution)/shard_map/concatenate | solution.py:181
  1.0 0.0 copy-start
  1.0 0.9 %copy-done = bf16[10,12,192]{2,1,0:T(8,128)(2,1)S(1)} copy-done((bf16[10,12,192]{2,1,0:T(8,128)(2,1)S(1)}, bf16[10,12,192]{2,1,0:T(8,128)(2,1)}, u32[]{:S(2)}) %copy-start) | copy-done | bytes 46104
  1.9 0.0 copy-start.1
  1.9 0.7 copy-done.1
  2.5 0.8 pack.1
  3.3 10.2 %all-to-all-start = ((bf16[4,240,128]{2,1,0:T(8,128)(2,1)}), bf16[4,240,128]{2,1,0:T(8,128)(2,1)S(1)}, u32[]{:S(2)}, u32[]{:S(2)}) async-start(bf16[4,240,128]{2,1,0:T(8,128)(2,1)} %get-tuple-element.7), calls=%async_computation | async-start | bytes 491520 | tf_op jit(solution)/shard_map/all_to_all | solution.py:194
  13.6 28.9 %all_gather.3.op_ref = bf16[16,180,128]{2,1,0:T(8,128)(2,1)S(1)} all-gather(bf16[1,180,128]{2,1,0:T(8,128)(2,1)S(1)} %get-tuple-element.8), channel_id=1, replica_groups=mesh['z'=16,'y_hi'=2,'core'=2,'x'=4,'y_lo'=2] {'z'}, dimensions={0}, use_global_device_ids=true | all-gather | bytes 783360 | tf_op jit(solution)/shard_map/all_gather | solution.py:195
  42.5 0.0 all-to-all-done.src_ref
  42.5 3.7 %roll.1.rolled_ref = bf16[768,2304]{1,0:T(8,128)(2,1)S(1)} custom-call(bf16[4,240,128]{2,1,0:T(8,128)(2,1)S(1)} %all-to-all-done.src_ref), custom_call_target="tpu_custom_call" | custom-call | tf_op jit(solution)/shard_map/roll/pallas_call | solution.py:196
  46.3 0.0 copy-start.2
  46.3 2.2 %rotate.1 = f32[32,32,128]{2,1,0:T(8,128)} custom-call(bf16[768,2304]{1,0:T(8,128)(2,1)S(1)} %roll.1.rolled_ref, bf16[16,180,128]{2,1,0:T(8,128)(2,1)S(1)} %all_gather.3.op_ref), custom_call_target="tpu_custom_call" | custom-call | tf_op jit(solution)/shard_map/rotate/pallas_call | solution.py:205
  48.4 13.8 %all-to-all-start.1 = ((f32[32,32,128]{2,1,0:T(8,128)}), f32[32,32,128]{2,1,0:T(8,128)S(1)}, u32[]{:S(2)}, u32[]{:S(2)}) async-start(f32[32,32,128]{2,1,0:T(8,128)} %rotate.1), calls=%async_computation.1 | async-start | bytes 1048576 | tf_op jit(solution)/shard_map/all_to_all | solution.py:218
  62.2 0.0 copy-done.2
  62.2 0.1 reshape.17
  62.4 0.1 reshape.18.weight_ref
  62.5 10.5 %all-to-all-done.1 = f32[32,32,128]{2,1,0:T(8,128)S(1)} async-done(((f32[32,32,128]{2,1,0:T(8,128)}), f32[32,32,128]{2,1,0:T(8,128)S(1)}, u32[]{:S(2)}, u32[]{:S(2)}) %all-to-all-start.1) | async-done | bytes 524320 | tf_op jit(solution)/shard_map/all_to_all | solution.py:218
  73.0 0.3 stokes.1
  73.3 7.9 %all_to_all.15 = f32[8,8,128]{2,1,0:T(8,128)S(1)} all-to-all(f32[8,8,128]{2,1,0:T(8,128)S(1)} %stokes.1), channel_id=1, replica_groups=mesh['z'=16,'y_hi'=2,'core'=2,'x'=4,'y_lo'=2] {'x','y_lo'}, dimensions={0} | all-to-all | bytes 65536 | tf_op jit(solution)/shard_map/all_to_all | solution.py:228
  81.2 0.7 copy.14
  (4 shorter events, 0.1 us)
Async XLA Ops:
  1.0 0.9 %copy-start = (bf16[10,12,192]{2,1,0:T(8,128)(2,1)S(1)}, bf16[10,12,192]{2,1,0:T(8,128)(2,1)}, u32[]{:S(2)}) copy-start(bf16[10,12,192]{2,1,0:T(8,128)(2,1)} %op_ref.1) | copy-start | bytes 138244
  1.9 0.7 copy-start.1
  3.3 39.2 %all-to-all-start = ((bf16[4,240,128]{2,1,0:T(8,128)(2,1)}), bf16[4,240,128]{2,1,0:T(8,128)(2,1)S(1)}, u32[]{:S(2)}, u32[]{:S(2)}) async-start(bf16[4,240,128]{2,1,0:T(8,128)(2,1)} %get-tuple-element.7), calls=%async_computation | async-start | bytes 491520 | tf_op jit(solution)/shard_map/all_to_all | solution.py:194
  46.3 16.0 %copy-start.2 = (f32[640]{0:T(1024)S(1)}, f32[640]{0:T(1024)}, u32[]{:S(2)}) copy-start(f32[640]{0:T(1024)} %param.9) | copy-start | bytes 7684
  48.4 24.6 %all-to-all-start.1 = ((f32[32,32,128]{2,1,0:T(8,128)}), f32[32,32,128]{2,1,0:T(8,128)S(1)}, u32[]{:S(2)}, u32[]{:S(2)}) async-start(f32[32,32,128]{2,1,0:T(8,128)} %rotate.1), calls=%async_computation.1 | async-start | bytes 1048576 | tf_op jit(solution)/shard_map/all_to_all | solution.py:218

commit v9 on v8

--- a/solution.py
+++ b/solution.py
@@ -15,51 +15,62 @@
 TGT = 16
 ROWS_HERE = 10
 Z = 16
-QUAD = 4
+SIDES = 2
 BAND = 8
-CAPS = 2 * QUAD
+CAPS = 2 * SIDES
 NODES = Z * ROWS_HERE
 TILES = COLS // 128
 LINES = ROWS_HERE * TILES
+SENT_LINES = 184
 HIGH_AT = 160
 SOURCE_LINES = 240
 
 CELL = ("z", "y_hi", "core")
-GROUP = ("y_hi", "core")
 STRIP = ("x", "y_lo")
 
 blob_radius = 0.5
 
 
-def pack_kernel(op_ref, source_ref, shift_ref, op_out_ref, source_out_ref, lines):
+def pack_kernel(
+    op_hbm, source_ref, shift_hbm, op_out_ref, source_out_ref, op_ref, shift_ref, lines, arrived
+):
+    copies = (
+        pltpu.make_async_copy(shift_hbm, shift_ref, arrived.at[0]),
+        pltpu.make_async_copy(op_hbm, op_ref, arrived.at[1]),
+    )
+    for copy in copies:
+        copy.start()
+    rows = source_ref[...].astype(F32)
+    low = rows[:, 0:128].astype(BF16)
+    high = jnp.concatenate([rows[0:72, 128:LON], rows[72:144, 128:LON]], axis=1)
+    high = jnp.concatenate([high, jnp.zeros((8, 128), F32)], axis=0).astype(BF16)
+    for p in range(SIDES):
+        source_out_ref[p, 0:144, :] = low
+        source_out_ref[p, HIGH_AT:SOURCE_LINES, :] = high
+    copies[0].wait()
+    same = lax.broadcasted_iota(jnp.int32, (TGT, TGT), 0) == lax.broadcasted_iota(
+        jnp.int32, (TGT, TGT), 1
+    )
+    columns = []
+    for i in range(2):
+        shift = jnp.broadcast_to(shift_ref[i : i + 1, :].astype(F32), (TGT, TGT))
+        column = jnp.sum(jnp.where(same, shift, 0.0), axis=1, keepdims=True)
+        columns.append(jnp.broadcast_to(column, (TGT, 64)))
+    for p in range(SIDES):
+        source_out_ref[p, 144:HIGH_AT, :] = jnp.concatenate(columns, axis=1).astype(BF16)
+    copies[1].wait()
     for r in range(ROWS_HERE):
         row = op_ref[r].astype(F32)
         high = row[:, 128:LON]
         at = r * TILES
         lines[at : at + LAT_HERE, :] = row[:, 0:128]
         lines[at + LAT_HERE : at + TILES, :] = jnp.concatenate([high[0:6], high[6:12]], axis=1)
+    lines[LINES:SENT_LINES, :] = jnp.zeros((SENT_LINES - LINES, 128), F32)
     op_out_ref[0] = lines[...].astype(BF16)
-    rows = source_ref[...].astype(F32)
-    low = rows[:, 0:128].astype(BF16)
-    high = jnp.concatenate([rows[0:72, 128:LON], rows[72:144, 128:LON]], axis=1)
-    high = jnp.concatenate([high, jnp.zeros((8, 128), F32)], axis=0).astype(BF16)
-    same = lax.broadcasted_iota(jnp.int32, (TGT, TGT), 0) == lax.broadcasted_iota(
-        jnp.int32, (TGT, TGT), 1
-    )
-    columns = []
-    for i in range(2):
-        shift = jnp.broadcast_to(shift_ref[i : i + 1, :].astype(F32), (TGT, TGT))
-        column = jnp.sum(jnp.where(same, shift, 0.0), axis=1, keepdims=True)
-        columns.append(jnp.broadcast_to(column, (TGT, 64)))
-    columns = jnp.concatenate(columns, axis=1).astype(BF16)
-    for p in range(QUAD):
-        source_out_ref[p, 0:144, :] = low
-        source_out_ref[p, 144:HIGH_AT, :] = columns
-        source_out_ref[p, HIGH_AT:SOURCE_LINES, :] = high
 
 
 def roll_kernel(src_ref, rolled_ref, tiles):
-    for p in range(QUAD):
+    for p in range(SIDES):
         high = src_ref[p, HIGH_AT:SOURCE_LINES, :].astype(F32)[0:72, :]
         for i in range(2):
             here = pl.ds(p * 144 + i * 72, 72)
@@ -108,34 +119,47 @@
     lax.fori_loop(0, CAPS, per_capsule, 0)
 
 
-def rotate_kernel(rolled_ref, op_ref, out_ref, lines, held, acc):
+def contract(rolled_ref, op_ref, lines, held, acc):
     for z in range(Z):
-        lines[z * LINES : (z + 1) * LINES, :] = op_ref[z].astype(F32)
+        lines[z * LINES : (z + 1) * LINES, :] = op_ref[z].astype(F32)[0:LINES, :]
     for n in range(TILES):
-        rows = lines[pl.ds(n, NODES, stride=TILES), :]
-        held[:, n * 128 : (n + 1) * 128] = rows.astype(BF16)
+        held[:, n * 128 : (n + 1) * 128] = lines[pl.ds(n, NODES, stride=TILES), :].astype(BF16)
     acc[...] = lax.dot_general(
         rolled_ref[...], held[...], (((1,), (1,)), ((), ())), preferred_element_type=F32
     )
 
+
+def by_target(acc, out_ref, at):
     upper = lax.broadcasted_iota(jnp.int32, (8, NODES), 0) < 4
+    blank = jnp.zeros((8, 32), F32)
     for c in range(CAPS):
+        first = (c // 2) * BAND + (c % 2) * 4
         for half in range(2):
             tails = [[], []]
             for pair in range(3):
-                at = c * 96 + pair * 32 + half * 8
-                one = acc[at : at + 8, :]
-                two = acc[at + 16 : at + 24, :]
+                row = c * 96 + pair * 32 + half * 8
+                one = acc[row : row + 8, :]
+                two = acc[row + 16 : row + 24, :]
                 lo = jnp.where(upper, one, pltpu.roll(two, 4, 0))
                 hi = jnp.where(upper, pltpu.roll(one, 4, 0), two)
                 for j, tile in enumerate((lo, hi)):
-                    dest = (c // 2) * BAND + (c % 2) * 4 + half * 2 + j
-                    out_ref[dest, pair * 8 : pair * 8 + 8, :] = tile[:, 0:128]
+                    out_ref[first + half * 2 + j, pl.ds(at + pair * 8, 8), :] = tile[:, 0:128]
                     tails[j].append(tile[:, 128:NODES])
             for j in range(2):
-                dest = (c // 2) * BAND + (c % 2) * 4 + half * 2 + j
-                blank = jnp.zeros((8, 32), F32)
-                out_ref[dest, 24:32, :] = jnp.concatenate([*tails[j], blank], axis=1)
+                tail = jnp.concatenate([*tails[j], blank], axis=1)
+                out_ref[first + half * 2 + j, pl.ds(at + 24, 8), :] = tail
+
+
+def rotate_mine_kernel(rolled_ref, op_ref, out_ref, lines, held, acc):
+    contract(rolled_ref, op_ref, lines, held, acc)
+    by_target(acc, out_ref, 0)
+
+
+def rotate_next_kernel(rolled_ref, op_ref, mine_ref, core_ref, out_ref, lines, held, acc):
+    core = core_ref[0]
+    out_ref[:, pl.ds(pl.multiple_of(core * 32, 32), 32), :] = mine_ref[...]
+    contract(rolled_ref, op_ref, lines, held, acc)
+    by_target(acc, out_ref, pl.multiple_of((1 - core) * 32, 32))
 
 
 def stokes_kernel(parts_ref, weight_ref, out_ref):
@@ -143,10 +167,11 @@
     total = jnp.zeros((3, 4, 1), F32)
     pole = None
     sums = [jnp.zeros((4, 1), F32) for _ in range(3)]
-    for g in range(QUAD):
-        whole = parts_ref[g, 0]
+    for g in range(2 * SIDES):
+        here = slice(32 * (g % 2), 32 * (g % 2) + 32)
+        whole = parts_ref[g // 2, 0, here, :]
         for b in range(1, BAND):
-            whole = whole + parts_ref[g, b]
+            whole = whole + parts_ref[g // 2, b, here, :]
         main = [whole[4 * k : 4 * k + 4, :] for k in range(6)]
         tail = whole[24:32, :]
         rest = [
@@ -178,53 +203,76 @@
 
 def per_device(positions, densities, operator, target_shift, weights):
     vmem = pl.BlockSpec(memory_space=pltpu.VMEM)
+    smem = pl.BlockSpec(memory_space=pltpu.SMEM)
+    hbm = pl.BlockSpec(memory_space=pl.ANY)
     source = jnp.concatenate([positions, densities], axis=1).reshape(144, LON)
     lines, source = pl.pallas_call(
         pack_kernel,
         out_shape=(
-            jax.ShapeDtypeStruct((1, LINES, 128), BF16),
-            jax.ShapeDtypeStruct((QUAD, SOURCE_LINES, 128), BF16),
+            jax.ShapeDtypeStruct((1, SENT_LINES, 128), BF16),
+            jax.ShapeDtypeStruct((SIDES, SOURCE_LINES, 128), BF16),
         ),
-        in_specs=[vmem] * 3,
+        in_specs=[hbm, vmem, hbm],
         out_specs=(vmem, vmem),
-        scratch_shapes=[pltpu.VMEM((LINES, 128), F32)],
-        compiler_params=pltpu.CompilerParams(vmem_limit_bytes=16 * 2**20),
+        scratch_shapes=[
+            pltpu.VMEM((ROWS_HERE, LAT_HERE, LON), BF16),
+            pltpu.VMEM((2, TGT), jnp.int32),
+            pltpu.VMEM((SENT_LINES, 128), F32),
+            pltpu.SemaphoreType.DMA((2,)),
+        ],
+        compiler_params=pltpu.CompilerParams(vmem_limit_bytes=60 * 2**20),
         name="pack",
     )(operator, source, target_shift)
-    source = lax.all_to_all(source, GROUP, 0, 0, tiled=True)
-    lines = lax.all_gather(lines, "z", axis=0, tiled=True)
+    source = lax.all_to_all(source, "y_hi", 0, 0, tiled=True)
+    mine = lax.all_gather(lines, "z", axis=0, tiled=True)
+    mine, source = lax.optimization_barrier((mine, source))
+    other = lax.ppermute(mine, "core", [(0, 1), (1, 0)])
     rolled = pl.pallas_call(
         roll_kernel,
         out_shape=jax.ShapeDtypeStruct((CAPS * 6 * TGT, COLS), BF16),
         in_specs=[vmem],
         out_specs=vmem,
-        scratch_shapes=[pltpu.VMEM((3, QUAD * 144, 128), F32)],
-        compiler_params=pltpu.CompilerParams(vmem_limit_bytes=24 * 2**20),
+        scratch_shapes=[pltpu.VMEM((3, SIDES * 144, 128), F32)],
+        compiler_params=pltpu.CompilerParams(vmem_limit_bytes=16 * 2**20),
+        cost_estimate=pl.CostEstimate(flops=10**9, bytes_accessed=2**22, transcendentals=0),
         name="roll",
     )(source)
+    scratch = [
+        pltpu.VMEM((Z * LINES, 128), F32),
+        pltpu.VMEM((NODES, COLS), BF16),
+        pltpu.VMEM((CAPS * 6 * TGT, NODES), F32),
+    ]
+    core = lax.axis_index("core").astype(jnp.int32)[None]
     parts = pl.pallas_call(
-        rotate_kernel,
-        out_shape=jax.ShapeDtypeStruct((QUAD * BAND, 32, 128), F32),
+        rotate_mine_kernel,
+        out_shape=jax.ShapeDtypeStruct((SIDES * BAND, 32, 128), F32),
         in_specs=[vmem] * 2,
         out_specs=vmem,
-        scratch_shapes=[
-            pltpu.VMEM((Z * LINES, 128), F32),
-            pltpu.VMEM((NODES, COLS), BF16),
-            pltpu.VMEM((CAPS * 6 * TGT, NODES), F32),
-        ],
-        compiler_params=pltpu.CompilerParams(vmem_limit_bytes=24 * 2**20),
-        name="rotate",
-    )(rolled, lines)
-    parts = lax.all_to_all(parts, GROUP + STRIP, 0, 0, tiled=True)
-    weights = weights.reshape(Z, QUAD, ROWS_HERE).transpose(1, 0, 2).reshape(QUAD, NODES)
+        scratch_shapes=scratch,
+        compiler_params=pltpu.CompilerParams(vmem_limit_bytes=16 * 2**20),
+        cost_estimate=pl.CostEstimate(flops=10**9, bytes_accessed=2**22, transcendentals=0),
+        name="rotate_mine",
+    )(rolled, mine)
+    parts = pl.pallas_call(
+        rotate_next_kernel,
+        out_shape=jax.ShapeDtypeStruct((SIDES * BAND, 64, 128), F32),
+        in_specs=[vmem] * 3 + [smem],
+        out_specs=vmem,
+        scratch_shapes=scratch,
+        compiler_params=pltpu.CompilerParams(vmem_limit_bytes=16 * 2**20),
+        name="rotate_next",
+    )(rolled, other, parts, core)
+    parts = lax.all_to_all(parts, ("y_hi",) + STRIP, 0, 0, tiled=True)
+    weights = weights.reshape(Z, 2 * SIDES, ROWS_HERE).transpose(1, 0, 2)
+    weights = weights.reshape(2 * SIDES, NODES)
     found = pl.pallas_call(
         stokes_kernel,
         out_shape=jax.ShapeDtypeStruct((BAND, 8, 128), F32),
         in_specs=[vmem] * 2,
         out_specs=vmem,
-        compiler_params=pltpu.CompilerParams(vmem_limit_bytes=32 * 2**20),
+        compiler_params=pltpu.CompilerParams(vmem_limit_bytes=16 * 2**20),
         name="stokes",
-    )(parts.reshape(QUAD, BAND, 32, 128), weights)
+    )(parts.reshape(SIDES, BAND, 64, 128), weights)
     found = lax.all_to_all(found, STRIP, 0, 0, tiled=True)
     return found[:, 0:4, 0:3].reshape(2, TGT, 3).transpose(0, 2, 1)
 

time: 82.3 us -> 83.9 us (1.019)
  blocking collectives: 36.8 us -> 40.6 us
  starting transfers between devices: 24 us -> 21.9 us
  local copies, waits for them, and re-layouts: 2.53 us -> 1.59 us
    all_to_all x2, starting transfers between devices: 24 us -> 12 us  [the longest x1 6.99 us: per_device(): parts = lax.all_to_all(parts, ('y_hi',) + STRIP, 0, 0, tiled=True)]
    ppermute x0 -> x1, starting transfers between devices: none -> 9.93 us  [per_device(): other = lax.ppermute(mine, 'core', [(0, 1), (1, 0)])]
    all_gather x1, blocking collectives: 28.9 us -> 33.1 us  [per_device(): mine = lax.all_gather(lines, 'z', axis=0, tiled=True)]
    pallas_call x2 -> x3, Pallas kernels: 2.98 us -> 5.12 us  [the longest x1 2.52 us: per_device(): pl.pallas_call(pack_kernel, out_shape=(jax.ShapeDtypeStruct((1, SENT_LINE...]
    pallas_call x1, Pallas kernels: 3.74 us -> 1.91 us  [per_device(): pl.pallas_call(roll_kernel, out_shape=jax.ShapeDtypeStruct((CAPS * 6 * TG...]
    unnamed x6 -> x2, local copies, waits for them, and re-layouts: 1.57 us -> 0.01 us
  transfers between devices with their start and end apart: 2 -> 3, of which waited for: 1 -> 1; matrix products, arithmetic and copies ran while one was open for 0% -> 0% of each run, Pallas kernels for 0% -> 3%
where the time goes in v9:
time: 83.9 us; the launch traced here: 83.2 us
  blocking collectives  40.6 us (48%)
  starting transfers between devices  21.9 us (26%)
  waiting for transfers between devices  10.9 us (13%)
  Pallas kernels  7.28 us (9%)
  local copies, waits for them, and re-layouts  1.59 us (2%)
  other arithmetic  0.9 us (1%)
    all_gather x1, blocking collectives, per_device(): mine = lax.all_gather(lines, 'z', axis=0, tiled=True)  33.1 us
    all_to_all x1, waiting for transfers between devices, per_device(): parts = lax.all_to_all(parts, ('y_hi',) + STRIP, 0, 0, tiled=True)  10.9 us
    ppermute x1, starting transfers between devices, per_device(): other = lax.ppermute(mine, 'core', [(0, 1), (1, 0)])  9.93 us
    all_to_all x1, blocking collectives, per_device(): found = lax.all_to_all(found, STRIP, 0, 0, tiled=True)  7.44 us
    all_to_all x1, starting transfers between devices, per_device(): parts = lax.all_to_all(parts, ('y_hi',) + STRIP, 0, 0, tiled=True)  6.99 us
    all_to_all x1, starting transfers between devices, per_device(): source = lax.all_to_all(source, 'y_hi', 0, 0, tiled=True)  5.02 us
    pallas_call x1, Pallas kernels, per_device(): pl.pallas_call(pack_kernel, out_shape=(jax.ShapeDtypeStruct((1, SENT_LINE...  2.52 us
    pallas_call x1, Pallas kernels, per_device(): pl.pallas_call(roll_kernel, out_shape=jax.ShapeDtypeStruct((CAPS * 6 * TG...  1.91 us
  transfers between devices with their start and end apart: 3, of which 1 were waited for; matrix products, arithmetic and copies ran while one was open for 0% of the time, Pallas kernels for 3%

profile of v9, /device:TPU:1, one launch (start us, length us, event | category | flops | bytes accessed | tf_op | source)
XLA Modules:
  0.0 83.2 jit_solution(6565200253277220637)
XLA Ops:
  0.0 0.9 %pad_maximum_fusion = bf16[2,6,12,192]{3,0,2,1:T(2,128)(2,1)S(1)} fusion(bf16[2,3,12,192]{3,0,2,1:T(2,128)(2,1)} %param.6, bf16[2,3,12,192]{3,0,2,1:T(2,128)(2,1)} %param.5), kind=kLoop, calls=%fused_computation | loop fusion | flops 27648 | bytes 110592 | tf_op jit(solution)/shard_map/concatenate | solution.py:208
  0.9 0.7 reshape.15.source_ref
  1.6 2.5 %pack.1 = (bf16[1,184,128]{2,1,0:T(8,128)(2,1)}, bf16[2,240,128]{2,1,0:T(8,128)(2,1)}) custom-call(bf16[10,12,192]{2,1,0:T(8,128)(2,1)} %op_hbm.1, bf16[144,192]{1,0:T(8,128)(2,1)} %reshape.15.source_ref, s32[2,16]{1,0:T(2,128)} %shift_hbm.1), custom_call_target="tpu_custom_call" | custom-call | tf_op jit(solution)/shard_map/pack/pallas_call | solution.py:209
  4.1 5.0 %all-to-all-start = ((bf16[2,240,128]{2,1,0:T(8,128)(2,1)}), bf16[2,240,128]{2,1,0:T(8,128)(2,1)S(1)}, u32[]{:S(2)}, u32[]{:S(2)}) async-start(bf16[2,240,128]{2,1,0:T(8,128)(2,1)} %get-tuple-element.10), calls=%async_computation | async-start | bytes 245760 | tf_op jit(solution)/shard_map/all_to_all | solution.py:226
  9.1 33.1 %all_gather.3.op_ref = bf16[16,184,128]{2,1,0:T(8,128)(2,1)S(1)} all-gather(bf16[1,184,128]{2,1,0:T(8,128)(2,1)} %get-tuple-element.9), channel_id=1, replica_groups=mesh['z'=16,'y_hi'=2,'core'=2,'x'=4,'y_lo'=2] {'z'}, dimensions={0}, use_global_device_ids=true | all-gather | bytes 800768 | tf_op jit(solution)/shard_map/all_gather | solution.py:227
  42.3 0.0 all-to-all-done.src_ref
  42.3 9.9 %collective-permute-start = (bf16[16,184,128]{2,1,0:T(8,128)(2,1)S(1)}, bf16[16,184,128]{2,1,0:T(8,128)(2,1)S(1)}, u32[]{:S(2)}, u32[]{:S(2)}) collective-permute-start(bf16[16,184,128]{2,1,0:T(8,128)(2,1)S(1)} %all_gather.3.op_ref), channel_id=1, source_target_pairs={{0,8},{8,0},{1,9},{9,1},{2,10},{10,2},{3,11},{11,3},{4,12},{12,4},... | collective-permute-start | bytes 2261000 | tf_op jit(solution)/shard_map/ppermute | solution.py:229
  52.2 1.9 %roll.1.rolled_ref = bf16[384,2304]{1,0:T(8,128)(2,1)S(1)} custom-call(bf16[2,240,128]{2,1,0:T(8,128)(2,1)S(1)} %all-to-all-done.src_ref), custom_call_target="tpu_custom_call" | custom-call | flops 1000000000 | bytes 4194304 | tf_op jit(solution)/shard_map/roll/pallas_call | solution.py:230
  54.1 0.9 %rotate_mine.1.mine_ref = f32[16,32,128]{2,1,0:T(8,128)S(1)} custom-call(bf16[384,2304]{1,0:T(8,128)(2,1)S(1)} %roll.1.rolled_ref, bf16[16,184,128]{2,1,0:T(8,128)(2,1)S(1)} %all_gather.3.op_ref), custom_call_target="tpu_custom_call" | custom-call | flops 1000000000 | bytes 4194304 | tf_op jit(solution)/shard_map/rotate_mine/pallas_call | solution.py:246
  55.0 0.0 collective-permute-done.op_ref
  55.0 0.0 copy-start
  55.0 1.7 %rotate_next.1 = f32[16,64,128]{2,1,0:T(8,128)} custom-call(bf16[384,2304]{1,0:T(8,128)(2,1)S(1)} %roll.1.rolled_ref, bf16[16,184,128]{2,1,0:T(8,128)(2,1)S(1)} %collective-permute-done.op_ref, f32[16,32,128]{2,1,0:T(8,128)S(1)} %rotate_mine.1.mine_ref, s32[1]{0:T(128)} %bitcast.core_ref), custom_call_target="tpu_custom_call" | custom-call | tf_op jit(solution)/shard_map/rotate_next/pallas_call | solution.py:256
  56.7 7.0 %all-to-all-start.1 = ((f32[16,64,128]{2,1,0:T(8,128)}), f32[16,64,128]{2,1,0:T(8,128)S(1)}, u32[]{:S(2)}, u32[]{:S(2)}) async-start(f32[16,64,128]{2,1,0:T(8,128)} %rotate_next.1), calls=%async_computation.1 | async-start | bytes 1048576 | tf_op jit(solution)/shard_map/all_to_all | solution.py:265
  63.7 0.0 copy-done
  63.7 0.1 reshape.17
  63.9 0.1 reshape.18.weight_ref
  64.0 10.9 %all-to-all-done.1 = f32[16,64,128]{2,1,0:T(8,128)S(1)} async-done(((f32[16,64,128]{2,1,0:T(8,128)}), f32[16,64,128]{2,1,0:T(8,128)S(1)}, u32[]{:S(2)}, u32[]{:S(2)}) %all-to-all-start.1) | async-done | bytes 524320 | tf_op jit(solution)/shard_map/all_to_all | solution.py:265
  74.9 0.3 stokes.1
  75.1 7.4 %all_to_all.15 = f32[8,8,128]{2,1,0:T(8,128)S(1)} all-to-all(f32[8,8,128]{2,1,0:T(8,128)S(1)} %stokes.1), channel_id=1, replica_groups=mesh['z'=16,'y_hi'=2,'core'=2,'x'=4,'y_lo'=2] {'x','y_lo'}, dimensions={0} | all-to-all | bytes 65536 | tf_op jit(solution)/shard_map/all_to_all | solution.py:276
  82.6 0.7 copy.14
  (3 shorter events, 0.0 us)
Async XLA Ops:
  4.1 38.2 %all-to-all-start = ((bf16[2,240,128]{2,1,0:T(8,128)(2,1)}), bf16[2,240,128]{2,1,0:T(8,128)(2,1)S(1)}, u32[]{:S(2)}, u32[]{:S(2)}) async-start(bf16[2,240,128]{2,1,0:T(8,128)(2,1)} %get-tuple-element.10), calls=%async_computation | async-start | bytes 245760 | tf_op jit(solution)/shard_map/all_to_all | solution.py:226
  42.3 12.8 %collective-permute-start = (bf16[16,184,128]{2,1,0:T(8,128)(2,1)S(1)}, bf16[16,184,128]{2,1,0:T(8,128)(2,1)S(1)}, u32[]{:S(2)}, u32[]{:S(2)}) collective-permute-start(bf16[16,184,128]{2,1,0:T(8,128)(2,1)S(1)} %all_gather.3.op_ref), channel_id=1, source_target_pairs={{0,8},{8,0},{1,9},{9,1},{2,10},{10,2},{3,11},{11,3},{4,12},{12,4},... | collective-permute-start | bytes 2261000 | tf_op jit(solution)/shard_map/ppermute | solution.py:229
  55.0 8.7 %copy-start = (f32[640]{0:T(1024)S(1)}, f32[640]{0:T(1024)}, u32[]{:S(2)}) copy-start(f32[640]{0:T(1024)} %param.9) | copy-start | bytes 7684
  56.7 18.1 %all-to-all-start.1 = ((f32[16,64,128]{2,1,0:T(8,128)}), f32[16,64,128]{2,1,0:T(8,128)S(1)}, u32[]{:S(2)}, u32[]{:S(2)}) async-start(f32[16,64,128]{2,1,0:T(8,128)} %rotate_next.1), calls=%async_computation.1 | async-start | bytes 1048576 | tf_op jit(solution)/shard_map/all_to_all | solution.py:265

commit v10 on v6

--- a/solution.py
+++ b/solution.py
@@ -24,16 +24,18 @@
 LEFT = 128 - NODES
 HIGH_AT = 160
 SOURCE_LINES = 240
-HALF_ROWS = CAPS // 2 * 6 * TGT
+STEPS = 4
+STEP_CAPS = CAPS // STEPS
+STEP_ROWS = STEP_CAPS * 6 * TGT
 
 CELL = ("z_half", "z_low", "y_hi", "core")
-GROUP = ("z_low", "y_hi", "core")
+GROUP = ("y_hi", "core")
 STRIP = ("x", "y_lo")
 
 blob_radius = 0.5
 
 
-def pack_kernel(op_ref, out_ref, lines):
+def pack_kernel(op_ref, op_out_ref, lines):
     for r in range(ROWS_HERE):
         row = op_ref[r].astype(F32)
         high = row[:, 128:LON]
@@ -42,15 +44,14 @@
         lines[at + LAT_HERE : at + TILES, :] = jnp.concatenate([high[0:6], high[6:12]], axis=1)
     packed = lines[...].astype(BF16)
     for z in range(Z):
-        out_ref[z] = packed
-
-
-def pack_source_kernel(source_ref, shift_ref, out_ref):
+        op_out_ref[z] = packed
+
+
+def pack_source_kernel(source_ref, shift_ref, source_out_ref):
     rows = source_ref[...].astype(F32)
-    out_ref[0:144, :] = rows[:, 0:128].astype(BF16)
+    low = rows[:, 0:128].astype(BF16)
     high = jnp.concatenate([rows[0:72, 128:LON], rows[72:144, 128:LON]], axis=1)
-    high = jnp.concatenate([high, jnp.zeros((8, 128), F32)], axis=0)
-    out_ref[HIGH_AT:SOURCE_LINES, :] = high.astype(BF16)
+    high = jnp.concatenate([high, jnp.zeros((8, 128), F32)], axis=0).astype(BF16)
     same = lax.broadcasted_iota(jnp.int32, (TGT, TGT), 0) == lax.broadcasted_iota(
         jnp.int32, (TGT, TGT), 1
     )
@@ -59,16 +60,18 @@
         shift = jnp.broadcast_to(shift_ref[i : i + 1, :].astype(F32), (TGT, TGT))
         column = jnp.sum(jnp.where(same, shift, 0.0), axis=1, keepdims=True)
         columns.append(jnp.broadcast_to(column, (TGT, 64)))
-    out_ref[144:HIGH_AT, :] = jnp.concatenate(columns, axis=1).astype(BF16)
-
-
-def roll_half(src_ref, half, rolled_ref, tiles):
-    base_p = half * (GROUPS // 2)
-    for p in range(GROUPS // 2):
-        high = src_ref[base_p + p, HIGH_AT:SOURCE_LINES, :].astype(F32)[0:72, :]
+    columns = jnp.concatenate(columns, axis=1).astype(BF16)
+    source_out_ref[0:144, :] = low
+    source_out_ref[144:HIGH_AT, :] = columns
+    source_out_ref[HIGH_AT:SOURCE_LINES, :] = high
+
+
+def roll_kernel(src_ref, rolled_ref, tiles):
+    for p in range(2):
+        high = src_ref[p, 0, HIGH_AT:SOURCE_LINES, :].astype(F32)[0:72, :]
         for i in range(2):
             here = pl.ds(p * 144 + i * 72, 72)
-            low = src_ref[base_p + p, 0:144, :].astype(F32)[72 * i : 72 * i + 72, :]
+            low = src_ref[p, 0, 0:144, :].astype(F32)[72 * i : 72 * i + 72, :]
             rest = high[:, 64 * i : 64 * i + 64]
             tiles[0, here, :] = low
             tiles[1, here, :] = jnp.concatenate([rest, low[:, 0:64]], axis=1)
@@ -77,7 +80,7 @@
     lane = lax.broadcasted_iota(jnp.int32, (TGT, 128), 1)
 
     def per_capsule(c, carry):
-        column = src_ref[base_p + c // 2, 144:HIGH_AT, :].astype(F32)
+        column = src_ref[c // 2, 0, 144:HIGH_AT, :].astype(F32)
         column = jnp.where(c % 2 == 0, column[:, 0:1], column[:, 64:65])
         shift = jnp.broadcast_to(column.astype(jnp.int32), (TGT, 128))
         take = jnp.bitwise_and(lane + shift, 127)
@@ -110,26 +113,23 @@
                 rolled_ref[to, (m + 12) * 128 : (m + 12) * 128 + 128] = rolled(high)
         return carry
 
-    lax.fori_loop(0, CAPS // 2, per_capsule, 0)
-
-
-def roll_kernel(src_ref, rolled_ref, tiles):
-    roll_half(src_ref, 0, rolled_ref, tiles)
-
-
-def rotate_kernel(src_ref, rolled_ref, op_ref, out_ref, tiles, rolled, lines, held, acc):
-    roll_half(src_ref, 1, rolled, tiles)
-    for z in range(Z):
-        lines[z * LINES : (z + 1) * LINES, :] = op_ref[z].astype(F32)
-    for n in range(TILES):
-        held[:, n * 128 : (n + 1) * 128] = lines[pl.ds(n, NODES, stride=TILES), :].astype(BF16)
-    for i, half_ref in enumerate((rolled_ref, rolled)):
-        acc[i * HALF_ROWS : (i + 1) * HALF_ROWS, :] = lax.dot_general(
-            half_ref[...], held[...], (((1,), (1,)), ((), ())), preferred_element_type=F32
-        )
+    lax.fori_loop(0, STEP_CAPS, per_capsule, 0)
+
+
+def rotate_kernel(rolled_ref, op_ref, out_ref, lines, held, acc):
+    @pl.when(pl.program_id(0) == 0)
+    def _():
+        for z in range(Z):
+            lines[z * LINES : (z + 1) * LINES, :] = op_ref[z].astype(F32)
+        for n in range(TILES):
+            held[:, n * 128 : (n + 1) * 128] = lines[pl.ds(n, NODES, stride=TILES), :].astype(BF16)
+
+    acc[...] = lax.dot_general(
+        rolled_ref[...], held[...], (((1,), (1,)), ((), ())), preferred_element_type=F32
+    )
     upper = lax.broadcasted_iota(jnp.int32, (8, NODES), 0) < 4
     blank = jnp.zeros((8, 2 * 128 - 3 * NODES), F32)
-    for c in range(CAPS):
+    for c in range(STEP_CAPS):
         for half in range(2):
             found = [[], []]
             for pair in range(3):
@@ -183,19 +183,6 @@
 
 def per_device(positions, densities, operator, target_shift, weights):
     vmem = pl.BlockSpec(memory_space=pltpu.VMEM)
-    lines = pl.pallas_call(
-        pack_kernel,
-        out_shape=jax.ShapeDtypeStruct((Z, LINES, 128), BF16),
-        in_specs=[vmem],
-        out_specs=vmem,
-        scratch_shapes=[pltpu.VMEM((LINES, 128), F32)],
-        compiler_params=pltpu.CompilerParams(vmem_limit_bytes=16 * 2**20),
-        name="pack",
-    )(operator)
-    lines, positions, densities, target_shift = lax.optimization_barrier(
-        (lines, positions, densities, target_shift)
-    )
-    lines = lax.all_to_all(lines, "z_half", 0, 0, tiled=True)
     source = jnp.concatenate([positions, densities], axis=1).reshape(144, LON)
     source = pl.pallas_call(
         pack_source_kernel,
@@ -205,33 +192,52 @@
         compiler_params=pltpu.CompilerParams(vmem_limit_bytes=16 * 2**20),
         name="pack_source",
     )(source, target_shift)
+    operator, source = lax.optimization_barrier((operator, source))
+    other = lax.ppermute(source, "z_low", [(0, 1), (1, 0)])
+    lines = pl.pallas_call(
+        pack_kernel,
+        out_shape=jax.ShapeDtypeStruct((Z, LINES, 128), BF16),
+        in_specs=[vmem],
+        out_specs=vmem,
+        scratch_shapes=[pltpu.VMEM((LINES, 128), F32)],
+        compiler_params=pltpu.CompilerParams(vmem_limit_bytes=16 * 2**20),
+        cost_estimate=pl.CostEstimate(flops=2 * 10**10, bytes_accessed=2**25, transcendentals=0),
+        name="pack",
+    )(operator)
+    lines, other = lax.optimization_barrier((lines, other))
+    lines = lax.all_to_all(lines, "z_half", 0, 0, tiled=True)
+    even = lax.axis_index("z_low") == 0
+    source = jnp.stack([jnp.where(even, source, other), jnp.where(even, other, source)])
     source = lax.all_gather(source[None], GROUP, axis=0, tiled=True)
     rolled = pl.pallas_call(
         roll_kernel,
-        out_shape=jax.ShapeDtypeStruct((HALF_ROWS, COLS), BF16),
-        in_specs=[vmem],
-        out_specs=vmem,
-        scratch_shapes=[pltpu.VMEM((3, GROUPS * 72, 128), F32)],
-        compiler_params=pltpu.CompilerParams(vmem_limit_bytes=16 * 2**20),
+        grid=(STEPS,),
+        out_shape=jax.ShapeDtypeStruct((CAPS * 6 * TGT, COLS), BF16),
+        in_specs=[pl.BlockSpec((2, 1, SOURCE_LINES, 128), lambda n: (n % 2, n // 2, 0, 0))],
+        out_specs=pl.BlockSpec((STEP_ROWS, COLS), lambda n: (n, 0)),
+        scratch_shapes=[pltpu.VMEM((3, 2 * 144, 128), F32)],
+        compiler_params=pltpu.CompilerParams(vmem_limit_bytes=60 * 2**20),
         cost_estimate=pl.CostEstimate(flops=10**9, bytes_accessed=2**22, transcendentals=0),
         name="roll",
     )(source)
     parts = pl.pallas_call(
         rotate_kernel,
+        grid=(STEPS,),
         out_shape=jax.ShapeDtypeStruct((GROUPS * BAND, 16, 128), F32),
-        in_specs=[vmem] * 3,
-        out_specs=vmem,
+        in_specs=[
+            pl.BlockSpec((STEP_ROWS, COLS), lambda n: (n, 0)),
+            pl.BlockSpec((Z, LINES, 128), lambda n: (0, 0, 0)),
+        ],
+        out_specs=pl.BlockSpec((GROUPS * BAND // STEPS, 16, 128), lambda n: (n, 0, 0)),
         scratch_shapes=[
-            pltpu.VMEM((3, GROUPS * 72, 128), F32),
-            pltpu.VMEM((HALF_ROWS, COLS), BF16),
             pltpu.VMEM((Z * LINES, 128), F32),
             pltpu.VMEM((NODES, COLS), BF16),
-            pltpu.VMEM((CAPS * 6 * TGT, NODES), F32),
+            pltpu.VMEM((STEP_ROWS, NODES), F32),
         ],
-        compiler_params=pltpu.CompilerParams(vmem_limit_bytes=16 * 2**20),
+        compiler_params=pltpu.CompilerParams(vmem_limit_bytes=54 * 2**20),
         name="rotate",
-    )(source, rolled, lines)
-    parts = lax.all_to_all(parts, GROUP + STRIP, 0, 0, tiled=True)
+    )(rolled, lines)
+    parts = lax.all_to_all(parts, ("z_low",) + GROUP + STRIP, 0, 0, tiled=True)
     weights = weights.reshape(Z, GROUPS, ROWS_HERE).transpose(1, 0, 2).reshape(GROUPS, NODES)
     found = pl.pallas_call(
         stokes_kernel,

time: 87.7 us -> 84.7 us (0.966); the launches traced: 86.2 us -> 84.2 us
  blocking collectives: 34.4 us -> 18.5 us
  starting transfers between devices: 21.5 us -> 31.9 us
  Pallas kernels: 12 us -> 17.3 us
  local copies, waits for them, and re-layouts: 5.09 us -> 3.22 us
    all_gather x1, blocking collectives: 26.9 us -> 11.1 us  [per_device(): source = lax.all_gather(source[None], GROUP, axis=0, tiled=True)]
    all_to_all x1, starting transfers between devices: 5.9 us -> 13 us  [per_device(): parts = lax.all_to_all(parts, ('z_low',) + GROUP + STRIP, 0, 0, tiled=True)]
    pallas_call x2, Pallas kernels: 10.7 us -> 16 us  [the longest x1 9.9 us: per_device(): pl.pallas_call(roll_kernel, grid=(STEPS,), out_shape=jax.ShapeDtypeStruct...]
    ppermute x0 -> x1, starting transfers between devices: none -> 4.38 us  [per_device(): other = lax.ppermute(source, 'z_low', [(0, 1), (1, 0)])]
    unnamed x12 -> x8, local copies, waits for them, and re-layouts: 4.16 us -> 2.3 us
    all_to_all x1, starting transfers between devices: 15.6 us -> 14.5 us  [per_device(): lines = lax.all_to_all(lines, 'z_half', 0, 0, tiled=True)]
  transfers between devices with their start and end apart: 2 -> 3, of which waited for: 1 -> 1; matrix products, arithmetic and copies ran while one was open for 1% -> 0% of each run, Pallas kernels for 4% -> 13%
where the time goes in v10:
time: 84.7 us; the launch traced here: 84.2 us
  starting transfers between devices  31.9 us (38%)
  blocking collectives  18.5 us (22%)
  Pallas kernels  17.3 us (20%)
  waiting for transfers between devices  12.3 us (15%)
  local copies, waits for them, and re-layouts  3.22 us (4%)
  other arithmetic  0.92 us (1%)
    all_to_all x1, starting transfers between devices, per_device(): lines = lax.all_to_all(lines, 'z_half', 0, 0, tiled=True)  14.5 us
    all_to_all x1, starting transfers between devices, per_device(): parts = lax.all_to_all(parts, ('z_low',) + GROUP + STRIP, 0, 0, tiled=True)  13 us
    all_to_all x1, waiting for transfers between devices, per_device(): parts = lax.all_to_all(parts, ('z_low',) + GROUP + STRIP, 0, 0, tiled=True)  12.2 us
    all_gather x1, blocking collectives, per_device(): source = lax.all_gather(source[None], GROUP, axis=0, tiled=True)  11.1 us
    pallas_call x1, Pallas kernels, per_device(): pl.pallas_call(roll_kernel, grid=(STEPS,), out_shape=jax.ShapeDtypeStruct...  9.9 us
    all_to_all x1, blocking collectives, per_device(): found = lax.all_to_all(found, STRIP, 0, 0, tiled=True)  7.44 us
    pallas_call x1, Pallas kernels, per_device(): pl.pallas_call(rotate_kernel, grid=(STEPS,), out_shape=jax.ShapeDtypeStru...  6.1 us
    ppermute x1, starting transfers between devices, per_device(): other = lax.ppermute(source, 'z_low', [(0, 1), (1, 0)])  4.38 us
  transfers between devices with their start and end apart: 3, of which 1 were waited for; matrix products, arithmetic and copies ran while one was open for 0% of the time, Pallas kernels for 13%

profile of v10, /device:TPU:1, one launch (start us, length us, event | category | flops | bytes accessed | tf_op | source)
XLA Modules:
  0.0 84.2 jit_solution(1193010326063992467)
XLA Ops:
  0.0 0.9 %pad_maximum_fusion.1 = bf16[2,6,12,192]{3,0,2,1:T(2,128)(2,1)S(1)} fusion(bf16[2,3,12,192]{3,0,2,1:T(2,128)(2,1)} %param.6, bf16[2,3,12,192]{3,0,2,1:T(2,128)(2,1)} %param.5), kind=kLoop, calls=%fused_computation.1 | loop fusion | flops 27648 | bytes 110592 | tf_op jit(solution)/shard_map/concatenate | solution.py:186
  1.0 0.0 copy-start
  1.0 0.7 copy-done
  1.6 0.1 pack_source.1
  1.7 4.4 %collective-permute-start = (bf16[240,128]{1,0:T(8,128)(2,1)S(1)}, bf16[240,128]{1,0:T(8,128)(2,1)S(1)}, u32[]{:S(2)}, u32[]{:S(2)}) collective-permute-start(bf16[240,128]{1,0:T(8,128)(2,1)S(1)} %pack_source.1), channel_id=1, source_target_pairs={{0,32},{32,0},{1,33},{33,1},{2,34},{34,2},{3,35},{35,3},{4,36},{36... | collective-permute-start | bytes 184328 | tf_op jit(solution)/shard_map/ppermute | solution.py:196
  6.1 0.0 copy-start.1
  6.1 0.9 %copy-done.1 = bf16[10,12,192]{2,1,0:T(8,128)(2,1)S(1)} copy-done((bf16[10,12,192]{2,1,0:T(8,128)(2,1)S(1)}, bf16[10,12,192]{2,1,0:T(8,128)(2,1)}, u32[]{:S(2)}) %copy-start.1) | copy-done | bytes 46104
  7.0 0.9 %pack.1 = bf16[8,180,128]{2,1,0:T(8,128)(2,1)} custom-call(bf16[10,12,192]{2,1,0:T(8,128)(2,1)S(1)} %copy-done.1), custom_call_target="tpu_custom_call" | custom-call | flops 20000000000 | bytes 33554432 | tf_op jit(solution)/shard_map/pack/pallas_call | solution.py:197
  7.9 0.0 collective-permute-done
  7.9 14.5 %all-to-all-start = ((bf16[8,180,128]{2,1,0:T(8,128)(2,1)}), bf16[8,180,128]{2,1,0:T(8,128)(2,1)S(1)}, u32[]{:S(2)}, u32[]{:S(2)}) async-start(bf16[8,180,128]{2,1,0:T(8,128)(2,1)} %pack.1), calls=%async_computation | async-start | bytes 753664 | tf_op jit(solution)/shard_map/all_to_all | solution.py:208
  22.4 11.1 %all-gather = bf16[8,240,128]{2,1,0:T(8,128)(2,1)} all-gather(bf16[2,240,128]{2,1,0:T(8,128)(2,1)S(1)} %pad_maximum_fusion), channel_id=2, replica_groups=mesh['z_half'=8,'z_low'=2,'y_hi'=2,'core'=2,'x'=4,'y_lo'=2] {'y_hi','core'}, dimensions={0}, use_global_device_ids=true | all-gather | bytes 614400 | tf_op jit(solution)/shard_map/all_gather | solution.py:211
  33.5 0.0 copy-start.3
  33.5 9.9 %roll.1.rolled_ref = bf16[1536,2304]{1,0:T(8,128)(2,1)} custom-call(bf16[4,2,240,128]{3,2,1,0:T(8,128)(2,1)} %bitcast.10), custom_call_target="tpu_custom_call" | custom-call | flops 1000000000 | bytes 4194304 | tf_op jit(solution)/shard_map/roll/pallas_call | solution.py:212
  43.4 0.0 all-to-all-done.op_ref
  43.4 0.7 copy-done.2
  44.1 6.1 %rotate.1 = f32[64,16,128]{2,1,0:T(8,128)} custom-call(bf16[1536,2304]{1,0:T(8,128)(2,1)} %roll.1.rolled_ref, bf16[8,180,128]{2,1,0:T(8,128)(2,1)} %copy-done.2), custom_call_target="tpu_custom_call" | custom-call | tf_op jit(solution)/shard_map/rotate/pallas_call | solution.py:223
  50.2 13.0 %all-to-all-start.1 = ((f32[64,16,128]{2,1,0:T(8,128)}), f32[64,16,128]{2,1,0:T(8,128)S(1)}, u32[]{:S(2)}, u32[]{:S(2)}) async-start(f32[64,16,128]{2,1,0:T(8,128)} %rotate.1), calls=%async_computation.1 | async-start | bytes 1048576 | tf_op jit(solution)/shard_map/all_to_all | solution.py:240
  63.3 0.0 copy-done.3
  63.3 0.1 reshape.17
  63.4 0.1 reshape.18.weight_ref
  63.5 12.2 %all-to-all-done.1 = f32[64,16,128]{2,1,0:T(8,128)S(1)} async-done(((f32[64,16,128]{2,1,0:T(8,128)}), f32[64,16,128]{2,1,0:T(8,128)S(1)}, u32[]{:S(2)}, u32[]{:S(2)}) %all-to-all-start.1) | async-done | bytes 524320 | tf_op jit(solution)/shard_map/all_to_all | solution.py:240
  75.7 0.3 stokes.1
  76.1 7.4 %all_to_all.15 = f32[8,8,128]{2,1,0:T(8,128)S(1)} all-to-all(f32[8,8,128]{2,1,0:T(8,128)S(1)} %stokes.1), channel_id=1, replica_groups=mesh['z_half'=8,'z_low'=2,'y_hi'=2,'core'=2,'x'=4,'y_lo'=2] {'x','y_lo'}, dimensions={0} | all-to-all | bytes 65536 | tf_op jit(solution)/shard_map/all_to_all | solution.py:250
  83.5 0.7 copy.14
  (7 shorter events, 0.1 us)
Async XLA Ops:
  1.0 0.7 copy-start
  1.7 6.1 %collective-permute-start = (bf16[240,128]{1,0:T(8,128)(2,1)S(1)}, bf16[240,128]{1,0:T(8,128)(2,1)S(1)}, u32[]{:S(2)}, u32[]{:S(2)}) collective-permute-start(bf16[240,128]{1,0:T(8,128)(2,1)S(1)} %pack_source.1), channel_id=1, source_target_pairs={{0,32},{32,0},{1,33},{33,1},{2,34},{34,2},{3,35},{35,3},{4,36},{36... | collective-permute-start | bytes 184328 | tf_op jit(solution)/shard_map/ppermute | solution.py:196
  6.1 0.9 %copy-start.1 = (bf16[10,12,192]{2,1,0:T(8,128)(2,1)S(1)}, bf16[10,12,192]{2,1,0:T(8,128)(2,1)}, u32[]{:S(2)}) copy-start(bf16[10,12,192]{2,1,0:T(8,128)(2,1)} %op_ref) | copy-start | bytes 138244
  7.9 35.5 %all-to-all-start = ((bf16[8,180,128]{2,1,0:T(8,128)(2,1)}), bf16[8,180,128]{2,1,0:T(8,128)(2,1)S(1)}, u32[]{:S(2)}, u32[]{:S(2)}) async-start(bf16[8,180,128]{2,1,0:T(8,128)(2,1)} %pack.1), calls=%async_computation | async-start | bytes 753664 | tf_op jit(solution)/shard_map/all_to_all | solution.py:208
  33.5 29.8 %copy-start.3 = (f32[640]{0:T(1024)S(1)}, f32[640]{0:T(1024)}, u32[]{:S(2)}) copy-start(f32[640]{0:T(1024)} %param.9) | copy-start | bytes 7684
  43.4 0.7 copy-start.2
  50.2 25.5 %all-to-all-start.1 = ((f32[64,16,128]{2,1,0:T(8,128)}), f32[64,16,128]{2,1,0:T(8,128)S(1)}, u32[]{:S(2)}, u32[]{:S(2)}) async-start(f32[64,16,128]{2,1,0:T(8,128)} %rotate.1), calls=%async_computation.1 | async-start | bytes 1048576 | tf_op jit(solution)/shard_map/all_to_all | solution.py:240

commit v11 on v9

--- a/solution.py
+++ b/solution.py
@@ -31,34 +31,7 @@
 blob_radius = 0.5
 
 
-def pack_kernel(
-    op_hbm, source_ref, shift_hbm, op_out_ref, source_out_ref, op_ref, shift_ref, lines, arrived
-):
-    copies = (
-        pltpu.make_async_copy(shift_hbm, shift_ref, arrived.at[0]),
-        pltpu.make_async_copy(op_hbm, op_ref, arrived.at[1]),
-    )
-    for copy in copies:
-        copy.start()
-    rows = source_ref[...].astype(F32)
-    low = rows[:, 0:128].astype(BF16)
-    high = jnp.concatenate([rows[0:72, 128:LON], rows[72:144, 128:LON]], axis=1)
-    high = jnp.concatenate([high, jnp.zeros((8, 128), F32)], axis=0).astype(BF16)
-    for p in range(SIDES):
-        source_out_ref[p, 0:144, :] = low
-        source_out_ref[p, HIGH_AT:SOURCE_LINES, :] = high
-    copies[0].wait()
-    same = lax.broadcasted_iota(jnp.int32, (TGT, TGT), 0) == lax.broadcasted_iota(
-        jnp.int32, (TGT, TGT), 1
-    )
-    columns = []
-    for i in range(2):
-        shift = jnp.broadcast_to(shift_ref[i : i + 1, :].astype(F32), (TGT, TGT))
-        column = jnp.sum(jnp.where(same, shift, 0.0), axis=1, keepdims=True)
-        columns.append(jnp.broadcast_to(column, (TGT, 64)))
-    for p in range(SIDES):
-        source_out_ref[p, 144:HIGH_AT, :] = jnp.concatenate(columns, axis=1).astype(BF16)
-    copies[1].wait()
+def pack_kernel(op_ref, source_ref, shift_ref, op_out_ref, source_out_ref, lines):
     for r in range(ROWS_HERE):
         row = op_ref[r].astype(F32)
         high = row[:, 128:LON]
@@ -67,14 +40,30 @@
         lines[at + LAT_HERE : at + TILES, :] = jnp.concatenate([high[0:6], high[6:12]], axis=1)
     lines[LINES:SENT_LINES, :] = jnp.zeros((SENT_LINES - LINES, 128), F32)
     op_out_ref[0] = lines[...].astype(BF16)
-
-
-def roll_kernel(src_ref, rolled_ref, tiles):
-    for p in range(SIDES):
-        high = src_ref[p, HIGH_AT:SOURCE_LINES, :].astype(F32)[0:72, :]
+    rows = source_ref[...].astype(F32)
+    low = rows[:, 0:128].astype(BF16)
+    high = jnp.concatenate([rows[0:72, 128:LON], rows[72:144, 128:LON]], axis=1)
+    high = jnp.concatenate([high, jnp.zeros((8, 128), F32)], axis=0).astype(BF16)
+    same = lax.broadcasted_iota(jnp.int32, (TGT, TGT), 0) == lax.broadcasted_iota(
+        jnp.int32, (TGT, TGT), 1
+    )
+    columns = []
+    for i in range(2):
+        shift = jnp.broadcast_to(shift_ref[i : i + 1, :].astype(F32), (TGT, TGT))
+        column = jnp.sum(jnp.where(same, shift, 0.0), axis=1, keepdims=True)
+        columns.append(jnp.broadcast_to(column, (TGT, 64)))
+    columns = jnp.concatenate(columns, axis=1).astype(BF16)
+    source_out_ref[0:144, :] = low
+    source_out_ref[144:HIGH_AT, :] = columns
+    source_out_ref[HIGH_AT:SOURCE_LINES, :] = high
+
+
+def roll_kernel(mine_ref, next_ref, rolled_ref, tiles):
+    for p, src_ref in enumerate((mine_ref, next_ref)):
+        high = src_ref[HIGH_AT:SOURCE_LINES, :].astype(F32)[0:72, :]
         for i in range(2):
             here = pl.ds(p * 144 + i * 72, 72)
-            low = src_ref[p, 0:144, :].astype(F32)[72 * i : 72 * i + 72, :]
+            low = src_ref[0:144, :].astype(F32)[72 * i : 72 * i + 72, :]
             rest = high[:, 64 * i : 64 * i + 64]
             tiles[0, here, :] = low
             tiles[1, here, :] = jnp.concatenate([rest, low[:, 0:64]], axis=1)
@@ -83,7 +72,7 @@
     lane = lax.broadcasted_iota(jnp.int32, (TGT, 128), 1)
 
     def per_capsule(c, carry):
-        column = src_ref[c // 2, 144:HIGH_AT, :].astype(F32)
+        column = jnp.where(c // 2 == 0, mine_ref[144:HIGH_AT, :], next_ref[144:HIGH_AT, :]).astype(F32)
         column = jnp.where(c % 2 == 0, column[:, 0:1], column[:, 64:65])
         shift = jnp.broadcast_to(column.astype(jnp.int32), (TGT, 128))
         take = jnp.bitwise_and(lane + shift, 127)
@@ -129,11 +118,11 @@
     )
 
 
-def by_target(acc, out_ref, at):
+def by_target(acc, side, out_ref, at):
     upper = lax.broadcasted_iota(jnp.int32, (8, NODES), 0) < 4
     blank = jnp.zeros((8, 32), F32)
     for c in range(CAPS):
-        first = (c // 2) * BAND + (c % 2) * 4
+        first = jnp.bitwise_xor(side, c // 2) * BAND + (c % 2) * 4
         for half in range(2):
             tails = [[], []]
             for pair in range(3):
@@ -150,16 +139,16 @@
                 out_ref[first + half * 2 + j, pl.ds(at + 24, 8), :] = tail
 
 
-def rotate_mine_kernel(rolled_ref, op_ref, out_ref, lines, held, acc):
+def rotate_mine_kernel(rolled_ref, op_ref, place_ref, out_ref, lines, held, acc):
     contract(rolled_ref, op_ref, lines, held, acc)
-    by_target(acc, out_ref, 0)
-
-
-def rotate_next_kernel(rolled_ref, op_ref, mine_ref, core_ref, out_ref, lines, held, acc):
-    core = core_ref[0]
+    by_target(acc, place_ref[0], out_ref, 0)
+
+
+def rotate_next_kernel(rolled_ref, op_ref, mine_ref, place_ref, out_ref, lines, held, acc):
+    core = place_ref[1]
     out_ref[:, pl.ds(pl.multiple_of(core * 32, 32), 32), :] = mine_ref[...]
     contract(rolled_ref, op_ref, lines, held, acc)
-    by_target(acc, out_ref, pl.multiple_of((1 - core) * 32, 32))
+    by_target(acc, place_ref[0], out_ref, pl.multiple_of((1 - core) * 32, 32))
 
 
 def stokes_kernel(parts_ref, weight_ref, out_ref):
@@ -204,55 +193,49 @@
 def per_device(positions, densities, operator, target_shift, weights):
     vmem = pl.BlockSpec(memory_space=pltpu.VMEM)
     smem = pl.BlockSpec(memory_space=pltpu.SMEM)
-    hbm = pl.BlockSpec(memory_space=pl.ANY)
     source = jnp.concatenate([positions, densities], axis=1).reshape(144, LON)
     lines, source = pl.pallas_call(
         pack_kernel,
         out_shape=(
             jax.ShapeDtypeStruct((1, SENT_LINES, 128), BF16),
-            jax.ShapeDtypeStruct((SIDES, SOURCE_LINES, 128), BF16),
+            jax.ShapeDtypeStruct((SOURCE_LINES, 128), BF16),
         ),
-        in_specs=[hbm, vmem, hbm],
+        in_specs=[vmem] * 3,
         out_specs=(vmem, vmem),
-        scratch_shapes=[
-            pltpu.VMEM((ROWS_HERE, LAT_HERE, LON), BF16),
-            pltpu.VMEM((2, TGT), jnp.int32),
-            pltpu.VMEM((SENT_LINES, 128), F32),
-            pltpu.SemaphoreType.DMA((2,)),
-        ],
-        compiler_params=pltpu.CompilerParams(vmem_limit_bytes=60 * 2**20),
+        scratch_shapes=[pltpu.VMEM((SENT_LINES, 128), F32)],
+        compiler_params=pltpu.CompilerParams(vmem_limit_bytes=16 * 2**20),
         name="pack",
     )(operator, source, target_shift)
-    source = lax.all_to_all(source, "y_hi", 0, 0, tiled=True)
+    other_source = lax.ppermute(source, "y_hi", [(0, 1), (1, 0)])
     mine = lax.all_gather(lines, "z", axis=0, tiled=True)
-    mine, source = lax.optimization_barrier((mine, source))
+    mine, other_source = lax.optimization_barrier((mine, other_source))
     other = lax.ppermute(mine, "core", [(0, 1), (1, 0)])
     rolled = pl.pallas_call(
         roll_kernel,
         out_shape=jax.ShapeDtypeStruct((CAPS * 6 * TGT, COLS), BF16),
-        in_specs=[vmem],
+        in_specs=[vmem] * 2,
         out_specs=vmem,
         scratch_shapes=[pltpu.VMEM((3, SIDES * 144, 128), F32)],
         compiler_params=pltpu.CompilerParams(vmem_limit_bytes=16 * 2**20),
         cost_estimate=pl.CostEstimate(flops=10**9, bytes_accessed=2**22, transcendentals=0),
         name="roll",
-    )(source)
+    )(source, other_source)
     scratch = [
         pltpu.VMEM((Z * LINES, 128), F32),
         pltpu.VMEM((NODES, COLS), BF16),
         pltpu.VMEM((CAPS * 6 * TGT, NODES), F32),
     ]
-    core = lax.axis_index("core").astype(jnp.int32)[None]
+    place = jnp.stack([lax.axis_index("y_hi"), lax.axis_index("core")]).astype(jnp.int32)
     parts = pl.pallas_call(
         rotate_mine_kernel,
         out_shape=jax.ShapeDtypeStruct((SIDES * BAND, 32, 128), F32),
-        in_specs=[vmem] * 2,
+        in_specs=[vmem] * 2 + [smem],
         out_specs=vmem,
         scratch_shapes=scratch,
         compiler_params=pltpu.CompilerParams(vmem_limit_bytes=16 * 2**20),
         cost_estimate=pl.CostEstimate(flops=10**9, bytes_accessed=2**22, transcendentals=0),
         name="rotate_mine",
-    )(rolled, mine)
+    )(rolled, mine, place)
     parts = pl.pallas_call(
         rotate_next_kernel,
         out_shape=jax.ShapeDtypeStruct((SIDES * BAND, 64, 128), F32),
@@ -261,7 +244,7 @@
         scratch_shapes=scratch,
         compiler_params=pltpu.CompilerParams(vmem_limit_bytes=16 * 2**20),
         name="rotate_next",
-    )(rolled, other, parts, core)
+    )(rolled, other, parts, place)
     parts = lax.all_to_all(parts, ("y_hi",) + STRIP, 0, 0, tiled=True)
     weights = weights.reshape(Z, 2 * SIDES, ROWS_HERE).transpose(1, 0, 2)
     weights = weights.reshape(2 * SIDES, NODES)

time: 83.9 us -> 81.7 us (0.974)
  starting transfers between devices: 21.9 us -> 20.2 us
  Pallas kernels: 7.28 us -> 5.97 us
  local copies, waits for them, and re-layouts: 1.59 us -> 2.53 us
    ppermute x0 -> x1, starting transfers between devices: none -> 5.65 us  [per_device(): other_source = lax.ppermute(source, 'y_hi', [(0, 1), (1, 0)])]
    all_to_all x1 -> x0, starting transfers between devices: 5.02 us -> none  [per_device(): source = lax.all_to_all(source, 'y_hi', 0, 0, tiled=True)]
    pallas_call x1, Pallas kernels: 2.52 us -> 0.11 us  [per_device(): pl.pallas_call(pack_kernel, out_shape=(jax.ShapeDtypeStruct((1, SENT_LINE...]
    all_to_all x1, starting transfers between devices: 6.99 us -> 4.69 us  [per_device(): parts = lax.all_to_all(parts, ('y_hi',) + STRIP, 0, 0, tiled=True)]
    unnamed x2 -> x6, local copies, waits for them, and re-layouts: 0.01 us -> 1.57 us
  transfers between devices with their start and end apart: 3 -> 3, of which waited for: 1 -> 1; matrix products, arithmetic and copies ran while one was open for 0% -> 0% of each run, Pallas kernels for 3% -> 4%
where the time goes in v11:
time: 81.7 us; the launch traced here: 81.1 us
  blocking collectives  40.4 us (49%)
  starting transfers between devices  20.2 us (25%)
  waiting for transfers between devices  10.9 us (13%)
  Pallas kernels  5.97 us (7%)
  local copies, waits for them, and re-layouts  2.53 us (3%)
  other arithmetic  0.97 us (1%)
    all_gather x1, blocking collectives, per_device(): mine = lax.all_gather(lines, 'z', axis=0, tiled=True)  33 us
    all_to_all x1, waiting for transfers between devices, per_device(): parts = lax.all_to_all(parts, ('y_hi',) + STRIP, 0, 0, tiled=True)  10.9 us
    ppermute x1, starting transfers between devices, per_device(): other = lax.ppermute(mine, 'core', [(0, 1), (1, 0)])  9.9 us
    all_to_all x1, blocking collectives, per_device(): found = lax.all_to_all(found, STRIP, 0, 0, tiled=True)  7.44 us
    ppermute x1, starting transfers between devices, per_device(): other_source = lax.ppermute(source, 'y_hi', [(0, 1), (1, 0)])  5.65 us
    all_to_all x1, starting transfers between devices, per_device(): parts = lax.all_to_all(parts, ('y_hi',) + STRIP, 0, 0, tiled=True)  4.69 us
    pallas_call x1, Pallas kernels, per_device(): pl.pallas_call(rotate_next_kernel, out_shape=jax.ShapeDtypeStruct((SIDES...  2.24 us
    pallas_call x1, Pallas kernels, per_device(): pl.pallas_call(roll_kernel, out_shape=jax.ShapeDtypeStruct((CAPS * 6 * TG...  1.91 us
  transfers between devices with their start and end apart: 3, of which 1 were waited for; matrix products, arithmetic and copies ran while one was open for 0% of the time, Pallas kernels for 4%

profile of v11, /device:TPU:1, one launch (start us, length us, event | category | flops | bytes accessed | tf_op | source)
XLA Modules:
  0.0 81.1 jit_solution(6171976445024903396)
XLA Ops:
  0.0 0.9 %pad_maximum_fusion = bf16[2,6,12,192]{3,0,2,1:T(2,128)(2,1)S(1)} fusion(bf16[2,3,12,192]{3,0,2,1:T(2,128)(2,1)} %param.6, bf16[2,3,12,192]{3,0,2,1:T(2,128)(2,1)} %param.5), kind=kLoop, calls=%fused_computation | loop fusion | flops 27648 | bytes 110592 | tf_op jit(solution)/shard_map/concatenate | solution.py:196
  1.0 0.0 copy-start
  1.0 0.9 %copy-done = bf16[10,12,192]{2,1,0:T(8,128)(2,1)S(1)} copy-done((bf16[10,12,192]{2,1,0:T(8,128)(2,1)S(1)}, bf16[10,12,192]{2,1,0:T(8,128)(2,1)}, u32[]{:S(2)}) %copy-start) | copy-done | bytes 46104
  1.9 0.0 copy-start.1
  1.9 0.7 copy-done.1
  2.5 0.1 pack.1
  2.6 5.7 %collective-permute-start = (bf16[240,128]{1,0:T(8,128)(2,1)S(1)}, bf16[240,128]{1,0:T(8,128)(2,1)S(1)}, u32[]{:S(2)}, u32[]{:S(2)}) collective-permute-start(bf16[240,128]{1,0:T(8,128)(2,1)S(1)} %get-tuple-element.9.mine_ref), channel_id=1, source_target_pairs={{0,16},{16,0},{1,17},{17,1},{2,18},{18,2},{3,19},{19,3},{4,20},{20... | collective-permute-start | bytes 184328 | tf_op jit(solution)/shard_map/ppermute | solution.py:209
  8.3 33.0 %all_gather.3.op_ref = bf16[16,184,128]{2,1,0:T(8,128)(2,1)S(1)} all-gather(bf16[1,184,128]{2,1,0:T(8,128)(2,1)S(1)} %get-tuple-element.10), channel_id=1, replica_groups=mesh['z'=16,'y_hi'=2,'core'=2,'x'=4,'y_lo'=2] {'z'}, dimensions={0}, use_global_device_ids=true | all-gather | bytes 800768 | tf_op jit(solution)/shard_map/all_gather | solution.py:210
  41.3 0.0 collective-permute-done.next_ref
  41.3 9.9 %collective-permute-start.1 = (bf16[16,184,128]{2,1,0:T(8,128)(2,1)S(1)}, bf16[16,184,128]{2,1,0:T(8,128)(2,1)S(1)}, u32[]{:S(2)}, u32[]{:S(2)}) collective-permute-start(bf16[16,184,128]{2,1,0:T(8,128)(2,1)S(1)} %all_gather.3.op_ref), channel_id=1, source_target_pairs={{0,8},{8,0},{1,9},{9,1},{2,10},{10,2},{3,11},{11,3},{4,12},{12,4},... | collective-permute-start | bytes 2261000 | tf_op jit(solution)/shard_map/ppermute | solution.py:212
  51.2 0.1 pad_add_fusion.place_ref
  51.3 1.9 %roll.1.rolled_ref = bf16[384,2304]{1,0:T(8,128)(2,1)S(1)} custom-call(bf16[240,128]{1,0:T(8,128)(2,1)S(1)} %get-tuple-element.9.mine_ref, bf16[240,128]{1,0:T(8,128)(2,1)S(1)} %collective-permute-done.next_ref), custom_call_target="tpu_custom_call" | custom-call | flops 1000000000 | bytes 4194304 | tf_op jit(solution)/shard_map/roll/pallas_call | solution.py:213
  53.2 1.4 %rotate_mine.1.mine_ref = f32[16,32,128]{2,1,0:T(8,128)S(1)} custom-call(bf16[384,2304]{1,0:T(8,128)(2,1)S(1)} %roll.1.rolled_ref, bf16[16,184,128]{2,1,0:T(8,128)(2,1)S(1)} %all_gather.3.op_ref, s32[2]{0:T(128)S(1)} %pad_add_fusion.place_ref), custom_call_target="tpu_custom_call" | custom-call | flops 1000000000 | bytes 4194304 | tf_op jit(solution)/shard_map/rotate_mine/pallas_call | solution.py:229
  54.7 0.0 copy-start.2
  54.7 0.0 collective-permute-done.1.op_ref
  54.7 2.2 %rotate_next.1 = f32[16,64,128]{2,1,0:T(8,128)} custom-call(bf16[384,2304]{1,0:T(8,128)(2,1)S(1)} %roll.1.rolled_ref, bf16[16,184,128]{2,1,0:T(8,128)(2,1)S(1)} %collective-permute-done.1.op_ref, f32[16,32,128]{2,1,0:T(8,128)S(1)} %rotate_mine.1.mine_ref, s32[2]{0:T(128)S(1)} %pad_add_fusion.place_ref), custom_call_target="tpu_custom_call" | custom-call | tf_op jit(solution)/shard_map/rotate_next/pallas_call | solution.py:239
  56.9 4.7 %all-to-all-start = ((f32[16,64,128]{2,1,0:T(8,128)}), f32[16,64,128]{2,1,0:T(8,128)S(1)}, u32[]{:S(2)}, u32[]{:S(2)}) async-start(f32[16,64,128]{2,1,0:T(8,128)} %rotate_next.1), calls=%async_computation | async-start | bytes 1048576 | tf_op jit(solution)/shard_map/all_to_all | solution.py:248
  61.6 0.0 copy-done.2
  61.6 0.1 reshape.17
  61.8 0.1 reshape.18.weight_ref
  61.9 10.9 %all-to-all-done = f32[16,64,128]{2,1,0:T(8,128)S(1)} async-done(((f32[16,64,128]{2,1,0:T(8,128)}), f32[16,64,128]{2,1,0:T(8,128)S(1)}, u32[]{:S(2)}, u32[]{:S(2)}) %all-to-all-start) | async-done | bytes 524320 | tf_op jit(solution)/shard_map/all_to_all | solution.py:248
  72.8 0.3 stokes.1
  73.0 7.4 %all_to_all.10 = f32[8,8,128]{2,1,0:T(8,128)S(1)} all-to-all(f32[8,8,128]{2,1,0:T(8,128)S(1)} %stokes.1), channel_id=1, replica_groups=mesh['z'=16,'y_hi'=2,'core'=2,'x'=4,'y_lo'=2] {'x','y_lo'}, dimensions={0} | all-to-all | bytes 65536 | tf_op jit(solution)/shard_map/all_to_all | solution.py:259
  80.5 0.7 copy.14
  (4 shorter events, 0.1 us)
Async XLA Ops:
  1.0 0.9 %copy-start = (bf16[10,12,192]{2,1,0:T(8,128)(2,1)S(1)}, bf16[10,12,192]{2,1,0:T(8,128)(2,1)}, u32[]{:S(2)}) copy-start(bf16[10,12,192]{2,1,0:T(8,128)(2,1)} %op_ref.1) | copy-start | bytes 138244
  1.9 0.7 copy-start.1
  2.6 38.7 %collective-permute-start = (bf16[240,128]{1,0:T(8,128)(2,1)S(1)}, bf16[240,128]{1,0:T(8,128)(2,1)S(1)}, u32[]{:S(2)}, u32[]{:S(2)}) collective-permute-start(bf16[240,128]{1,0:T(8,128)(2,1)S(1)} %get-tuple-element.9.mine_ref), channel_id=1, source_target_pairs={{0,16},{16,0},{1,17},{17,1},{2,18},{18,2},{3,19},{19,3},{4,20},{20... | collective-permute-start | bytes 184328 | tf_op jit(solution)/shard_map/ppermute | solution.py:209
  41.3 13.4 %collective-permute-start.1 = (bf16[16,184,128]{2,1,0:T(8,128)(2,1)S(1)}, bf16[16,184,128]{2,1,0:T(8,128)(2,1)S(1)}, u32[]{:S(2)}, u32[]{:S(2)}) collective-permute-start(bf16[16,184,128]{2,1,0:T(8,128)(2,1)S(1)} %all_gather.3.op_ref), channel_id=1, source_target_pairs={{0,8},{8,0},{1,9},{9,1},{2,10},{10,2},{3,11},{11,3},{4,12},{12,4},... | collective-permute-start | bytes 2261000 | tf_op jit(solution)/shard_map/ppermute | solution.py:212
  54.7 7.0 %copy-start.2 = (f32[640]{0:T(1024)S(1)}, f32[640]{0:T(1024)}, u32[]{:S(2)}) copy-start(f32[640]{0:T(1024)} %param.9) | copy-start | bytes 7684
  56.9 15.9 %all-to-all-start = ((f32[16,64,128]{2,1,0:T(8,128)}), f32[16,64,128]{2,1,0:T(8,128)S(1)}, u32[]{:S(2)}, u32[]{:S(2)}) async-start(f32[16,64,128]{2,1,0:T(8,128)} %rotate_next.1), calls=%async_computation | async-start | bytes 1048576 | tf_op jit(solution)/shard_map/all_to_all | solution.py:248

commit v12 on v11

--- a/solution.py
+++ b/solution.py
@@ -58,12 +58,12 @@
     source_out_ref[HIGH_AT:SOURCE_LINES, :] = high
 
 
-def roll_kernel(mine_ref, next_ref, rolled_ref, tiles):
-    for p, src_ref in enumerate((mine_ref, next_ref)):
-        high = src_ref[HIGH_AT:SOURCE_LINES, :].astype(F32)[0:72, :]
+def roll_kernel(src_ref, rolled_ref, tiles):
+    for p in range(SIDES):
+        high = src_ref[p, HIGH_AT:SOURCE_LINES, :].astype(F32)[0:72, :]
         for i in range(2):
             here = pl.ds(p * 144 + i * 72, 72)
-            low = src_ref[0:144, :].astype(F32)[72 * i : 72 * i + 72, :]
+            low = src_ref[p, 0:144, :].astype(F32)[72 * i : 72 * i + 72, :]
             rest = high[:, 64 * i : 64 * i + 64]
             tiles[0, here, :] = low
             tiles[1, here, :] = jnp.concatenate([rest, low[:, 0:64]], axis=1)
@@ -72,7 +72,7 @@
     lane = lax.broadcasted_iota(jnp.int32, (TGT, 128), 1)
 
     def per_capsule(c, carry):
-        column = jnp.where(c // 2 == 0, mine_ref[144:HIGH_AT, :], next_ref[144:HIGH_AT, :]).astype(F32)
+        column = src_ref[c // 2, 144:HIGH_AT, :].astype(F32)
         column = jnp.where(c % 2 == 0, column[:, 0:1], column[:, 64:65])
         shift = jnp.broadcast_to(column.astype(jnp.int32), (TGT, 128))
         take = jnp.bitwise_and(lane + shift, 127)
@@ -118,11 +118,11 @@
     )
 
 
-def by_target(acc, side, out_ref, at):
+def by_target(acc, out_ref, at):
     upper = lax.broadcasted_iota(jnp.int32, (8, NODES), 0) < 4
     blank = jnp.zeros((8, 32), F32)
     for c in range(CAPS):
-        first = jnp.bitwise_xor(side, c // 2) * BAND + (c % 2) * 4
+        first = (c // 2) * BAND + (c % 2) * 4
         for half in range(2):
             tails = [[], []]
             for pair in range(3):
@@ -139,16 +139,16 @@
                 out_ref[first + half * 2 + j, pl.ds(at + 24, 8), :] = tail
 
 
-def rotate_mine_kernel(rolled_ref, op_ref, place_ref, out_ref, lines, held, acc):
+def rotate_mine_kernel(rolled_ref, op_ref, out_ref, lines, held, acc):
     contract(rolled_ref, op_ref, lines, held, acc)
-    by_target(acc, place_ref[0], out_ref, 0)
-
-
-def rotate_next_kernel(rolled_ref, op_ref, mine_ref, place_ref, out_ref, lines, held, acc):
-    core = place_ref[1]
+    by_target(acc, out_ref, 0)
+
+
+def rotate_next_kernel(rolled_ref, op_ref, mine_ref, core_ref, out_ref, lines, held, acc):
+    core = core_ref[0]
     out_ref[:, pl.ds(pl.multiple_of(core * 32, 32), 32), :] = mine_ref[...]
     contract(rolled_ref, op_ref, lines, held, acc)
-    by_target(acc, place_ref[0], out_ref, pl.multiple_of((1 - core) * 32, 32))
+    by_target(acc, out_ref, pl.multiple_of((1 - core) * 32, 32))
 
 
 def stokes_kernel(parts_ref, weight_ref, out_ref):
@@ -210,32 +210,36 @@
     mine = lax.all_gather(lines, "z", axis=0, tiled=True)
     mine, other_source = lax.optimization_barrier((mine, other_source))
     other = lax.ppermute(mine, "core", [(0, 1), (1, 0)])
+    first = lax.axis_index("y_hi") == 0
+    source = jnp.stack(
+        [jnp.where(first, source, other_source), jnp.where(first, other_source, source)]
+    )
     rolled = pl.pallas_call(
         roll_kernel,
         out_shape=jax.ShapeDtypeStruct((CAPS * 6 * TGT, COLS), BF16),
-        in_specs=[vmem] * 2,
+        in_specs=[vmem],
         out_specs=vmem,
         scratch_shapes=[pltpu.VMEM((3, SIDES * 144, 128), F32)],
         compiler_params=pltpu.CompilerParams(vmem_limit_bytes=16 * 2**20),
         cost_estimate=pl.CostEstimate(flops=10**9, bytes_accessed=2**22, transcendentals=0),
         name="roll",
-    )(source, other_source)
+    )(source)
     scratch = [
         pltpu.VMEM((Z * LINES, 128), F32),
         pltpu.VMEM((NODES, COLS), BF16),
         pltpu.VMEM((CAPS * 6 * TGT, NODES), F32),
     ]
-    place = jnp.stack([lax.axis_index("y_hi"), lax.axis_index("core")]).astype(jnp.int32)
+    core = lax.axis_index("core").astype(jnp.int32)[None]
     parts = pl.pallas_call(
         rotate_mine_kernel,
         out_shape=jax.ShapeDtypeStruct((SIDES * BAND, 32, 128), F32),
-        in_specs=[vmem] * 2 + [smem],
+        in_specs=[vmem] * 2,
         out_specs=vmem,
         scratch_shapes=scratch,
         compiler_params=pltpu.CompilerParams(vmem_limit_bytes=16 * 2**20),
         cost_estimate=pl.CostEstimate(flops=10**9, bytes_accessed=2**22, transcendentals=0),
         name="rotate_mine",
-    )(rolled, mine, place)
+    )(rolled, mine)
     parts = pl.pallas_call(
         rotate_next_kernel,
         out_shape=jax.ShapeDtypeStruct((SIDES * BAND, 64, 128), F32),
@@ -244,7 +248,7 @@
         scratch_shapes=scratch,
         compiler_params=pltpu.CompilerParams(vmem_limit_bytes=16 * 2**20),
         name="rotate_next",
-    )(rolled, other, parts, place)
+    )(rolled, other, parts, core)
     parts = lax.all_to_all(parts, ("y_hi",) + STRIP, 0, 0, tiled=True)
     weights = weights.reshape(Z, 2 * SIDES, ROWS_HERE).transpose(1, 0, 2)
     weights = weights.reshape(2 * SIDES, NODES)

time: 81.7 us -> 80.6 us (0.987)
  Pallas kernels: 5.97 us -> 4.89 us
where the time goes in v12:
time: 80.6 us; the launch traced here: 80 us
  blocking collectives  40.4 us (50%)
  starting transfers between devices  20.2 us (25%)
  waiting for transfers between devices  10.9 us (14%)
  Pallas kernels  4.89 us (6%)
  local copies, waits for them, and re-layouts  2.53 us (3%)
  other arithmetic  0.93 us (1%)
    all_gather x1, blocking collectives, per_device(): mine = lax.all_gather(lines, 'z', axis=0, tiled=True)  33 us
    all_to_all x1, waiting for transfers between devices, per_device(): parts = lax.all_to_all(parts, ('y_hi',) + STRIP, 0, 0, tiled=True)  10.9 us
    ppermute x1, starting transfers between devices, per_device(): other = lax.ppermute(mine, 'core', [(0, 1), (1, 0)])  9.9 us
    all_to_all x1, blocking collectives, per_device(): found = lax.all_to_all(found, STRIP, 0, 0, tiled=True)  7.44 us
    ppermute x1, starting transfers between devices, per_device(): other_source = lax.ppermute(source, 'y_hi', [(0, 1), (1, 0)])  5.65 us
    all_to_all x1, starting transfers between devices, per_device(): parts = lax.all_to_all(parts, ('y_hi',) + STRIP, 0, 0, tiled=True)  4.69 us
    pallas_call x1, Pallas kernels, per_device(): pl.pallas_call(roll_kernel, out_shape=jax.ShapeDtypeStruct((CAPS * 6 * TG...  1.91 us
    pallas_call x1, Pallas kernels, per_device(): pl.pallas_call(rotate_next_kernel, out_shape=jax.ShapeDtypeStruct((SIDES...  1.72 us
  transfers between devices with their start and end apart: 3, of which 1 were waited for; matrix products, arithmetic and copies ran while one was open for 0% of the time, Pallas kernels for 4%

profile of v12, /device:TPU:1, one launch (start us, length us, event | category | flops | bytes accessed | tf_op | source)
XLA Modules:
  0.0 80.0 jit_solution(11330303926041205487)
XLA Ops:
  0.0 0.9 %pad_maximum_fusion.1 = bf16[2,6,12,192]{3,0,2,1:T(2,128)(2,1)S(1)} fusion(bf16[2,3,12,192]{3,0,2,1:T(2,128)(2,1)} %param.6, bf16[2,3,12,192]{3,0,2,1:T(2,128)(2,1)} %param.5), kind=kLoop, calls=%fused_computation.1 | loop fusion | flops 27648 | bytes 110592 | tf_op jit(solution)/shard_map/concatenate | solution.py:196
  1.0 0.0 copy-start
  1.0 0.9 %copy-done = bf16[10,12,192]{2,1,0:T(8,128)(2,1)S(1)} copy-done((bf16[10,12,192]{2,1,0:T(8,128)(2,1)S(1)}, bf16[10,12,192]{2,1,0:T(8,128)(2,1)}, u32[]{:S(2)}) %copy-start) | copy-done | bytes 46104
  1.9 0.0 copy-start.1
  1.9 0.7 copy-done.1
  2.5 0.1 pack.1
  2.6 5.7 %collective-permute-start = (bf16[240,128]{1,0:T(8,128)(2,1)S(1)}, bf16[240,128]{1,0:T(8,128)(2,1)S(1)}, u32[]{:S(2)}, u32[]{:S(2)}) collective-permute-start(bf16[240,128]{1,0:T(8,128)(2,1)S(1)} %get-tuple-element.9), channel_id=1, source_target_pairs={{0,16},{16,0},{1,17},{17,1},{2,18},{18,2},{3,19},{19,3},{4,20},{20... | collective-permute-start | bytes 184328 | tf_op jit(solution)/shard_map/ppermute | solution.py:209
  8.3 33.0 %all_gather.3.op_ref = bf16[16,184,128]{2,1,0:T(8,128)(2,1)S(1)} all-gather(bf16[1,184,128]{2,1,0:T(8,128)(2,1)S(1)} %get-tuple-element.10), channel_id=1, replica_groups=mesh['z'=16,'y_hi'=2,'core'=2,'x'=4,'y_lo'=2] {'z'}, dimensions={0}, use_global_device_ids=true | all-gather | bytes 800768 | tf_op jit(solution)/shard_map/all_gather | solution.py:210
  41.3 0.0 collective-permute-done
  41.3 9.9 %collective-permute-start.1 = (bf16[16,184,128]{2,1,0:T(8,128)(2,1)S(1)}, bf16[16,184,128]{2,1,0:T(8,128)(2,1)S(1)}, u32[]{:S(2)}, u32[]{:S(2)}) collective-permute-start(bf16[16,184,128]{2,1,0:T(8,128)(2,1)S(1)} %all_gather.3.op_ref), channel_id=1, source_target_pairs={{0,8},{8,0},{1,9},{9,1},{2,10},{10,2},{3,11},{11,3},{4,12},{12,4},... | collective-permute-start | bytes 2261000 | tf_op jit(solution)/shard_map/ppermute | solution.py:212
  51.3 1.9 %roll.1.rolled_ref = bf16[384,2304]{1,0:T(8,128)(2,1)S(1)} custom-call(bf16[2,240,128]{2,1,0:T(8,128)(2,1)S(1)} %pad_maximum_fusion.src_ref), custom_call_target="tpu_custom_call" | custom-call | flops 1000000000 | bytes 4194304 | tf_op jit(solution)/shard_map/roll/pallas_call | solution.py:217
  53.2 0.9 %rotate_mine.1.mine_ref = f32[16,32,128]{2,1,0:T(8,128)S(1)} custom-call(bf16[384,2304]{1,0:T(8,128)(2,1)S(1)} %roll.1.rolled_ref, bf16[16,184,128]{2,1,0:T(8,128)(2,1)S(1)} %all_gather.3.op_ref), custom_call_target="tpu_custom_call" | custom-call | flops 1000000000 | bytes 4194304 | tf_op jit(solution)/shard_map/rotate_mine/pallas_call | solution.py:233
  54.1 0.0 collective-permute-done.1.op_ref
  54.1 0.0 copy-start.2
  54.1 1.7 %rotate_next.1 = f32[16,64,128]{2,1,0:T(8,128)} custom-call(bf16[384,2304]{1,0:T(8,128)(2,1)S(1)} %roll.1.rolled_ref, bf16[16,184,128]{2,1,0:T(8,128)(2,1)S(1)} %collective-permute-done.1.op_ref, f32[16,32,128]{2,1,0:T(8,128)S(1)} %rotate_mine.1.mine_ref, s32[1]{0:T(128)} %bitcast.2.core_ref), custom_call_target="tpu_custom_call" | custom-call | tf_op jit(solution)/shard_map/rotate_next/pallas_call | solution.py:243
  55.8 4.7 %all-to-all-start = ((f32[16,64,128]{2,1,0:T(8,128)}), f32[16,64,128]{2,1,0:T(8,128)S(1)}, u32[]{:S(2)}, u32[]{:S(2)}) async-start(f32[16,64,128]{2,1,0:T(8,128)} %rotate_next.1), calls=%async_computation | async-start | bytes 1048576 | tf_op jit(solution)/shard_map/all_to_all | solution.py:252
  60.5 0.0 copy-done.2
  60.5 0.1 reshape.17
  60.7 0.1 reshape.18.weight_ref
  60.8 10.9 %all-to-all-done = f32[16,64,128]{2,1,0:T(8,128)S(1)} async-done(((f32[16,64,128]{2,1,0:T(8,128)}), f32[16,64,128]{2,1,0:T(8,128)S(1)}, u32[]{:S(2)}, u32[]{:S(2)}) %all-to-all-start) | async-done | bytes 524320 | tf_op jit(solution)/shard_map/all_to_all | solution.py:252
  71.7 0.3 stokes.1
  71.9 7.4 %all_to_all.10 = f32[8,8,128]{2,1,0:T(8,128)S(1)} all-to-all(f32[8,8,128]{2,1,0:T(8,128)S(1)} %stokes.1), channel_id=1, replica_groups=mesh['z'=16,'y_hi'=2,'core'=2,'x'=4,'y_lo'=2] {'x','y_lo'}, dimensions={0} | all-to-all | bytes 65536 | tf_op jit(solution)/shard_map/all_to_all | solution.py:263
  79.4 0.7 copy.14
  (6 shorter events, 0.1 us)
Async XLA Ops:
  1.0 0.9 %copy-start = (bf16[10,12,192]{2,1,0:T(8,128)(2,1)S(1)}, bf16[10,12,192]{2,1,0:T(8,128)(2,1)}, u32[]{:S(2)}) copy-start(bf16[10,12,192]{2,1,0:T(8,128)(2,1)} %op_ref.1) | copy-start | bytes 138244
  1.9 0.7 copy-start.1
  2.6 38.7 %collective-permute-start = (bf16[240,128]{1,0:T(8,128)(2,1)S(1)}, bf16[240,128]{1,0:T(8,128)(2,1)S(1)}, u32[]{:S(2)}, u32[]{:S(2)}) collective-permute-start(bf16[240,128]{1,0:T(8,128)(2,1)S(1)} %get-tuple-element.9), channel_id=1, source_target_pairs={{0,16},{16,0},{1,17},{17,1},{2,18},{18,2},{3,19},{19,3},{4,20},{20... | collective-permute-start | bytes 184328 | tf_op jit(solution)/shard_map/ppermute | solution.py:209
  41.3 12.8 %collective-permute-start.1 = (bf16[16,184,128]{2,1,0:T(8,128)(2,1)S(1)}, bf16[16,184,128]{2,1,0:T(8,128)(2,1)S(1)}, u32[]{:S(2)}, u32[]{:S(2)}) collective-permute-start(bf16[16,184,128]{2,1,0:T(8,128)(2,1)S(1)} %all_gather.3.op_ref), channel_id=1, source_target_pairs={{0,8},{8,0},{1,9},{9,1},{2,10},{10,2},{3,11},{11,3},{4,12},{12,4},... | collective-permute-start | bytes 2261000 | tf_op jit(solution)/shard_map/ppermute | solution.py:212
  54.1 6.4 %copy-start.2 = (f32[640]{0:T(1024)S(1)}, f32[640]{0:T(1024)}, u32[]{:S(2)}) copy-start(f32[640]{0:T(1024)} %param.9) | copy-start | bytes 7684
  55.8 15.9 %all-to-all-start = ((f32[16,64,128]{2,1,0:T(8,128)}), f32[16,64,128]{2,1,0:T(8,128)S(1)}, u32[]{:S(2)}, u32[]{:S(2)}) async-start(f32[16,64,128]{2,1,0:T(8,128)} %rotate_next.1), calls=%async_computation | async-start | bytes 1048576 | tf_op jit(solution)/shard_map/all_to_all | solution.py:252

commit v13 on v12

--- a/solution.py
+++ b/solution.py
@@ -144,7 +144,10 @@
     by_target(acc, out_ref, 0)
 
 
-def rotate_next_kernel(rolled_ref, op_ref, mine_ref, core_ref, out_ref, lines, held, acc):
+def rotate_next_kernel(
+    rolled_ref, op_ref, mine_ref, weight_ref, core_ref, out_ref, weight_out_ref, lines, held, acc
+):
+    weight_out_ref[...] = weight_ref[...]
     core = core_ref[0]
     out_ref[:, pl.ds(pl.multiple_of(core * 32, 32), 32), :] = mine_ref[...]
     contract(rolled_ref, op_ref, lines, held, acc)
@@ -208,7 +211,9 @@
     )(operator, source, target_shift)
     other_source = lax.ppermute(source, "y_hi", [(0, 1), (1, 0)])
     mine = lax.all_gather(lines, "z", axis=0, tiled=True)
-    mine, other_source = lax.optimization_barrier((mine, other_source))
+    mine, other_source, weights = lax.optimization_barrier((mine, other_source, weights))
+    weights = weights.reshape(Z, 2 * SIDES, ROWS_HERE).transpose(1, 0, 2)
+    weights = weights.reshape(2 * SIDES, NODES)
     other = lax.ppermute(mine, "core", [(0, 1), (1, 0)])
     first = lax.axis_index("y_hi") == 0
     source = jnp.stack(
@@ -240,18 +245,19 @@
         cost_estimate=pl.CostEstimate(flops=10**9, bytes_accessed=2**22, transcendentals=0),
         name="rotate_mine",
     )(rolled, mine)
-    parts = pl.pallas_call(
+    parts, weights = pl.pallas_call(
         rotate_next_kernel,
-        out_shape=jax.ShapeDtypeStruct((SIDES * BAND, 64, 128), F32),
-        in_specs=[vmem] * 3 + [smem],
-        out_specs=vmem,
+        out_shape=(
+            jax.ShapeDtypeStruct((SIDES * BAND, 64, 128), F32),
+            jax.ShapeDtypeStruct((2 * SIDES, NODES), F32),
+        ),
+        in_specs=[vmem] * 4 + [smem],
+        out_specs=(vmem, vmem),
         scratch_shapes=scratch,
         compiler_params=pltpu.CompilerParams(vmem_limit_bytes=16 * 2**20),
         name="rotate_next",
-    )(rolled, other, parts, core)
+    )(rolled, other, parts, weights, core)
     parts = lax.all_to_all(parts, ("y_hi",) + STRIP, 0, 0, tiled=True)
-    weights = weights.reshape(Z, 2 * SIDES, ROWS_HERE).transpose(1, 0, 2)
-    weights = weights.reshape(2 * SIDES, NODES)
     found = pl.pallas_call(
         stokes_kernel,
         out_shape=jax.ShapeDtypeStruct((BAND, 8, 128), F32),

time: 80.6 us -> 80.5 us (level)
  blocking collectives: 40.4 us -> 56.1 us
  waiting for transfers between devices: 10.9 us -> 0.01 us
  starting transfers between devices: 20.2 us -> 15.6 us
    all_to_all x0 -> x1, blocking collectives: none -> 15.7 us  [per_device(): parts = lax.all_to_all(parts, ('y_hi',) + STRIP, 0, 0, tiled=True)]
    all_to_all x1 -> x0, waiting for transfers between devices: 10.9 us -> none  [per_device(): parts = lax.all_to_all(parts, ('y_hi',) + STRIP, 0, 0, tiled=True)]
    all_to_all x1 -> x0, starting transfers between devices: 4.69 us -> none  [per_device(): parts = lax.all_to_all(parts, ('y_hi',) + STRIP, 0, 0, tiled=True)]
  transfers between devices with their start and end apart: 3 -> 2, of which waited for: 1 -> 0; matrix products, arithmetic and copies ran while one was open for 0% -> 1% of each run, Pallas kernels for 4% -> 4%
where the time goes in v13:
time: 80.5 us; the launch traced here: 80 us
  blocking collectives  56.1 us (70%)
  starting transfers between devices  15.6 us (19%)
  Pallas kernels  4.11 us (5%)
  local copies, waits for them, and re-layouts  3.21 us (4%)
  other arithmetic  0.93 us (1%)
    all_gather x1, blocking collectives, per_device(): mine = lax.all_gather(lines, 'z', axis=0, tiled=True)  33 us
    all_to_all x1, blocking collectives, per_device(): parts = lax.all_to_all(parts, ('y_hi',) + STRIP, 0, 0, tiled=True)  15.7 us
    ppermute x1, starting transfers between devices, per_device(): other = lax.ppermute(mine, 'core', [(0, 1), (1, 0)])  9.9 us
    all_to_all x1, blocking collectives, per_device(): found = lax.all_to_all(found, STRIP, 0, 0, tiled=True)  7.44 us
    ppermute x1, starting transfers between devices, per_device(): other_source = lax.ppermute(source, 'y_hi', [(0, 1), (1, 0)])  5.65 us
    pallas_call x1, Pallas kernels, per_device(): pl.pallas_call(roll_kernel, out_shape=jax.ShapeDtypeStruct((CAPS * 6 * TG...  1.91 us
  transfers between devices with their start and end apart: 2, of which 0 were waited for; matrix products, arithmetic and copies ran while one was open for 1% of the time, Pallas kernels for 4%

profile of v13, /device:TPU:1, one launch (start us, length us, event | category | flops | bytes accessed | tf_op | source)
XLA Modules:
  0.0 80.0 jit_solution(4798251122026519410)
XLA Ops:
  0.0 0.9 %pad_maximum_fusion.1 = bf16[2,6,12,192]{3,0,2,1:T(2,128)(2,1)S(1)} fusion(bf16[2,3,12,192]{3,0,2,1:T(2,128)(2,1)} %param.6, bf16[2,3,12,192]{3,0,2,1:T(2,128)(2,1)} %param.5), kind=kLoop, calls=%fused_computation.1 | loop fusion | flops 27648 | bytes 110592 | tf_op jit(solution)/shard_map/concatenate | solution.py:199
  1.0 0.0 copy-start
  1.0 0.9 %copy-done = bf16[10,12,192]{2,1,0:T(8,128)(2,1)S(1)} copy-done((bf16[10,12,192]{2,1,0:T(8,128)(2,1)S(1)}, bf16[10,12,192]{2,1,0:T(8,128)(2,1)}, u32[]{:S(2)}) %copy-start) | copy-done | bytes 46104
  1.9 0.0 copy-start.1
  1.9 0.7 copy-done.1
  2.5 0.1 pack.1
  2.6 5.7 %collective-permute-start = (bf16[240,128]{1,0:T(8,128)(2,1)S(1)}, bf16[240,128]{1,0:T(8,128)(2,1)S(1)}, u32[]{:S(2)}, u32[]{:S(2)}) collective-permute-start(bf16[240,128]{1,0:T(8,128)(2,1)S(1)} %get-tuple-element.12), channel_id=1, source_target_pairs={{0,16},{16,0},{1,17},{17,1},{2,18},{18,2},{3,19},{19,3},{4,20},{20... | collective-permute-start | bytes 184328 | tf_op jit(solution)/shard_map/ppermute | solution.py:212
  8.3 33.0 %all_gather.3.op_ref = bf16[16,184,128]{2,1,0:T(8,128)(2,1)S(1)} all-gather(bf16[1,184,128]{2,1,0:T(8,128)(2,1)S(1)} %get-tuple-element.13), channel_id=1, replica_groups=mesh['z'=16,'y_hi'=2,'core'=2,'x'=4,'y_lo'=2] {'z'}, dimensions={0}, use_global_device_ids=true | all-gather | bytes 800768 | tf_op jit(solution)/shard_map/all_gather | solution.py:213
  41.3 0.0 collective-permute-done
  41.3 9.9 %collective-permute-start.1 = (bf16[16,184,128]{2,1,0:T(8,128)(2,1)S(1)}, bf16[16,184,128]{2,1,0:T(8,128)(2,1)S(1)}, u32[]{:S(2)}, u32[]{:S(2)}) collective-permute-start(bf16[16,184,128]{2,1,0:T(8,128)(2,1)S(1)} %all_gather.3.op_ref), channel_id=1, source_target_pairs={{0,8},{8,0},{1,9},{9,1},{2,10},{10,2},{3,11},{11,3},{4,12},{12,4},... | collective-permute-start | bytes 2261000 | tf_op jit(solution)/shard_map/ppermute | solution.py:217
  51.2 0.8 %reshape.16 = f32[16,4,10]{2,1,0:T(4,128)S(1)} reshape(f32[640]{0:T(1024)} %param.9) | data formatting | bytes 5120 | tf_op jit(solution)/shard_map/reshape | solution.py:215
  52.1 0.1 reshape.17.weight_ref
  52.2 1.9 %roll.1.rolled_ref = bf16[384,2304]{1,0:T(8,128)(2,1)S(1)} custom-call(bf16[2,240,128]{2,1,0:T(8,128)(2,1)S(1)} %pad_maximum_fusion.src_ref), custom_call_target="tpu_custom_call" | custom-call | flops 1000000000 | bytes 4194304 | tf_op jit(solution)/shard_map/roll/pallas_call | solution.py:222
  54.1 0.9 %rotate_mine.1.mine_ref = f32[16,32,128]{2,1,0:T(8,128)S(1)} custom-call(bf16[384,2304]{1,0:T(8,128)(2,1)S(1)} %roll.1.rolled_ref, bf16[16,184,128]{2,1,0:T(8,128)(2,1)S(1)} %all_gather.3.op_ref), custom_call_target="tpu_custom_call" | custom-call | flops 1000000000 | bytes 4194304 | tf_op jit(solution)/shard_map/rotate_mine/pallas_call | solution.py:238
  55.0 0.0 collective-permute-done.1.op_ref
  55.0 0.9 %rotate_next.1 = (f32[16,64,128]{2,1,0:T(8,128)S(1)}, f32[4,160]{1,0:T(4,128)S(1)}) custom-call(bf16[384,2304]{1,0:T(8,128)(2,1)S(1)} %roll.1.rolled_ref, bf16[16,184,128]{2,1,0:T(8,128)(2,1)S(1)} %collective-permute-done.1.op_ref, f32[16,32,128]{2,1,0:T(8,128)S(1)} %rotate_mine.1.mine_ref, f32[4,160]{1,0:T(4,128)S(1)} %reshape.17.weight_ref, s32[1]{0:T(128)} %bitcast.3.core_ref), custom_call_target="tpu_custom_call" | custom-call | tf_op jit(solution)/shard_map/rotate_next/pallas_call | solution.py:248
  56.0 15.7 %all_to_all.10 = f32[16,64,128]{2,1,0:T(8,128)S(1)} all-to-all(f32[16,64,128]{2,1,0:T(8,128)S(1)} %get-tuple-element.17), channel_id=1, replica_groups=mesh['z'=16,'y_hi'=2,'core'=2,'x'=4,'y_lo'=2] {'y_hi','x','y_lo'}, dimensions={0} | all-to-all | bytes 1048576 | tf_op jit(solution)/shard_map/all_to_all | solution.py:260
  71.6 0.3 stokes.1
  71.9 7.4 %all_to_all.11 = f32[8,8,128]{2,1,0:T(8,128)S(1)} all-to-all(f32[8,8,128]{2,1,0:T(8,128)S(1)} %stokes.1), channel_id=1, replica_groups=mesh['z'=16,'y_hi'=2,'core'=2,'x'=4,'y_lo'=2] {'x','y_lo'}, dimensions={0} | all-to-all | bytes 65536 | tf_op jit(solution)/shard_map/all_to_all | solution.py:269
  79.3 0.7 copy.14
  (6 shorter events, 0.1 us)
Async XLA Ops:
  1.0 0.9 %copy-start = (bf16[10,12,192]{2,1,0:T(8,128)(2,1)S(1)}, bf16[10,12,192]{2,1,0:T(8,128)(2,1)}, u32[]{:S(2)}) copy-start(bf16[10,12,192]{2,1,0:T(8,128)(2,1)} %op_ref.1) | copy-start | bytes 138244
  1.9 0.7 copy-start.1
  2.6 38.7 %collective-permute-start = (bf16[240,128]{1,0:T(8,128)(2,1)S(1)}, bf16[240,128]{1,0:T(8,128)(2,1)S(1)}, u32[]{:S(2)}, u32[]{:S(2)}) collective-permute-start(bf16[240,128]{1,0:T(8,128)(2,1)S(1)} %get-tuple-element.12), channel_id=1, source_target_pairs={{0,16},{16,0},{1,17},{17,1},{2,18},{18,2},{3,19},{19,3},{4,20},{20... | collective-permute-start | bytes 184328 | tf_op jit(solution)/shard_map/ppermute | solution.py:212
  41.3 13.7 %collective-permute-start.1 = (bf16[16,184,128]{2,1,0:T(8,128)(2,1)S(1)}, bf16[16,184,128]{2,1,0:T(8,128)(2,1)S(1)}, u32[]{:S(2)}, u32[]{:S(2)}) collective-permute-start(bf16[16,184,128]{2,1,0:T(8,128)(2,1)S(1)} %all_gather.3.op_ref), channel_id=1, source_target_pairs={{0,8},{8,0},{1,9},{9,1},{2,10},{10,2},{3,11},{11,3},{4,12},{12,4},... | collective-permute-start | bytes 2261000 | tf_op jit(solution)/shard_map/ppermute | solution.py:217

commit v14 on v13

--- a/solution.py
+++ b/solution.py
@@ -147,7 +147,13 @@
 def rotate_next_kernel(
     rolled_ref, op_ref, mine_ref, weight_ref, core_ref, out_ref, weight_out_ref, lines, held, acc
 ):
-    weight_out_ref[...] = weight_ref[...]
+    group = 2 * SIDES * ROWS_HERE
+    row = weight_ref[...].reshape(1, Z * group)
+    for g in range(2 * SIDES):
+        parts = [
+            row[:, z * group + g * ROWS_HERE : z * group + (g + 1) * ROWS_HERE] for z in range(Z)
+        ]
+        weight_out_ref[g : g + 1, :] = jnp.concatenate(parts, axis=1)
     core = core_ref[0]
     out_ref[:, pl.ds(pl.multiple_of(core * 32, 32), 32), :] = mine_ref[...]
     contract(rolled_ref, op_ref, lines, held, acc)
@@ -212,8 +218,6 @@
     other_source = lax.ppermute(source, "y_hi", [(0, 1), (1, 0)])
     mine = lax.all_gather(lines, "z", axis=0, tiled=True)
     mine, other_source, weights = lax.optimization_barrier((mine, other_source, weights))
-    weights = weights.reshape(Z, 2 * SIDES, ROWS_HERE).transpose(1, 0, 2)
-    weights = weights.reshape(2 * SIDES, NODES)
     other = lax.ppermute(mine, "core", [(0, 1), (1, 0)])
     first = lax.axis_index("y_hi") == 0
     source = jnp.stack(

time: 80.5 us -> 79.5 us (0.988)
  local copies, waits for them, and re-layouts: 3.21 us -> 2.28 us
    reshape x2 -> x0, local copies, waits for them, and re-layouts: 0.93 us -> none  [the longest x1 0.84 us: per_device(): weights = weights.reshape(Z, 2 * SIDES, ROWS_HERE).transpose(1, 0, 2)]
  transfers between devices with their start and end apart: 2 -> 2, of which waited for: 0 -> 0; matrix products, arithmetic and copies ran while one was open for 1% -> 0% of each run, Pallas kernels for 4% -> 4%
where the time goes in v14:
time: 79.5 us; the launch traced here: 79 us
  blocking collectives  56.1 us (71%)
  starting transfers between devices  15.6 us (20%)
  Pallas kernels  4.09 us (5%)
  local copies, waits for them, and re-layouts  2.28 us (3%)
  other arithmetic  0.93 us (1%)
    all_gather x1, blocking collectives, per_device(): mine = lax.all_gather(lines, 'z', axis=0, tiled=True)  33 us
    all_to_all x1, blocking collectives, per_device(): parts = lax.all_to_all(parts, ('y_hi',) + STRIP, 0, 0, tiled=True)  15.6 us
    ppermute x1, starting transfers between devices, per_device(): other = lax.ppermute(mine, 'core', [(0, 1), (1, 0)])  9.9 us
    all_to_all x1, blocking collectives, per_device(): found = lax.all_to_all(found, STRIP, 0, 0, tiled=True)  7.44 us
    ppermute x1, starting transfers between devices, per_device(): other_source = lax.ppermute(source, 'y_hi', [(0, 1), (1, 0)])  5.65 us
    pallas_call x1, Pallas kernels, per_device(): pl.pallas_call(roll_kernel, out_shape=jax.ShapeDtypeStruct((CAPS * 6 * TG...  1.91 us
  transfers between devices with their start and end apart: 2, of which 0 were waited for; matrix products, arithmetic and copies ran while one was open for 0% of the time, Pallas kernels for 4%

profile of v14, /device:TPU:1, one launch (start us, length us, event | category | flops | bytes accessed | tf_op | source)
XLA Modules:
  0.0 79.0 jit_solution(10168709190766837465)
XLA Ops:
  0.0 0.9 %pad_maximum_fusion.1 = bf16[2,6,12,192]{3,0,2,1:T(2,128)(2,1)S(1)} fusion(bf16[2,3,12,192]{3,0,2,1:T(2,128)(2,1)} %param.6, bf16[2,3,12,192]{3,0,2,1:T(2,128)(2,1)} %param.5), kind=kLoop, calls=%fused_computation.1 | loop fusion | flops 27648 | bytes 110592 | tf_op jit(solution)/shard_map/concatenate | solution.py:205
  1.0 0.0 copy-start
  1.0 0.9 %copy-done = bf16[10,12,192]{2,1,0:T(8,128)(2,1)S(1)} copy-done((bf16[10,12,192]{2,1,0:T(8,128)(2,1)S(1)}, bf16[10,12,192]{2,1,0:T(8,128)(2,1)}, u32[]{:S(2)}) %copy-start) | copy-done | bytes 46104
  1.9 0.0 copy-start.2
  1.9 0.7 copy-done.2
  2.5 0.1 pack.1
  2.6 5.7 %collective-permute-start = (bf16[240,128]{1,0:T(8,128)(2,1)S(1)}, bf16[240,128]{1,0:T(8,128)(2,1)S(1)}, u32[]{:S(2)}, u32[]{:S(2)}) collective-permute-start(bf16[240,128]{1,0:T(8,128)(2,1)S(1)} %get-tuple-element.12), channel_id=1, source_target_pairs={{0,16},{16,0},{1,17},{17,1},{2,18},{18,2},{3,19},{19,3},{4,20},{20... | collective-permute-start | bytes 184328 | tf_op jit(solution)/shard_map/ppermute | solution.py:218
  8.3 33.0 %all_gather.3.op_ref = bf16[16,184,128]{2,1,0:T(8,128)(2,1)S(1)} all-gather(bf16[1,184,128]{2,1,0:T(8,128)(2,1)S(1)} %get-tuple-element.13), channel_id=1, replica_groups=mesh['z'=16,'y_hi'=2,'core'=2,'x'=4,'y_lo'=2] {'z'}, dimensions={0}, use_global_device_ids=true | all-gather | bytes 800768 | tf_op jit(solution)/shard_map/all_gather | solution.py:219
  41.3 0.0 collective-permute-done
  41.3 9.9 %collective-permute-start.1 = (bf16[16,184,128]{2,1,0:T(8,128)(2,1)S(1)}, bf16[16,184,128]{2,1,0:T(8,128)(2,1)S(1)}, u32[]{:S(2)}, u32[]{:S(2)}) collective-permute-start(bf16[16,184,128]{2,1,0:T(8,128)(2,1)S(1)} %all_gather.3.op_ref), channel_id=1, source_target_pairs={{0,8},{8,0},{1,9},{9,1},{2,10},{10,2},{3,11},{11,3},{4,12},{12,4},... | collective-permute-start | bytes 2261000 | tf_op jit(solution)/shard_map/ppermute | solution.py:221
  51.3 1.9 %roll.1.rolled_ref = bf16[384,2304]{1,0:T(8,128)(2,1)S(1)} custom-call(bf16[2,240,128]{2,1,0:T(8,128)(2,1)S(1)} %pad_maximum_fusion.src_ref), custom_call_target="tpu_custom_call" | custom-call | flops 1000000000 | bytes 4194304 | tf_op jit(solution)/shard_map/roll/pallas_call | solution.py:226
  53.2 0.0 copy-start.1
  53.2 0.9 %rotate_mine.1.mine_ref = f32[16,32,128]{2,1,0:T(8,128)S(1)} custom-call(bf16[384,2304]{1,0:T(8,128)(2,1)S(1)} %roll.1.rolled_ref, bf16[16,184,128]{2,1,0:T(8,128)(2,1)S(1)} %all_gather.3.op_ref), custom_call_target="tpu_custom_call" | custom-call | flops 1000000000 | bytes 4194304 | tf_op jit(solution)/shard_map/rotate_mine/pallas_call | solution.py:242
  54.1 0.0 collective-permute-done.1.op_ref
  54.1 0.0 copy-done.1
  54.1 0.9 %rotate_next.1 = (f32[16,64,128]{2,1,0:T(8,128)S(1)}, f32[4,160]{1,0:T(4,128)S(1)}) custom-call(bf16[384,2304]{1,0:T(8,128)(2,1)S(1)} %roll.1.rolled_ref, bf16[16,184,128]{2,1,0:T(8,128)(2,1)S(1)} %collective-permute-done.1.op_ref, f32[16,32,128]{2,1,0:T(8,128)S(1)} %rotate_mine.1.mine_ref, f32[640]{0:T(1024)S(1)} %copy-done.1, s32[1]{0:T(128)} %bitcast.2.core_ref), custom_call_target="tpu_custom_call" | custom-call | tf_op jit(solution)/shard_map/rotate_next/pallas_call | solution.py:252
  55.0 15.6 %all_to_all.10 = f32[16,64,128]{2,1,0:T(8,128)S(1)} all-to-all(f32[16,64,128]{2,1,0:T(8,128)S(1)} %get-tuple-element.17), channel_id=1, replica_groups=mesh['z'=16,'y_hi'=2,'core'=2,'x'=4,'y_lo'=2] {'y_hi','x','y_lo'}, dimensions={0} | all-to-all | bytes 1048576 | tf_op jit(solution)/shard_map/all_to_all | solution.py:264
  70.7 0.3 stokes.1
  70.9 7.4 %all_to_all.11 = f32[8,8,128]{2,1,0:T(8,128)S(1)} all-to-all(f32[8,8,128]{2,1,0:T(8,128)S(1)} %stokes.1), channel_id=1, replica_groups=mesh['z'=16,'y_hi'=2,'core'=2,'x'=4,'y_lo'=2] {'x','y_lo'}, dimensions={0} | all-to-all | bytes 65536 | tf_op jit(solution)/shard_map/all_to_all | solution.py:273
  78.4 0.7 copy.12
  (5 shorter events, 0.1 us)
Async XLA Ops:
  1.0 0.9 %copy-start = (bf16[10,12,192]{2,1,0:T(8,128)(2,1)S(1)}, bf16[10,12,192]{2,1,0:T(8,128)(2,1)}, u32[]{:S(2)}) copy-start(bf16[10,12,192]{2,1,0:T(8,128)(2,1)} %op_ref.1) | copy-start | bytes 138244
  1.9 0.7 copy-start.2
  2.6 38.7 %collective-permute-start = (bf16[240,128]{1,0:T(8,128)(2,1)S(1)}, bf16[240,128]{1,0:T(8,128)(2,1)S(1)}, u32[]{:S(2)}, u32[]{:S(2)}) collective-permute-start(bf16[240,128]{1,0:T(8,128)(2,1)S(1)} %get-tuple-element.12), channel_id=1, source_target_pairs={{0,16},{16,0},{1,17},{17,1},{2,18},{18,2},{3,19},{19,3},{4,20},{20... | collective-permute-start | bytes 184328 | tf_op jit(solution)/shard_map/ppermute | solution.py:218
  41.3 12.8 %collective-permute-start.1 = (bf16[16,184,128]{2,1,0:T(8,128)(2,1)S(1)}, bf16[16,184,128]{2,1,0:T(8,128)(2,1)S(1)}, u32[]{:S(2)}, u32[]{:S(2)}) collective-permute-start(bf16[16,184,128]{2,1,0:T(8,128)(2,1)S(1)} %all_gather.3.op_ref), channel_id=1, source_target_pairs={{0,8},{8,0},{1,9},{9,1},{2,10},{10,2},{3,11},{11,3},{4,12},{12,4},... | collective-permute-start | bytes 2261000 | tf_op jit(solution)/shard_map/ppermute | solution.py:221
  53.2 0.9 %copy-start.1 = (f32[640]{0:T(1024)S(1)}, f32[640]{0:T(1024)}, u32[]{:S(2)}) copy-start(f32[640]{0:T(1024)} %weight_ref) | copy-start | bytes 7684

commit v15 on v14

--- a/solution.py
+++ b/solution.py
@@ -105,7 +105,7 @@
                 rolled_ref[to, (m + 12) * 128 : (m + 12) * 128 + 128] = rolled(high)
         return carry
 
-    lax.fori_loop(0, CAPS, per_capsule, 0)
+    lax.fori_loop(0, CAPS, per_capsule, 0, unroll=2)
 
 
 def contract(rolled_ref, op_ref, lines, held, acc):

time: 79.5 us -> 79.4 us (level)
  transfers between devices with their start and end apart: 2 -> 2, of which waited for: 0 -> 0; matrix products, arithmetic and copies ran while one was open for 0% -> 0% of each run, Pallas kernels for 4% -> 3%
where the time goes in v15:
time: 79.4 us; the launch traced here: 78.9 us
  blocking collectives  56.1 us (71%)
  starting transfers between devices  15.6 us (20%)
  Pallas kernels  3.92 us (5%)
  local copies, waits for them, and re-layouts  2.28 us (3%)
  other arithmetic  0.93 us (1%)
    all_gather x1, blocking collectives, per_device(): mine = lax.all_gather(lines, 'z', axis=0, tiled=True)  33 us
    all_to_all x1, blocking collectives, per_device(): parts = lax.all_to_all(parts, ('y_hi',) + STRIP, 0, 0, tiled=True)  15.7 us
    ppermute x1, starting transfers between devices, per_device(): other = lax.ppermute(mine, 'core', [(0, 1), (1, 0)])  9.9 us
    all_to_all x1, blocking collectives, per_device(): found = lax.all_to_all(found, STRIP, 0, 0, tiled=True)  7.44 us
    ppermute x1, starting transfers between devices, per_device(): other_source = lax.ppermute(source, 'y_hi', [(0, 1), (1, 0)])  5.65 us
    pallas_call x1, Pallas kernels, per_device(): pl.pallas_call(roll_kernel, out_shape=jax.ShapeDtypeStruct((CAPS * 6 * TG...  1.74 us
  transfers between devices with their start and end apart: 2, of which 0 were waited for; matrix products, arithmetic and copies ran while one was open for 0% of the time, Pallas kernels for 3%

profile of v15, /device:TPU:1, one launch (start us, length us, event | category | flops | bytes accessed | tf_op | source)
XLA Modules:
  0.0 78.9 jit_solution(16530993914240468934)
XLA Ops:
  0.0 0.9 %pad_maximum_fusion.1 = bf16[2,6,12,192]{3,0,2,1:T(2,128)(2,1)S(1)} fusion(bf16[2,3,12,192]{3,0,2,1:T(2,128)(2,1)} %param.6, bf16[2,3,12,192]{3,0,2,1:T(2,128)(2,1)} %param.5), kind=kLoop, calls=%fused_computation.1 | loop fusion | flops 27648 | bytes 110592 | tf_op jit(solution)/shard_map/concatenate | solution.py:205
  1.0 0.0 copy-start
  1.0 0.9 %copy-done = bf16[10,12,192]{2,1,0:T(8,128)(2,1)S(1)} copy-done((bf16[10,12,192]{2,1,0:T(8,128)(2,1)S(1)}, bf16[10,12,192]{2,1,0:T(8,128)(2,1)}, u32[]{:S(2)}) %copy-start) | copy-done | bytes 46104
  1.9 0.0 copy-start.2
  1.9 0.7 copy-done.2
  2.5 0.1 pack.1
  2.6 5.7 %collective-permute-start = (bf16[240,128]{1,0:T(8,128)(2,1)S(1)}, bf16[240,128]{1,0:T(8,128)(2,1)S(1)}, u32[]{:S(2)}, u32[]{:S(2)}) collective-permute-start(bf16[240,128]{1,0:T(8,128)(2,1)S(1)} %get-tuple-element.12), channel_id=1, source_target_pairs={{0,16},{16,0},{1,17},{17,1},{2,18},{18,2},{3,19},{19,3},{4,20},{20... | collective-permute-start | bytes 184328 | tf_op jit(solution)/shard_map/ppermute | solution.py:218
  8.3 33.0 %all_gather.3.op_ref = bf16[16,184,128]{2,1,0:T(8,128)(2,1)S(1)} all-gather(bf16[1,184,128]{2,1,0:T(8,128)(2,1)S(1)} %get-tuple-element.13), channel_id=1, replica_groups=mesh['z'=16,'y_hi'=2,'core'=2,'x'=4,'y_lo'=2] {'z'}, dimensions={0}, use_global_device_ids=true | all-gather | bytes 800768 | tf_op jit(solution)/shard_map/all_gather | solution.py:219
  41.3 0.0 collective-permute-done
  41.3 9.9 %collective-permute-start.1 = (bf16[16,184,128]{2,1,0:T(8,128)(2,1)S(1)}, bf16[16,184,128]{2,1,0:T(8,128)(2,1)S(1)}, u32[]{:S(2)}, u32[]{:S(2)}) collective-permute-start(bf16[16,184,128]{2,1,0:T(8,128)(2,1)S(1)} %all_gather.3.op_ref), channel_id=1, source_target_pairs={{0,8},{8,0},{1,9},{9,1},{2,10},{10,2},{3,11},{11,3},{4,12},{12,4},... | collective-permute-start | bytes 2261000 | tf_op jit(solution)/shard_map/ppermute | solution.py:221
  51.3 1.7 %roll.1.rolled_ref = bf16[384,2304]{1,0:T(8,128)(2,1)S(1)} custom-call(bf16[2,240,128]{2,1,0:T(8,128)(2,1)S(1)} %pad_maximum_fusion.src_ref), custom_call_target="tpu_custom_call" | custom-call | flops 1000000000 | bytes 4194304 | tf_op jit(solution)/shard_map/roll/pallas_call | solution.py:226
  53.0 0.0 copy-start.1
  53.0 0.9 %rotate_mine.1.mine_ref = f32[16,32,128]{2,1,0:T(8,128)S(1)} custom-call(bf16[384,2304]{1,0:T(8,128)(2,1)S(1)} %roll.1.rolled_ref, bf16[16,184,128]{2,1,0:T(8,128)(2,1)S(1)} %all_gather.3.op_ref), custom_call_target="tpu_custom_call" | custom-call | flops 1000000000 | bytes 4194304 | tf_op jit(solution)/shard_map/rotate_mine/pallas_call | solution.py:242
  53.9 0.0 collective-permute-done.1.op_ref
  53.9 0.0 copy-done.1
  53.9 0.9 %rotate_next.1 = (f32[16,64,128]{2,1,0:T(8,128)S(1)}, f32[4,160]{1,0:T(4,128)S(1)}) custom-call(bf16[384,2304]{1,0:T(8,128)(2,1)S(1)} %roll.1.rolled_ref, bf16[16,184,128]{2,1,0:T(8,128)(2,1)S(1)} %collective-permute-done.1.op_ref, f32[16,32,128]{2,1,0:T(8,128)S(1)} %rotate_mine.1.mine_ref, f32[640]{0:T(1024)S(1)} %copy-done.1, s32[1]{0:T(128)} %bitcast.2.core_ref), custom_call_target="tpu_custom_call" | custom-call | tf_op jit(solution)/shard_map/rotate_next/pallas_call | solution.py:252
  54.9 15.7 %all_to_all.10 = f32[16,64,128]{2,1,0:T(8,128)S(1)} all-to-all(f32[16,64,128]{2,1,0:T(8,128)S(1)} %get-tuple-element.17), channel_id=1, replica_groups=mesh['z'=16,'y_hi'=2,'core'=2,'x'=4,'y_lo'=2] {'y_hi','x','y_lo'}, dimensions={0} | all-to-all | bytes 1048576 | tf_op jit(solution)/shard_map/all_to_all | solution.py:264
  70.5 0.3 stokes.1
  70.8 7.4 %all_to_all.11 = f32[8,8,128]{2,1,0:T(8,128)S(1)} all-to-all(f32[8,8,128]{2,1,0:T(8,128)S(1)} %stokes.1), channel_id=1, replica_groups=mesh['z'=16,'y_hi'=2,'core'=2,'x'=4,'y_lo'=2] {'x','y_lo'}, dimensions={0} | all-to-all | bytes 65536 | tf_op jit(solution)/shard_map/all_to_all | solution.py:273
  78.2 0.7 copy.12
  (5 shorter events, 0.1 us)
Async XLA Ops:
  1.0 0.9 %copy-start = (bf16[10,12,192]{2,1,0:T(8,128)(2,1)S(1)}, bf16[10,12,192]{2,1,0:T(8,128)(2,1)}, u32[]{:S(2)}) copy-start(bf16[10,12,192]{2,1,0:T(8,128)(2,1)} %op_ref.1) | copy-start | bytes 138244
  1.9 0.7 copy-start.2
  2.6 38.7 %collective-permute-start = (bf16[240,128]{1,0:T(8,128)(2,1)S(1)}, bf16[240,128]{1,0:T(8,128)(2,1)S(1)}, u32[]{:S(2)}, u32[]{:S(2)}) collective-permute-start(bf16[240,128]{1,0:T(8,128)(2,1)S(1)} %get-tuple-element.12), channel_id=1, source_target_pairs={{0,16},{16,0},{1,17},{17,1},{2,18},{18,2},{3,19},{19,3},{4,20},{20... | collective-permute-start | bytes 184328 | tf_op jit(solution)/shard_map/ppermute | solution.py:218
  41.3 12.6 %collective-permute-start.1 = (bf16[16,184,128]{2,1,0:T(8,128)(2,1)S(1)}, bf16[16,184,128]{2,1,0:T(8,128)(2,1)S(1)}, u32[]{:S(2)}, u32[]{:S(2)}) collective-permute-start(bf16[16,184,128]{2,1,0:T(8,128)(2,1)S(1)} %all_gather.3.op_ref), channel_id=1, source_target_pairs={{0,8},{8,0},{1,9},{9,1},{2,10},{10,2},{3,11},{11,3},{4,12},{12,4},... | collective-permute-start | bytes 2261000 | tf_op jit(solution)/shard_map/ppermute | solution.py:221
  53.0 0.9 %copy-start.1 = (f32[640]{0:T(1024)S(1)}, f32[640]{0:T(1024)}, u32[]{:S(2)}) copy-start(f32[640]{0:T(1024)} %weight_ref) | copy-start | bytes 7684
